TPU v7x, 128 devices: a whole 4x4x4 slice. The times are simulated.
128 devices in a mesh: dp: 16 (over y_hi, x, core), tensor: 8 (over y_lo, z).
Axes of the slice: x: 4, y: 4 (y_hi: 2, y_lo: 2; y = y_hi * 2 + y_lo), z: 4, core: 2. Of those that a mesh axis runs over, the one named last changes fastest.
Arguments:
- hidden_in: bfloat16 [16384, 1024], P(('dp', 'tensor')), may hold values from -25 to 25
- cotangent: bfloat16 [16384, 1024], P(('dp', 'tensor')), may hold values from -6 to 6
- norm_gain: float32 [2, 2, 1024], replicated, may hold values from 0.5 to 1.5
- norm_shift: float32 [2, 2, 1024], replicated, may hold values from -4 to 4
- inward: bfloat16 [2, 1024, 3, 1024], P(None, None, None, 'tensor'), may hold values from -0.1875 to 0.1875
- inward_bias: float32 [2, 2, 1024], P(None, None, 'tensor'), may hold values from -4 to 4
- outward: bfloat16 [2, 1024, 1024], P(None, 'tensor'), may hold values from -0.75 to 0.75
- outward_bias: float32 [2, 1024], replicated, may hold values from -4 to 4
- expand: bfloat16 [2, 1024, 4096], P(None, None, 'tensor'), may hold values from -0.1875 to 0.1875
- expand_bias: float32 [2, 4096], P(None, 'tensor'), may hold values from -4 to 4
- shrink: bfloat16 [2, 4096, 1024], P(None, 'tensor'), may hold values from -0.125 to 0.125
- shrink_bias: float32 [2, 1024], replicated, may hold values from -4 to 4
Outputs:
- hidden_out: float32 [16384, 1024], P(('dp', 'tensor'))
- grad_hidden: float32 [16384, 1024], P(('dp', 'tensor'))
- grad_gain: float32 [2, 2, 1024], replicated
- grad_shift: float32 [2, 2, 1024], replicated
- grad_inward: float32 [2, 1024, 3, 1024], P(None, 'dp', None, 'tensor')
- grad_inward_bias: float32 [2, 2, 1024], P(None, None, 'tensor')
- grad_outward: float32 [2, 1024, 1024], P(None, 'tensor', 'dp')
- grad_outward_bias: float32 [2, 1024], replicated
- grad_expand: float32 [2, 1024, 4096], P(None, 'dp', 'tensor')
- grad_expand_bias: float32 [2, 4096], P(None, 'tensor')
- grad_shrink: float32 [2, 4096, 1024], P(None, 'tensor', 'dp')
- grad_shrink_bias: float32 [2, 1024], replicated
All inputs are finite; a program needn't handle non-finite values.
Results may differ from a plain program's by a relative error of at most 0.025.
Values may be sent and summed in bfloat16 or wider, within the bound.
No kernel may reach another device: no remote copies, remote signals or barrier semaphores. Data moves between devices by JAX's collectives and lax.ppermute only.
A program may use at most 128 MiB of HBM per device.

v0:
```python
import jax
import jax.numpy as jnp
from jax import lax
from jax.sharding import PartitionSpec as P

HEAD_DIM = 64
LAYERS = 2
SEQ_LEN = 1024


EPS_NORM = 1e-05
NEG_FILL = -1000000000.0


def layer_norm(stream, norm_gain, norm_shift):
    center = stream - jnp.mean(stream, -1, keepdims=True)
    spread = jnp.mean(center * center, -1, keepdims=True)
    return center * lax.rsqrt(spread + EPS_NORM) * norm_gain + norm_shift


def gelu_tanh(values):
    return (
        0.5
        * values
        * (1.0 + jnp.tanh(0.7978845608028654 * (values + 0.044715 * values * values * values)))
    )


def tokens_inner(left, right):
    return lax.dot_general(
        left, right, (((0,), (0,)), ((), ())), preferred_element_type=jnp.float32
    )


def against_rows(left, right):
    return lax.dot_general(
        left, right, (((1,), (1,)), ((), ())), preferred_element_type=jnp.float32
    )


def share_rows(values):
    return lax.all_gather(values, "tensor", axis=0, tiled=True)


def return_rows(values):
    return lax.all_gather(values, "tensor", axis=0, tiled=True)


def sum_forward(left, weight, local_rows):

    def term(first_row, row_count):
        return jnp.dot(left, weight, preferred_element_type=jnp.float32)

    return lax.psum_scatter(
        term(jnp.int32(0), local_rows * lax.axis_size("tensor")).astype(jnp.bfloat16),
        "tensor",
        scatter_dimension=0,
        tiled=True,
    ).astype(jnp.float32)


def sum_backward(left, weight, local_rows):

    def term(first_row, row_count):
        return against_rows(left, weight)

    return lax.psum_scatter(
        term(jnp.int32(0), local_rows * lax.axis_size("tensor")).astype(jnp.bfloat16),
        "tensor",
        scatter_dimension=0,
        tiled=True,
    ).astype(jnp.float32)


def send_weights(grad_in, grad_out, grad_up, grad_down):
    return (
        lax.psum_scatter(
            grad_in.astype(jnp.bfloat16), "dp", scatter_dimension=0, tiled=True
        ).astype(jnp.float32),
        lax.psum_scatter(
            grad_out.astype(jnp.bfloat16), "dp", scatter_dimension=1, tiled=True
        ).astype(jnp.float32),
        lax.psum_scatter(
            grad_up.astype(jnp.bfloat16), "dp", scatter_dimension=0, tiled=True
        ).astype(jnp.float32),
        lax.psum_scatter(
            grad_down.astype(jnp.bfloat16), "dp", scatter_dimension=1, tiled=True
        ).astype(jnp.float32),
    )


def send_biases(bias_in, bias_up):
    return lax.psum((bias_in, bias_up), "dp")


def send_vectors(gain_terms, shift_terms, bias_out, bias_down):
    return lax.psum((gain_terms, shift_terms, bias_out, bias_down), ("dp", "tensor"))


def split_heads(flat):
    seq_count = flat.shape[0] // SEQ_LEN
    return flat.reshape(seq_count, SEQ_LEN, flat.shape[1] // HEAD_DIM, HEAD_DIM)


def causal_mask(query_start, query_count, key_end):
    query_place = query_start + lax.iota(jnp.int32, query_count)
    key_place = lax.iota(jnp.int32, key_end)
    return query_place[:, None] >= key_place[None, :]


def attend_forward(queries, key_rows, value_rows):
    query_heads = split_heads(queries)
    key_heads = split_heads(key_rows)
    value_heads = split_heads(value_rows)
    block_rows = min(512, SEQ_LEN)
    score_scale = HEAD_DIM ** (-0.5)
    outputs = []
    totals = []
    for block_index in range(SEQ_LEN // block_rows):
        query_start = block_index * block_rows
        key_end = query_start + block_rows
        scores = (
            jnp.einsum(
                "sqhd,skhd->shqk",
                query_heads[:, query_start:key_end],
                key_heads[:, :key_end],
                preferred_element_type=jnp.float32,
            )
            * score_scale
        )
        scores = jnp.where(causal_mask(query_start, block_rows, key_end), scores, NEG_FILL)
        row_peak = jnp.max(scores, -1, keepdims=True)
        weights = jnp.exp(scores - row_peak)
        row_total = jnp.sum(weights, -1, keepdims=True)
        weights = weights / row_total
        mixed_heads = jnp.einsum(
            "shqk,skhd->sqhd",
            weights.astype(jnp.bfloat16),
            value_heads[:, :key_end],
            preferred_element_type=jnp.float32,
        )
        outputs.append(mixed_heads.astype(jnp.bfloat16))
        totals.append(row_peak + jnp.log(row_total))
    return (jnp.concatenate(outputs, 1).reshape(queries.shape), jnp.concatenate(totals, 2))


def attend_backward(queries, key_rows, value_rows, grad_out, log_totals):
    query_heads = split_heads(queries)
    key_heads = split_heads(key_rows)
    value_heads = split_heads(value_rows)
    grad_heads = split_heads(grad_out)
    block_rows = min(512, SEQ_LEN)
    score_scale = HEAD_DIM ** (-0.5)
    key_grad = jnp.zeros(key_heads.shape, jnp.float32)
    value_grad = jnp.zeros(value_heads.shape, jnp.float32)
    query_parts = []
    for block_index in range(SEQ_LEN // block_rows):
        query_start = block_index * block_rows
        key_end = query_start + block_rows
        scores = (
            jnp.einsum(
                "sqhd,skhd->shqk",
                query_heads[:, query_start:key_end],
                key_heads[:, :key_end],
                preferred_element_type=jnp.float32,
            )
            * score_scale
        )
        scores = jnp.where(causal_mask(query_start, block_rows, key_end), scores, NEG_FILL)
        weights = jnp.exp(scores - log_totals[:, :, query_start:key_end])
        grad_weights = jnp.einsum(
            "sqhd,skhd->shqk",
            grad_heads[:, query_start:key_end],
            value_heads[:, :key_end],
            preferred_element_type=jnp.float32,
        )
        grad_scores = (
            weights * (grad_weights - jnp.sum(weights * grad_weights, -1, keepdims=True))
        ).astype(jnp.bfloat16)
        query_parts.append(
            jnp.einsum(
                "shqk,skhd->sqhd",
                grad_scores,
                key_heads[:, :key_end],
                preferred_element_type=jnp.float32,
            )
            * score_scale
        )
        key_grad = key_grad.at[:, :key_end].add(
            jnp.einsum(
                "shqk,sqhd->skhd",
                grad_scores,
                query_heads[:, query_start:key_end],
                preferred_element_type=jnp.float32,
            )
            * score_scale
        )
        value_grad = value_grad.at[:, :key_end].add(
            jnp.einsum(
                "shqk,sqhd->skhd",
                weights.astype(jnp.bfloat16),
                grad_heads[:, query_start:key_end],
                preferred_element_type=jnp.float32,
            )
        )
    query_grad = jnp.concatenate(query_parts, 1).reshape(queries.shape)
    return (query_grad, key_grad.reshape(key_rows.shape), value_grad.reshape(value_rows.shape))


def layer_forward(stream, layer_index, params):
    (
        norm_gain,
        norm_shift,
        inward,
        inward_bias,
        outward,
        outward_bias,
        expand,
        expand_bias,
        shrink,
        shrink_bias,
    ) = params
    local_rows = stream.shape[0]
    width_local = inward.shape[3]
    normed = layer_norm(stream, norm_gain[layer_index, 0], norm_shift[layer_index, 0]).astype(
        jnp.bfloat16
    )
    normed_all = share_rows(normed)
    mix_weight = inward[layer_index].reshape(inward.shape[1], 3 * width_local)
    projected = jnp.dot(normed_all, mix_weight, preferred_element_type=jnp.float32)
    queries = (projected[:, :width_local] + inward_bias[layer_index, 0]).astype(jnp.bfloat16)
    key_rows = projected[:, width_local : 2 * width_local].astype(jnp.bfloat16)
    value_rows = (projected[:, 2 * width_local :] + inward_bias[layer_index, 1]).astype(
        jnp.bfloat16
    )
    attended, log_totals = attend_forward(queries, key_rows, value_rows)
    middle = stream + (
        sum_forward(attended, outward[layer_index], local_rows) + outward_bias[layer_index]
    )
    normed_mid = layer_norm(middle, norm_gain[layer_index, 1], norm_shift[layer_index, 1]).astype(
        jnp.bfloat16
    )
    mid_all = share_rows(normed_mid)
    hidden_pre = (
        jnp.dot(mid_all, expand[layer_index], preferred_element_type=jnp.float32)
        + expand_bias[layer_index]
    )
    activated = gelu_tanh(hidden_pre).astype(jnp.bfloat16)
    result = middle + (
        sum_forward(activated, shrink[layer_index], local_rows) + shrink_bias[layer_index]
    )
    saved_state = (
        stream,
        normed_all,
        queries,
        key_rows,
        value_rows,
        attended,
        log_totals,
        middle,
        mid_all,
        hidden_pre,
        activated,
    )
    return (result, saved_state)


def layer_backward(grad_stream, layer_index, params, saved_state):
    (
        norm_gain,
        norm_shift,
        inward,
        inward_bias,
        outward,
        outward_bias,
        expand,
        expand_bias,
        shrink,
        shrink_bias,
    ) = params
    (
        stream,
        normed_all,
        queries,
        key_rows,
        value_rows,
        attended,
        log_totals,
        middle,
        mid_all,
        hidden_pre,
        activated,
    ) = saved_state
    local_rows = grad_stream.shape[0]
    width_local = inward.shape[3]
    grad_branch = grad_stream.astype(jnp.bfloat16)
    vector_down = jnp.sum(grad_branch, 0, dtype=jnp.float32)
    grad_all = return_rows(grad_branch)
    grad_shrink = tokens_inner(activated, grad_all)
    grad_act = against_rows(grad_all, shrink[layer_index])
    grad_pre = jax.vjp(gelu_tanh, hidden_pre)[1](grad_act)[0].astype(jnp.bfloat16)
    bias_up = jnp.sum(grad_pre, 0, dtype=jnp.float32)
    grad_expand = tokens_inner(mid_all, grad_pre)
    grad_norm_mid = sum_backward(grad_pre, expand[layer_index], local_rows)
    norm_back = jax.vjp(layer_norm, middle, norm_gain[layer_index, 1], norm_shift[layer_index, 1])[
        1
    ]
    grad_part, gain_mid, shift_mid = norm_back(grad_norm_mid)
    grad_middle = grad_stream + grad_part
    grad_attn = grad_middle.astype(jnp.bfloat16)
    vector_out = jnp.sum(grad_attn, 0, dtype=jnp.float32)
    grad_attn_all = return_rows(grad_attn)
    grad_outward = tokens_inner(attended, grad_attn_all)
    grad_attended = against_rows(grad_attn_all, outward[layer_index]).astype(jnp.bfloat16)
    query_grad, key_grad, value_grad = attend_backward(
        queries, key_rows, value_rows, grad_attended, log_totals
    )
    query_grad = query_grad.astype(jnp.bfloat16)
    key_grad = key_grad.astype(jnp.bfloat16)
    value_grad = value_grad.astype(jnp.bfloat16)
    bias_in = jnp.stack(
        [jnp.sum(query_grad, 0, dtype=jnp.float32), jnp.sum(value_grad, 0, dtype=jnp.float32)]
    )
    grad_mixed = jnp.concatenate([query_grad, key_grad, value_grad], 1)
    grad_inward = tokens_inner(normed_all, grad_mixed).reshape(inward.shape[1], 3, width_local)
    mix_weight = inward[layer_index].reshape(inward.shape[1], 3 * width_local)
    grad_normed = sum_backward(grad_mixed, mix_weight, local_rows)
    norm_back_in = jax.vjp(
        layer_norm, stream, norm_gain[layer_index, 0], norm_shift[layer_index, 0]
    )[1]
    grad_first, gain_in, shift_in = norm_back_in(grad_normed)
    grad_prev = grad_middle + grad_first
    weight_grads = (grad_inward, grad_outward, grad_expand, grad_shrink)
    bias_grads = (bias_in, bias_up)
    vector_grads = (
        jnp.stack([gain_in, gain_mid]),
        jnp.stack([shift_in, shift_mid]),
        vector_out,
        vector_down,
    )
    return (grad_prev, weight_grads, bias_grads, vector_grads)


def per_device(
    hidden_in,
    cotangent,
    norm_gain,
    norm_shift,
    inward,
    inward_bias,
    outward,
    outward_bias,
    expand,
    expand_bias,
    shrink,
    shrink_bias,
):
    params = (
        norm_gain,
        norm_shift,
        inward,
        inward_bias,
        outward,
        outward_bias,
        expand,
        expand_bias,
        shrink,
        shrink_bias,
    )
    stream = hidden_in.astype(jnp.float32)
    layer_inputs = []
    saved_states = []
    for layer_index in range(LAYERS):
        layer_inputs.append(stream)
        stream, saved_state = layer_forward(stream, layer_index, params)
        saved_states.append(saved_state)
    grad_stream = cotangent.astype(jnp.float32)
    weight_parts = [None] * LAYERS
    bias_parts = [None] * LAYERS
    vector_parts = [None] * LAYERS
    for layer_index in reversed(range(LAYERS)):
        saved_state = saved_states[layer_index]
        grad_stream, weight_grads, bias_grads, vector_grads = layer_backward(
            grad_stream, layer_index, params, saved_state
        )
        weight_parts[layer_index] = weight_grads
        bias_parts[layer_index] = bias_grads
        vector_parts[layer_index] = vector_grads
    joined = send_weights(
        jnp.concatenate([member[0] for member in weight_parts], 2),
        jnp.concatenate([member[1] for member in weight_parts], 0),
        jnp.concatenate([member[2] for member in weight_parts], 1),
        jnp.concatenate([member[3] for member in weight_parts], 0),
    )
    grad_inward = jnp.stack(jnp.split(joined[0], LAYERS, 2))
    grad_outward = jnp.stack(jnp.split(joined[1], LAYERS, 0))
    grad_expand = jnp.stack(jnp.split(joined[2], LAYERS, 1))
    grad_shrink = jnp.stack(jnp.split(joined[3], LAYERS, 0))
    bias_sums = send_biases(
        jnp.stack([member[0] for member in bias_parts]),
        jnp.stack([member[1] for member in bias_parts]),
    )
    vector_sums = send_vectors(
        jnp.stack([member[0] for member in vector_parts]),
        jnp.stack([member[1] for member in vector_parts]),
        jnp.stack([member[2] for member in vector_parts]),
        jnp.stack([member[3] for member in vector_parts]),
    )
    return (
        stream,
        grad_stream,
        vector_sums[0],
        vector_sums[1],
        grad_inward,
        bias_sums[0],
        grad_outward,
        vector_sums[2],
        grad_expand,
        bias_sums[1],
        grad_shrink,
        vector_sums[3],
    )


def solution(mesh):
    return jax.shard_map(
        per_device,
        mesh=mesh,
        in_specs=(
            P(("dp", "tensor"), None),
            P(("dp", "tensor"), None),
            P(),
            P(),
            P(None, None, None, "tensor"),
            P(None, None, "tensor"),
            P(None, "tensor", None),
            P(),
            P(None, None, "tensor"),
            P(None, "tensor"),
            P(None, "tensor", None),
            P(),
        ),
        out_specs=(
            P(("dp", "tensor"), None),
            P(("dp", "tensor"), None),
            P(),
            P(),
            P(None, "dp", None, "tensor"),
            P(None, None, "tensor"),
            P(None, "tensor", "dp"),
            P(),
            P(None, "dp", "tensor"),
            P(None, "tensor"),
            P(None, "tensor", "dp"),
            P(),
        ),
        check_vma=False,
    )
```

profile of v0, /device:TPU:1, one launch (start us, length us, event | category | flops | bytes accessed | tf_op | source)
XLA Modules:
  0.0 1141.4 jit_solution(7123736000726682099)
XLA Ops:
  14.8 2.4 fusion.151
  20.1 34.4 %all-gather.9.cloned.1.call-done = bf16[1024,1024]{1,0:T(8,128)(2,1)} async-done(((bf16[128,1024]{1,0:T(8,128)(2,1)}), bf16[1024,1024]{1,0:T(8,128)(2,1)}) %all-gather.9.cloned.1.call-update) | async-done | bytes 2097168 | tf_op jit(solution)/shard_map/all_gather | solution.py:42
  54.5 2.6 fusion.161
  67.1 41.5 %reduce-scatter.19.cloned.1.call-done = bf16[128,1024]{1,0:T(8,128)(2,1)} async-done(((bf16[1024,1024]{1,0:T(8,128)(2,1)}), bf16[128,1024]{1,0:T(8,128)(2,1)}) %reduce-scatter.19.cloned.1.call-update) | async-done | bytes 262160 | tf_op jit(solution)/shard_map/reduce_scatter | solution.py:54
  113.4 39.6 %all-gather.11.cloned.1.call-done = bf16[1024,1024]{1,0:T(8,128)(2,1)} async-done(((bf16[128,1024]{1,0:T(8,128)(2,1)}), bf16[1024,1024]{1,0:T(8,128)(2,1)}) %all-gather.11.cloned.1.call-update) | async-done | bytes 2097168 | tf_op jit(solution)/shard_map/all_gather | solution.py:42
  153.0 3.2 fusion.80
  157.6 2.8 convolution_convert_fusion.5
  161.7 40.9 %reduce-scatter.21.cloned.1.call-done = bf16[128,1024]{1,0:T(8,128)(2,1)} async-done(((bf16[1024,1024]{1,0:T(8,128)(2,1)}), bf16[128,1024]{1,0:T(8,128)(2,1)}) %reduce-scatter.21.cloned.1.call-update) | async-done | bytes 262160 | tf_op jit(solution)/shard_map/reduce_scatter | solution.py:54
  205.1 2.3 copy.82
  207.5 37.9 %all-gather.13.cloned.1.call-done = bf16[1024,1024]{1,0:T(8,128)(2,1)} async-done(((bf16[128,1024]{1,0:T(8,128)(2,1)}), bf16[1024,1024]{1,0:T(8,128)(2,1)}) %all-gather.13.cloned.1.call-update) | async-done | bytes 2097168 | tf_op jit(solution)/shard_map/all_gather | solution.py:42
  245.4 2.8 fusion.162
  257.3 42.2 %reduce-scatter.23.cloned.1.call-done = bf16[128,1024]{1,0:T(8,128)(2,1)} async-done(((bf16[1024,1024]{1,0:T(8,128)(2,1)}), bf16[128,1024]{1,0:T(8,128)(2,1)}) %reduce-scatter.23.cloned.1.call-update) | async-done | bytes 262160 | tf_op jit(solution)/shard_map/reduce_scatter | solution.py:54
  303.0 39.5 %all-gather.15.cloned.1.call-done = bf16[1024,1024]{1,0:T(8,128)(2,1)} async-done(((bf16[128,1024]{1,0:T(8,128)(2,1)}), bf16[1024,1024]{1,0:T(8,128)(2,1)}) %all-gather.15.cloned.1.call-update) | async-done | bytes 2097168 | tf_op jit(solution)/shard_map/all_gather | solution.py:42
  342.5 4.5 fusion.72
  347.0 38.0 %all-gather.17.cloned.1.call-done = bf16[1024,1024]{1,0:T(8,128)(2,1)} async-done(((bf16[128,1024]{1,0:T(8,128)(2,1)}), bf16[1024,1024]{1,0:T(8,128)(2,1)}) %all-gather.17.cloned.1.call-update) | async-done | bytes 2097168 | tf_op jit(solution)/shard_map/all_gather | solution.py:46
  385.0 6.1 convert_reduce_fusion
  392.1 2.6 convolution_convert_fusion.3
  395.0 4.8 convolution_convert_fusion.4
  399.9 36.9 %reduce-scatter.27.cloned.1.call-done = bf16[128,1024]{1,0:T(8,128)(2,1)} async-done(((bf16[1024,1024]{1,0:T(8,128)(2,1)}), bf16[128,1024]{1,0:T(8,128)(2,1)}) %reduce-scatter.27.cloned.1.call-update) | async-done | bytes 262160 | tf_op jit(solution)/shard_map/reduce_scatter | solution.py:67
  438.8 41.5 %reduce-scatter.25.cloned.1.call-done = bf16[128,1024]{1,0:T(8,128)(2,1)} async-done(((bf16[1024,1024]{1,0:T(8,128)(2,1)}), bf16[128,1024]{1,0:T(8,128)(2,1)}) %reduce-scatter.25.cloned.1.call-update) | async-done | bytes 262160 | tf_op jit(solution)/shard_map/reduce_scatter | solution.py:54
  485.0 40.3 %all-gather.19.cloned.1.call-done = bf16[1024,1024]{1,0:T(8,128)(2,1)} async-done(((bf16[128,1024]{1,0:T(8,128)(2,1)}), bf16[1024,1024]{1,0:T(8,128)(2,1)}) %all-gather.19.cloned.1.call-update) | async-done | bytes 2097168 | tf_op jit(solution)/shard_map/all_gather | solution.py:46
  525.3 2.6 convolution_convert_fusion.17
  537.6 2.7 convolution_convert_fusion.1
  540.3 42.1 %reduce-scatter.29.cloned.1.call-done = bf16[128,1024]{1,0:T(8,128)(2,1)} async-done(((bf16[1024,1024]{1,0:T(8,128)(2,1)}), bf16[128,1024]{1,0:T(8,128)(2,1)}) %reduce-scatter.29.cloned.1.call-update) | async-done | bytes 262160 | tf_op jit(solution)/shard_map/reduce_scatter | solution.py:67
  586.1 3.0 convert_reduce_fusion.8
  589.5 39.9 %all-gather.21.cloned.1.call-done = bf16[1024,1024]{1,0:T(8,128)(2,1)} async-done(((bf16[128,1024]{1,0:T(8,128)(2,1)}), bf16[1024,1024]{1,0:T(8,128)(2,1)}) %all-gather.21.cloned.1.call-update) | async-done | bytes 2097168 | tf_op jit(solution)/shard_map/all_gather | solution.py:46
  629.4 6.1 convert_reduce_fusion.1
  636.4 2.6 convolution_convert_fusion.2
  639.2 42.1 %reduce-scatter.31.cloned.1.call-done = bf16[128,1024]{1,0:T(8,128)(2,1)} async-done(((bf16[1024,1024]{1,0:T(8,128)(2,1)}), bf16[128,1024]{1,0:T(8,128)(2,1)}) %reduce-scatter.31.cloned.1.call-update) | async-done | bytes 262160 | tf_op jit(solution)/shard_map/reduce_scatter | solution.py:67
  685.0 2.5 convert_reduce_fusion.10
  687.6 3.8 convolution_convert_fusion.8
  694.4 3.9 copy.79
  699.1 4.3 convolution_convert_fusion.10
  705.4 2.3 copy.63
  707.7 3.0 convolution_convert_fusion.14
  710.7 2.6 convolution_convert_fusion.11
  715.0 4.0 copy.77
  719.1 8.8 all-gather.23.cloned.1.call-done
  732.9 2.4 convolution_convert_fusion.16
  746.3 3.4 convert_reduce_fusion.13
  754.9 3.8 convolution_convert_fusion
  759.5 45.6 %reduce-scatter.41.cloned.1.call-done = bf16[64,1024]{1,0:T(8,128)(2,1)} async-done(((bf16[1024,1024]{1,0:T(8,128)(2,1)}), bf16[64,1024]{1,0:T(8,128)(2,1)}) %reduce-scatter.41.cloned.1.call-update) | async-done | bytes 131088
  807.3 71.7 %reduce-scatter.39.cloned.1.call-done = bf16[64,1024]{1,0:T(8,128)(2,1)} async-done(((bf16[1024,1024]{1,0:T(8,128)(2,1)}), bf16[64,1024]{1,0:T(8,128)(2,1)}) %reduce-scatter.39.cloned.1.call-update) | async-done | bytes 131088
  881.4 36.1 %all-reduce.5 = (f32[2,2,128]{2,1,0:T(2,128)}, f32[2,512]{1,0:T(2,128)}) all-reduce(f32[2,2,128]{2,1,0:T(2,128)S(1)} %pad_maximum_fusion.21, f32[2,512]{1,0:T(2,128)S(1)} %pad_maximum_fusion.20), channel_id=1, replica_groups=mesh['dp'=16,'tensor'=8] {'dp'}, use_global_device_ids=true, to_apply=%region_51.52 | all-reduce | flops 1536 | bytes 12288 | tf_op jit(solution)/shard_map/psum | solution.py:93
  917.5 29.4 %reduce-scatter.37.cloned.1.call-done = bf16[64,256]{1,0:T(8,128)(2,1)} async-done(((bf16[1024,256]{1,0:T(8,128)(2,1)}), bf16[64,256]{1,0:T(8,128)(2,1)}) %reduce-scatter.37.cloned.1.call-update) | async-done | bytes 32784
  948.6 70.6 %reduce-scatter.35.cloned.1.call-done = bf16[64,3,256]{2,0,1:T(8,128)(2,1)} async-done(((bf16[1024,3,256]{2,0,1:T(8,128)(2,1)}), bf16[64,3,256]{2,0,1:T(8,128)(2,1)}) %reduce-scatter.35.cloned.1.call-update) | async-done | bytes 98320 | tf_op jit(solution)/shard_map/reduce_scatter | solution.py:77
  1020.9 39.3 %reduce-scatter.33.cloned.1.call-done = bf16[128,1024]{1,0:T(8,128)(2,1)} async-done(((bf16[1024,1024]{1,0:T(8,128)(2,1)}), bf16[128,1024]{1,0:T(8,128)(2,1)}) %reduce-scatter.33.cloned.1.call-update) | async-done | bytes 262160 | tf_op jit(solution)/shard_map/reduce_scatter | solution.py:67
  1062.9 69.2 %all-reduce.4 = (f32[2,2,1024]{2,1,0:T(2,128)}, f32[2,2,1024]{2,1,0:T(2,128)}, f32[2,1024]{1,0:T(2,128)}, f32[2,1024]{1,0:T(2,128)}) all-reduce(f32[2,2,1024]{2,1,0:T(2,128)S(1)} %pad_maximum_fusion.16, f32[2,2,1024]{2,1,0:T(2,128)S(1)} %pad_maximum_fusion.17, ...), channel_id=1, replica_groups=mesh['dp'=16,'tensor'=8] {'dp','tensor'}, use_global_device_ids=true, to_apply=%region_40.41 | all-reduce | flops 12288 | bytes 98304 | tf_op jit(solution)/shard_map/psum | solution.py:97
  (431 shorter events, 110.5 us)
Async XLA Ops:
  7.2 47.3 %all-gather.9.cloned.1.call-start = ((), (), s32[]{:S(2)}) async-start(), calls=%async_computation.12 | async-start | bytes 2359296 | tf_op jit(solution)/shard_map/all_gather | solution.py:42
  14.8 93.8 %reduce-scatter.19.cloned.1.call-start = ((), (), s32[]{:S(2)}) async-start(), calls=%async_computation.13 | async-start | bytes 2359296 | tf_op jit(solution)/shard_map/reduce_scatter | solution.py:54
  66.4 46.4 %copy-start.98 = (f32[2,512]{1,0:T(2,128)S(1)}, f32[2,512]{1,0:T(2,128)}, u32[]{:S(2)}) copy-start(f32[2,512]{1,0:T(2,128)} %param.45) | copy-start | bytes 12292
  66.4 86.5 %all-gather.11.cloned.1.call-start = ((), (), s32[]{:S(2)}) async-start(), calls=%async_computation.14 | async-start | bytes 2359296 | tf_op jit(solution)/shard_map/all_gather | solution.py:42
  109.7 46.5 %copy-start.49 = (f32[128]{0:T(128)}, f32[128]{0:T(128)S(1)}, u32[]{:S(2)}) copy-start(f32[128]{0:T(128)S(1)} %broadcast_multiply_fusion.2) | copy-start | bytes 1540
  112.8 89.8 %reduce-scatter.21.cloned.1.call-start = ((), (), s32[]{:S(2)}) async-start(), calls=%async_computation.15 | async-start | bytes 2359296 | tf_op jit(solution)/shard_map/reduce_scatter | solution.py:54
  160.4 84.9 %all-gather.13.cloned.1.call-start = ((), (), s32[]{:S(2)}) async-start(), calls=%async_computation.16 | async-start | bytes 2359296 | tf_op jit(solution)/shard_map/all_gather | solution.py:42
  204.9 94.5 %reduce-scatter.23.cloned.1.call-start = ((), (), s32[]{:S(2)}) async-start(), calls=%async_computation.17 | async-start | bytes 2359296 | tf_op jit(solution)/shard_map/reduce_scatter | solution.py:54
  257.2 85.3 %all-gather.15.cloned.1.call-start = ((), (), s32[]{:S(2)}) async-start(), calls=%async_computation.18 | async-start | bytes 2359296 | tf_op jit(solution)/shard_map/all_gather | solution.py:42
  302.2 82.8 %all-gather.17.cloned.1.call-start = ((), (), s32[]{:S(2)}) async-start(), calls=%async_computation.20 | async-start | bytes 2359296 | tf_op jit(solution)/shard_map/all_gather | solution.py:46
  303.0 82.0 %copy-start.105 = (f32[1,512]{1,0:T(1,128)S(1)}, f32[1,512]{1,0:T(1,128)}, u32[]{:S(2)}) copy-start(f32[1,512]{1,0:T(1,128)} %get-tuple-element.242) | copy-start | bytes 6148
  303.0 133.8 %reduce-scatter.27.cloned.1.call-start = ((), (), s32[]{:S(2)}) async-start(), calls=%async_computation.21 | async-start | bytes 2359296 | tf_op jit(solution)/shard_map/reduce_scatter | solution.py:67
  394.8 85.6 %reduce-scatter.25.cloned.1.call-start = ((), (), s32[]{:S(2)}) async-start(), calls=%async_computation.19 | async-start | bytes 2359296 | tf_op jit(solution)/shard_map/reduce_scatter | solution.py:54
  399.8 80.6 %copy-start.60 = (f32[1,1024]{1,0:T(1,128)S(1)}, f32[1,1024]{1,0:T(1,128)}, u32[]{:S(2)}) copy-start(f32[1,1024]{1,0:T(1,128)} %get-tuple-element.238) | copy-start | bytes 12292
  399.8 85.1 %copy-start.57 = (f32[2,512]{1,0:T(2,128)S(1)}, f32[2,512]{1,0:T(2,128)}, u32[]{:S(2)}) copy-start(f32[2,512]{1,0:T(2,128)} %copy-done.56) | copy-start | bytes 12292
  399.8 85.1 %copy-start.59 = (f32[2,512]{1,0:T(2,128)S(1)}, f32[2,512]{1,0:T(2,128)}, u32[]{:S(2)}) copy-start(f32[2,512]{1,0:T(2,128)} %copy-done.58) | copy-start | bytes 12292
  399.9 85.1 %copy-start.80 = (f32[2,512]{1,0:T(2,128)S(1)}, f32[2,512]{1,0:T(2,128)}, u32[]{:S(2)}) copy-start(f32[2,512]{1,0:T(2,128)} %copy-done.79) | copy-start | bytes 12292
  399.9 85.1 %copy-start.82 = (f32[2,512]{1,0:T(2,128)S(1)}, f32[2,512]{1,0:T(2,128)}, u32[]{:S(2)}) copy-start(f32[2,512]{1,0:T(2,128)} %copy-done.81) | copy-start | bytes 12292
  399.9 125.4 %all-gather.19.cloned.1.call-start = ((), (), s32[]{:S(2)}) async-start(), calls=%async_computation.22 | async-start | bytes 2359296 | tf_op jit(solution)/shard_map/all_gather | solution.py:46
  484.9 97.5 %reduce-scatter.29.cloned.1.call-start = ((), (), s32[]{:S(2)}) async-start(), calls=%async_computation.23 | async-start | bytes 2359296 | tf_op jit(solution)/shard_map/reduce_scatter | solution.py:67
  540.3 89.1 %copy-start.104 = (f32[1,512]{1,0:T(1,128)S(1)}, f32[1,512]{1,0:T(1,128)}, u32[]{:S(2)}) copy-start(f32[1,512]{1,0:T(1,128)} %copy-done.103) | copy-start | bytes 6148
  540.3 89.1 %all-gather.21.cloned.1.call-start = ((), (), s32[]{:S(2)}) async-start(), calls=%async_computation.24 | async-start | bytes 2359296 | tf_op jit(solution)/shard_map/all_gather | solution.py:46
  589.0 92.2 %reduce-scatter.31.cloned.1.call-start = ((), (), s32[]{:S(2)}) async-start(), calls=%async_computation.25 | async-start | bytes 2359296 | tf_op jit(solution)/shard_map/reduce_scatter | solution.py:67
  639.1 88.8 %all-gather.23.cloned.1.call-start = ((), (), s32[]{:S(2)}) async-start(), calls=%async_computation.26 | async-start | bytes 2359296 | tf_op jit(solution)/shard_map/all_gather | solution.py:46
  687.5 117.6 %reduce-scatter.41.cloned.1.call-start = ((), (), s32[]{:S(2)}) async-start(), calls=%async_computation.31 | async-start | bytes 2228224
  698.4 180.6 %reduce-scatter.39.cloned.1.call-start = ((), (), s32[]{:S(2)}) async-start(), calls=%async_computation.30 | async-start | bytes 2228224
  719.0 228.0 %reduce-scatter.37.cloned.1.call-start = ((), (), s32[]{:S(2)}) async-start(), calls=%async_computation.29 | async-start | bytes 557056
  744.7 274.6 %reduce-scatter.35.cloned.1.call-start = ((), (), s32[]{:S(2)}) async-start(), calls=%async_computation.28 | async-start | bytes 1671168 | tf_op jit(solution)/shard_map/reduce_scatter | solution.py:77
  754.6 305.5 %reduce-scatter.33.cloned.1.call-start = ((), (), s32[]{:S(2)}) async-start(), calls=%async_computation.27 | async-start | bytes 2359296 | tf_op jit(solution)/shard_map/reduce_scatter | solution.py:67
  807.2 74.0 %copy-start.66 = (f32[1024]{0:T(1024)S(1)}, f32[1024]{0:T(1024)}, u32[]{:S(2)}) copy-start(f32[1024]{0:T(1024)} %get-tuple-element.206) | copy-start | bytes 12292
  807.2 74.0 %copy-start.69 = (f32[1024]{0:T(1024)S(1)}, f32[1024]{0:T(1024)}, u32[]{:S(2)}) copy-start(f32[1024]{0:T(1024)} %get-tuple-element.201) | copy-start | bytes 12292
  807.2 74.0 %copy-start.70 = (f32[1024]{0:T(1024)S(1)}, f32[1024]{0:T(1024)}, u32[]{:S(2)}) copy-start(f32[1024]{0:T(1024)} %get-tuple-element.225) | copy-start | bytes 12292
  807.2 74.0 %copy-start.71 = (f32[1024]{0:T(1024)S(1)}, f32[1024]{0:T(1024)}, u32[]{:S(2)}) copy-start(f32[1024]{0:T(1024)} %get-tuple-element.204) | copy-start | bytes 12292
  807.2 74.1 %copy-start.111 = (f32[2,64]{1,0:T(2,128)S(1)}, f32[2,64]{1,0:T(2,128)}, u32[]{:S(2)}) copy-start(f32[2,64]{1,0:T(2,128)} %get-tuple-element.197) | copy-start | bytes 1540
  880.1 180.1 %copy-start.86 = (f32[128]{0:T(128)S(1)}, f32[128]{0:T(128)}, u32[]{:S(2)}) copy-start(f32[128]{0:T(128)} %copy-done.85) | copy-start | bytes 1540
  880.1 181.2 %copy-start.113 = (f32[128]{0:T(128)S(1)}, f32[128]{0:T(128)}, u32[]{:S(2)}) copy-start(f32[128]{0:T(128)} %copy-done.112) | copy-start | bytes 1540
  880.1 181.2 %copy-start.97 = (f32[128]{0:T(128)S(1)}, f32[128]{0:T(128)}, u32[]{:S(2)}) copy-start(f32[128]{0:T(128)} %copy-done.96) | copy-start | bytes 1540
  880.2 182.5 %copy-start.63 = (f32[1024]{0:T(1024)S(1)}, f32[1024]{0:T(1024)}, u32[]{:S(2)}) copy-start(f32[1024]{0:T(1024)} %get-tuple-element.190) | copy-start | bytes 12292
  880.2 182.5 %copy-start.65 = (f32[1024]{0:T(1024)S(1)}, f32[1024]{0:T(1024)}, u32[]{:S(2)}) copy-start(f32[1024]{0:T(1024)} %get-tuple-element.188) | copy-start | bytes 12292
  880.2 182.5 %copy-start.68 = (f32[1024]{0:T(1024)S(1)}, f32[1024]{0:T(1024)}, u32[]{:S(2)}) copy-start(f32[1024]{0:T(1024)} %get-tuple-element.186) | copy-start | bytes 12292
  880.2 182.6 %copy-start.62 = (f32[1024]{0:T(1024)S(1)}, f32[1024]{0:T(1024)}, u32[]{:S(2)}) copy-start(f32[1024]{0:T(1024)} %get-tuple-element.180) | copy-start | bytes 12292
  880.2 182.6 %copy-start.64 = (f32[1024]{0:T(1024)S(1)}, f32[1024]{0:T(1024)}, u32[]{:S(2)}) copy-start(f32[1024]{0:T(1024)} %get-tuple-element.178) | copy-start | bytes 12292
  880.3 182.6 %copy-start.67 = (f32[1024]{0:T(1024)S(1)}, f32[1024]{0:T(1024)}, u32[]{:S(2)}) copy-start(f32[1024]{0:T(1024)} %get-tuple-element.176) | copy-start | bytes 12292
  880.3 251.8 %copy-start.11 = (bf16[128,1024]{1,0:T(8,128)(2,1)S(1)}, bf16[128,1024]{1,0:T(8,128)(2,1)}, u32[]{:S(2)}) copy-start(bf16[128,1024]{1,0:T(8,128)(2,1)} %reduce-scatter.31.cloned.1.call-done) | copy-start | bytes 786436
  880.3 251.8 %copy-start.51 = (f32[128]{0:T(128)S(1)}, f32[128]{0:T(128)}, u32[]{:S(2)}) copy-start(f32[128]{0:T(128)} %copy-done.49) | copy-start | bytes 1540
  880.3 251.8 %copy-start.91 = (f32[128]{0:T(128)S(1)}, f32[128]{0:T(128)}, u32[]{:S(2)}) copy-start(f32[128]{0:T(128)} %copy-done.89) | copy-start | bytes 1540
  880.3 251.8 %copy-start.95 = (f32[128]{0:T(128)S(1)}, f32[128]{0:T(128)}, u32[]{:S(2)}) copy-start(f32[128]{0:T(128)} %copy-done.94) | copy-start | bytes 1540
  880.3 251.8 %copy-start.108 = (f32[128]{0:T(128)S(1)}, f32[128]{0:T(128)}, u32[]{:S(2)}) copy-start(f32[128]{0:T(128)} %copy-done.107) | copy-start | bytes 1540
  (101 other events, 1144.6 us)
Sparse Core Ops, SparseCore 0:
  14.9 39.6 all-gather.8
  66.6 42.0 reduce-scatter.18
  112.9 40.0 all-gather.10
  160.6 42.0 reduce-scatter.20
  205.0 40.2 all-gather.12
  257.3 42.0 reduce-scatter.22
  302.3 40.0 all-gather.14
  344.1 40.8 all-gather.16
  394.9 41.8 reduce-scatter.26
  439.1 41.2 reduce-scatter.24
  485.0 40.2 all-gather.18
  540.4 41.9 reduce-scatter.28
  589.2 40.1 all-gather.20
  639.2 41.9 reduce-scatter.30
  687.7 40.2 all-gather.22
  731.7 73.3 reduce-scatter.40
  808.9 69.9 reduce-scatter.38
  882.6 64.3 reduce-scatter.36
  951.3 67.8 reduce-scatter.34
  1021.6 38.4 reduce-scatter.32
where the time goes:
time: 1150 us; the launch traced here: 1140 us
  waiting for transfers between devices  823 us (72%)
  blocking collectives  105 us (9%)
  matrix products  98 us (9%)
  other arithmetic  53.4 us (5%)
  local copies, waits for them, and re-layouts  43.3 us (4%)
  between operations  16.2 us (1%)
    reduce_scatter x4, waiting for transfers between devices, sum_forward(): lax.psum_scatter(term(jnp.int32(0), local_rows * lax.axis_size('tensor'))...  166 us
    reduce_scatter x4, waiting for transfers between devices, sum_backward(): lax.psum_scatter(term(jnp.int32(0), local_rows * lax.axis_size('tensor'))...  160 us
    all_gather x4, waiting for transfers between devices, share_rows(): return lax.all_gather(values, 'tensor', axis=0, tiled=True)  151 us
    unnamed x23, waiting for transfers between devices  148 us
    all_gather x4, waiting for transfers between devices, return_rows(): return lax.all_gather(values, 'tensor', axis=0, tiled=True)  127 us
    reduce_scatter x1, waiting for transfers between devices, send_weights(): lax.psum_scatter(grad_in.astype(jnp.bfloat16), 'dp', scatter_dimension=0,...  70.6 us
    psum x1, blocking collectives, send_vectors(): lax.psum((gain_terms, shift_terms, bias_out, bias_down), ('dp', 'tensor'))  69.2 us
    psum x1, blocking collectives, send_biases(): return lax.psum((bias_in, bias_up), 'dp')  36.1 us
  transfers between devices with their start and end apart: 20, of which 20 were waited for; matrix products, arithmetic and copies ran while one was open for 8% of the time, Pallas kernels for 0%

commit v1 on v0

v1 whole, which is shorter than its diff:
```python
import jax
import jax.numpy as jnp
from jax import lax
from jax.sharding import Mesh
from jax.sharding import PartitionSpec as P

HEAD_DIM = 64
LAYERS = 2
EPS_NORM = 1e-05
NEG_FILL = -1000000000.0
BF = jnp.bfloat16
F32 = jnp.float32
RINGS = {"z": ("z",), "x": ("x",), "y": ("yh", "yl")}


def layer_norm(stream, norm_gain, norm_shift):
    center = stream - jnp.mean(stream, -1, keepdims=True)
    spread = jnp.mean(center * center, -1, keepdims=True)
    return center * lax.rsqrt(spread + EPS_NORM) * norm_gain + norm_shift


def gelu_tanh(values):
    return (
        0.5
        * values
        * (1.0 + jnp.tanh(0.7978845608028654 * (values + 0.044715 * values * values * values)))
    )


def tokens_inner(left, right):
    return lax.dot_general(left, right, (((0,), (0,)), ((), ())), preferred_element_type=F32)


def against_rows(left, right):
    return lax.dot_general(left, right, (((1,), (1,)), ((), ())), preferred_element_type=F32)


def ring(values, axis, step):
    return lax.ppermute(values, RINGS[axis], [(i, (i + step) % 4) for i in range(4)])


def swap_cores(values):
    return lax.ppermute(values, "c", [(0, 1), (1, 0)])


def swap_halves(values):
    return lax.ppermute(values, ("c", "yl"), [(0, 0), (1, 2), (2, 1), (3, 3)])


def y_pairs(rule):
    pairs = []
    for y in range(4):
        for core in range(2):
            target = rule(y, core)
            if target is not None:
                y2, core2 = target[0] % 4, target[1]
                pairs.append(
                    ((y // 2) * 4 + core * 2 + y % 2, (y2 // 2) * 4 + core2 * 2 + y2 % 2)
                )
    return pairs


def fetch_weights(values, step):
    return lax.ppermute(
        values,
        ("yh", "c", "yl"),
        y_pairs(lambda y, c: (y - step, y % 2) if c == y % 2 else (y, y % 2)),
    )


def gather_rows(values):
    before = ring(values, "z", 1)
    after = ring(values, "z", -1)
    across = ring(values, "z", 2)
    mine = jnp.concatenate([values, before, after, across])
    return jnp.concatenate([mine, swap_cores(mine)])


def scatter_rows(partial):
    half = partial.shape[0] // 2
    rows = half // 4
    other = swap_cores(partial[half:].astype(BF))
    both = partial[:half] + other.astype(F32)
    low = both.astype(BF)
    from_after = ring(low[rows : 2 * rows], "z", -1)
    from_before = ring(low[2 * rows : 3 * rows], "z", 1)
    from_across = ring(low[3 * rows :], "z", 2)
    return (
        both[:rows]
        + from_after.astype(F32)
        + from_before.astype(F32)
        + from_across.astype(F32)
    )


def scatter_grads(grad):
    columns = grad.shape[1]
    blocks = grad.reshape(2, 4, 128, columns)
    place = lax.axis_index("x")

    def pick(step):
        return lax.dynamic_index_in_dim(blocks, (place + step) % 4, 1, keepdims=False)

    summed = (
        pick(0).astype(F32)
        + ring(pick(1).astype(BF), "x", 1).astype(F32)
        + ring(pick(3).astype(BF), "x", -1).astype(F32)
        + ring(pick(2).astype(BF), "x", 2).astype(F32)
    )
    high = lax.axis_index("yh")
    y = high * 2 + lax.axis_index("yl")

    def pick_high(index):
        return lax.dynamic_index_in_dim(summed, index, 0, keepdims=False)

    axes = ("yh", "c", "yl")
    up = lax.ppermute(
        pick_high(((y + 1) % 4) // 2).astype(BF),
        axes,
        y_pairs(lambda y, c: (y + 1, c) if c != y % 2 else None),
    )
    down = lax.ppermute(
        pick_high(((y + 3) % 4) // 2).astype(BF),
        axes,
        y_pairs(lambda y, c: (y + 3, c) if c != y % 2 else None),
    )
    far = lax.ppermute(
        pick_high(1 - high).astype(BF),
        axes,
        y_pairs(lambda y, c: (y + 2, c) if c == y % 2 else None),
    )
    total = pick_high(high) + up.astype(F32) + down.astype(F32) + far.astype(F32)
    core = lax.axis_index("c")
    halves = total.reshape(2, 64, columns)
    keep = lax.dynamic_index_in_dim(halves, core, 0, keepdims=False)
    give = lax.dynamic_index_in_dim(halves, 1 - core, 0, keepdims=False)
    got = lax.ppermute(give, ("c", "yl"), [(0, 2), (3, 1)])
    return jnp.where(core == lax.axis_index("yl"), keep, got)


def sum_everywhere(values):
    values = values + swap_cores(values)
    for axis in ("z", "x", "y"):
        values = (values + ring(values, axis, 2)) + (
            ring(values, axis, 1) + ring(values, axis, -1)
        )
    return values


def split_heads(flat):
    return flat.reshape(flat.shape[0], flat.shape[1] // HEAD_DIM, HEAD_DIM)


def row_places():
    core, z = lax.axis_index("c"), lax.axis_index("z")
    blocks = jnp.stack([cc * 4 + (z + dz) % 4 for cc in (core, 1 - core) for dz in (0, 3, 1, 2)])
    return (blocks[:, None] * 128 + lax.iota(jnp.int32, 128)[None, :]).reshape(-1)


def masked_scores(queries, keys, mask):
    scores = jnp.einsum("qhd,khd->hqk", queries, keys, preferred_element_type=F32)
    return jnp.where(mask, scores * HEAD_DIM ** (-0.5), NEG_FILL)


def attend_forward(queries, keys, values, mask):
    scores = masked_scores(split_heads(queries), split_heads(keys), mask)
    peak = jnp.max(scores, -1, keepdims=True)
    weights = jnp.exp(scores - peak)
    total = jnp.sum(weights, -1, keepdims=True)
    weights = weights / total
    mixed = jnp.einsum(
        "hqk,khd->qhd", weights.astype(BF), split_heads(values), preferred_element_type=F32
    )
    return mixed.astype(BF).reshape(queries.shape), peak + jnp.log(total)


def attend_backward(queries, keys, values, grad_out, log_totals, mask):
    q, k, v, do = (split_heads(m) for m in (queries, keys, values, grad_out))
    scale = HEAD_DIM ** (-0.5)
    weights = jnp.exp(masked_scores(q, k, mask) - log_totals)
    grad_weights = jnp.einsum("qhd,khd->hqk", do, v, preferred_element_type=F32)
    grad_scores = (
        weights * (grad_weights - jnp.sum(weights * grad_weights, -1, keepdims=True))
    ).astype(BF)
    dq = jnp.einsum("hqk,khd->qhd", grad_scores, k, preferred_element_type=F32) * scale
    dk = jnp.einsum("hqk,qhd->khd", grad_scores, q, preferred_element_type=F32) * scale
    dv = jnp.einsum("hqk,qhd->khd", weights.astype(BF), do, preferred_element_type=F32)
    return tuple(m.astype(BF).reshape(queries.shape) for m in (dq, dk, dv))


def per_device(
    hidden_in,
    cotangent,
    norm_gain,
    norm_shift,
    inward,
    inward_bias,
    outward,
    outward_bias,
    expand,
    expand_bias,
    shrink,
    shrink_bias,
):
    stream = swap_halves(hidden_in).astype(F32)
    columns = inward.shape[3]
    w_in, w_out, w_up, w_down = [], [], [], []
    for layer in range(LAYERS):
        w_in.append(fetch_weights(inward[layer].reshape(-1, 3 * columns), 1))
        if layer == 0:
            biases = fetch_weights(
                jnp.concatenate([inward_bias.reshape(-1, 128), expand_bias.reshape(-1, 128)]), -1
            )
            bias_in = biases[:4].reshape(LAYERS, 2, columns)
            bias_up = biases[4:].reshape(LAYERS, -1)
        w_out.append(fetch_weights(outward[layer], -1))
        w_up.append(fetch_weights(expand[layer], -1))
        w_down.append(fetch_weights(shrink[layer], 1))
    cotangent = swap_halves(cotangent)

    places = row_places()
    mask = (places[:, None] >= places[None, :])[None]
    saved = []
    for layer in range(LAYERS):
        normed = layer_norm(stream, norm_gain[layer, 0], norm_shift[layer, 0]).astype(BF)
        normed_all = gather_rows(normed)
        projected = jnp.dot(normed_all, w_in[layer], preferred_element_type=F32)
        queries = (projected[:, :columns] + bias_in[layer, 0]).astype(BF)
        keys = projected[:, columns : 2 * columns].astype(BF)
        values = (projected[:, 2 * columns :] + bias_in[layer, 1]).astype(BF)
        attended, log_totals = attend_forward(queries, keys, values, mask)
        middle = stream + (
            scatter_rows(jnp.dot(attended, w_out[layer], preferred_element_type=F32))
            + outward_bias[layer]
        )
        normed_mid = layer_norm(middle, norm_gain[layer, 1], norm_shift[layer, 1]).astype(BF)
        mid_all = gather_rows(normed_mid)
        hidden_pre = (
            jnp.dot(mid_all, w_up[layer], preferred_element_type=F32) + bias_up[layer]
        )
        activated = gelu_tanh(hidden_pre).astype(BF)
        result = middle + (
            scatter_rows(jnp.dot(activated, w_down[layer], preferred_element_type=F32))
            + shrink_bias[layer]
        )
        saved.append(
            (stream, normed_all, queries, keys, values, attended, log_totals, middle, mid_all,
             hidden_pre, activated)
        )
        stream = result
    hidden_out = swap_halves(stream)

    grad_stream = cotangent.astype(F32)
    gains, shifts, sums_out, sums_down, sums_in, sums_up = {}, {}, {}, {}, {}, {}
    grads_mlp, grads_attn = [None] * LAYERS, [None] * LAYERS
    for layer in reversed(range(LAYERS)):
        (stream, normed_all, queries, keys, values, attended, log_totals, middle, mid_all,
         hidden_pre, activated) = saved[layer]
        dy = grad_stream.astype(BF)
        sums_down[layer] = jnp.sum(dy, 0, dtype=F32)
        dy_all = gather_rows(dy)
        grad_act = against_rows(dy_all, w_down[layer])
        du = jax.vjp(gelu_tanh, hidden_pre)[1](grad_act)[0].astype(BF)
        sums_up[layer] = jnp.sum(du, 0, dtype=F32)
        dh = scatter_rows(against_rows(du, w_up[layer]))
        grads_mlp[layer] = scatter_grads(
            jnp.concatenate(
                [tokens_inner(dy_all, activated), tokens_inner(mid_all, du)], 1
            )
        )
        back_mid = jax.vjp(layer_norm, middle, norm_gain[layer, 1], norm_shift[layer, 1])[1]
        grad_part, gains[layer, 1], shifts[layer, 1] = back_mid(dh)
        grad_middle = grad_stream + grad_part
        dz = grad_middle.astype(BF)
        sums_out[layer] = jnp.sum(dz, 0, dtype=F32)
        dz_all = gather_rows(dz)
        do = against_rows(dz_all, w_out[layer]).astype(BF)
        dq, dk, dv = attend_backward(queries, keys, values, do, log_totals, mask)
        sums_in[layer] = jnp.stack([jnp.sum(dq, 0, dtype=F32), jnp.sum(dv, 0, dtype=F32)])
        dqkv = jnp.concatenate([dq, dk, dv], 1)
        da = scatter_rows(against_rows(dqkv, w_in[layer]))
        grads_attn[layer] = scatter_grads(
            jnp.concatenate(
                [tokens_inner(dz_all, attended), tokens_inner(normed_all, dqkv)], 1
            )
        )
        back_in = jax.vjp(layer_norm, stream, norm_gain[layer, 0], norm_shift[layer, 0])[1]
        grad_first, gains[layer, 0], shifts[layer, 0] = back_in(da)
        grad_stream = grad_middle + grad_first
    grad_hidden = swap_halves(grad_stream)

    shard = lax.axis_index("c") * 4 + lax.axis_index("z")
    own = lax.axis_index("yl") * 4 + lax.axis_index("z")
    both = range(LAYERS)
    up = jnp.stack([sums_up[n] for n in both])[:, None]
    qv = jnp.stack([sums_in[n] for n in both])[:, :, None]
    up = lax.dynamic_update_slice_in_dim(jnp.zeros((LAYERS, 8, up.shape[2]), F32), up, shard, 1)
    qv = lax.dynamic_update_slice_in_dim(jnp.zeros((LAYERS, 2, 8, columns), F32), qv, shard, 2)
    vectors = jnp.concatenate(
        [
            m.reshape(-1, 128)
            for m in (
                [gains[n, i] for n in both for i in (0, 1)]
                + [shifts[n, i] for n in both for i in (0, 1)]
                + [sums_out[n] for n in both]
                + [sums_down[n] for n in both]
                + [up, qv]
            )
        ]
    )
    vectors = sum_everywhere(vectors)
    grad_gain = vectors[:32].reshape(LAYERS, 2, 1024)
    grad_shift = vectors[32:64].reshape(LAYERS, 2, 1024)
    grad_out_bias = vectors[64:80].reshape(LAYERS, 1024)
    grad_down_bias = vectors[80:96].reshape(LAYERS, 1024)
    up = vectors[96:160].reshape(LAYERS, 8, -1)
    qv = vectors[160:].reshape(LAYERS, 2, 8, columns)
    grad_up_bias = lax.dynamic_index_in_dim(up, own, 1, keepdims=False)
    grad_in_bias = lax.dynamic_index_in_dim(qv, own, 2, keepdims=False)

    width = activated.shape[1]
    return (
        hidden_out,
        grad_hidden,
        grad_gain,
        grad_shift,
        jnp.stack([g[:, columns:].reshape(-1, 3, columns) for g in grads_attn]),
        grad_in_bias,
        jnp.stack([g[:, :columns].T for g in grads_attn]),
        grad_out_bias,
        jnp.stack([g[:, width:] for g in grads_mlp]),
        grad_up_bias,
        jnp.stack([g[:, :width].T for g in grads_mlp]),
        grad_down_bias,
    )


def solution(mesh):
    fine = Mesh(mesh.devices.reshape(2, 4, 2, 2, 4), ("yh", "x", "c", "yl", "z"))
    dp, tensor = ("yh", "x", "c"), ("yl", "z")
    rows = P(dp + tensor, None)
    return jax.shard_map(
        per_device,
        mesh=fine,
        in_specs=(
            rows,
            rows,
            P(),
            P(),
            P(None, None, None, tensor),
            P(None, None, tensor),
            P(None, tensor, None),
            P(),
            P(None, None, tensor),
            P(None, tensor),
            P(None, tensor, None),
            P(),
        ),
        out_specs=(
            rows,
            rows,
            P(),
            P(),
            P(None, dp, None, tensor),
            P(None, None, tensor),
            P(None, tensor, dp),
            P(),
            P(None, dp, tensor),
            P(None, tensor),
            P(None, tensor, dp),
            P(),
        ),
        check_vma=False,
    )
```

time: 1150 us -> 641 us (0.56)
  waiting for transfers between devices: 823 us -> 228 us
  starting transfers between devices: 2 us -> 162 us
  blocking collectives: 105 us -> 0 us
  local copies, waits for them, and re-layouts: 43.3 us -> 135 us
  matrix products: 98 us -> 56.7 us
  between operations: 16.2 us -> 3.35 us
    reduce_scatter x9 -> x0, waiting for transfers between devices: 397 us -> none  [the longest x4 166 us: sum_forward(): lax.psum_scatter(term(jnp.int32(0), local_rows * lax.axis_size('tensor'))...]
    all_gather x8 -> x0, waiting for transfers between devices: 278 us -> none  [the longest x4 151 us: share_rows(): return lax.all_gather(values, 'tensor', axis=0, tiled=True)]
    ppermute x0 -> x115, waiting for transfers between devices: none -> 228 us  [the longest x69 177 us: ring(): lax.ppermute(values, RINGS[axis], [(i, (i + step) % 4) for i in range(4)])]
    ppermute x0 -> x115, starting transfers between devices: none -> 162 us  [the longest x69 66.2 us: ring(): lax.ppermute(values, RINGS[axis], [(i, (i + step) % 4) for i in range(4)])]
    unnamed x23 -> x0, waiting for transfers between devices: 148 us -> none
    psum x2 -> x0, blocking collectives: 105 us -> none  [the longest x1 69.2 us: send_vectors(): lax.psum((gain_terms, shift_terms, bias_out, bias_down), ('dp', 'tensor'))]
    dynamic_slice x0 -> x12, local copies, waits for them, and re-layouts: none -> 43.9 us  [the longest x10 43.3 us: pick(): lax.dynamic_index_in_dim(blocks, (place + step) % 4, 1, keepdims=False)]
    unnamed x269 -> x215, local copies, waits for them, and re-layouts: 31.5 us -> 53.5 us
  transfers between devices with their start and end apart: 20 -> 115, of which waited for: 20 -> 67; matrix products, arithmetic and copies ran while one was open for 8% -> 19% of each run, Pallas kernels for 0% -> 0%
where the time goes in v1:
time: 641 us; the launch traced here: 630 us
  waiting for transfers between devices  228 us (36%)
  starting transfers between devices  162 us (25%)
  local copies, waits for them, and re-layouts  135 us (21%)
  matrix products  56.7 us (9%)
  other arithmetic  44.9 us (7%)
    ppermute x69, waiting for transfers between devices, ring(): lax.ppermute(values, RINGS[axis], [(i, (i + step) % 4) for i in range(4)])  177 us
    ppermute x69, starting transfers between devices, ring(): lax.ppermute(values, RINGS[axis], [(i, (i + step) % 4) for i in range(4)])  66.2 us
    unnamed x215, local copies, waits for them, and re-layouts  53.5 us
    dynamic_slice x10, local copies, waits for them, and re-layouts, pick(): lax.dynamic_index_in_dim(blocks, (place + step) % 4, 1, keepdims=False)  43.3 us
    ppermute x9, waiting for transfers between devices, fetch_weights(): lax.ppermute(values, ('yh', 'c', 'yl'), y_pairs(lambda y, c: (y - step, y...  28.3 us
    ppermute x17, starting transfers between devices, swap_cores(): return lax.ppermute(values, 'c', [(0, 1), (1, 0)])  24.8 us
    ppermute x4, starting transfers between devices, scatter_grads(): lax.ppermute(pick_high((y + 3) % 4 // 2).astype(BF), axes, y_pairs(lambda...  18 us
    ppermute x4, starting transfers between devices, scatter_grads(): lax.ppermute(pick_high((y + 1) % 4 // 2).astype(BF), axes, y_pairs(lambda...  17.4 us
  transfers between devices with their start and end apart: 115, of which 67 were waited for; matrix products, arithmetic and copies ran while one was open for 19% of the time, Pallas kernels for 0%

profile of v1, /device:TPU:1, one launch (start us, length us, event | category | flops | bytes accessed | tf_op | source)
XLA Modules:
  0.0 630.1 jit_solution(5490206786235787647)
XLA Ops:
  12.9 3.6 collective-permute-start.3
  24.9 3.7 collective-permute-done.2
  53.0 9.8 %collective-permute-done.9 = bf16[128,1024]{1,0:T(8,128)(2,1)S(1)} collective-permute-done((bf16[128,1024]{1,0:T(8,128)(2,1)S(1)}, bf16[128,1024]{1,0:T(8,128)(2,1)S(1)}, u32[]{:S(2)}, u32[]{:S(2)}) %collective-permute-start.9) | collective-permute-done | bytes 262176 | tf_op jit(solution)/shard_map/ppermute | solution.py:39
  62.8 4.3 collective-permute-done.10
  69.9 6.8 %collective-permute-done.14 = bf16[128,1024]{1,0:T(8,128)(2,1)S(1)} collective-permute-done((bf16[128,1024]{1,0:T(8,128)(2,1)S(1)}, bf16[128,1024]{1,0:T(8,128)(2,1)S(1)}, u32[]{:S(2)}, u32[]{:S(2)}) %collective-permute-start.14) | collective-permute-done | bytes 262176 | tf_op jit(solution)/shard_map/ppermute | solution.py:39
  79.7 3.6 collective-permute-done.12
  88.2 12.3 %collective-permute-done.16 = bf16[1024,512]{1,0:T(8,128)(2,1)S(1)} collective-permute-done((bf16[1024,512]{1,0:T(8,128)(2,1)S(1)}, bf16[1024,512]{1,0:T(8,128)(2,1)S(1)}, u32[]{:S(2)}, u32[]{:S(2)}) %collective-permute-start.16) | collective-permute-done | bytes 1048608 | tf_op jit(solution)/shard_map/ppermute | solution.py:64
  110.2 6.0 collective-permute-done.19
  117.8 6.6 %collective-permute-done.20 = bf16[128,1024]{1,0:T(8,128)(2,1)S(1)} collective-permute-done((bf16[128,1024]{1,0:T(8,128)(2,1)S(1)}, bf16[128,1024]{1,0:T(8,128)(2,1)S(1)}, u32[]{:S(2)}, u32[]{:S(2)}) %collective-permute-start.20) | collective-permute-done | bytes 262176 | tf_op jit(solution)/shard_map/ppermute | solution.py:39
  127.7 7.0 %collective-permute-done.24 = bf16[128,1024]{1,0:T(8,128)(2,1)S(1)} collective-permute-done((bf16[128,1024]{1,0:T(8,128)(2,1)S(1)}, bf16[128,1024]{1,0:T(8,128)(2,1)S(1)}, u32[]{:S(2)}, u32[]{:S(2)}) %collective-permute-start.24) | collective-permute-done | bytes 262176 | tf_op jit(solution)/shard_map/ppermute | solution.py:39
  137.5 3.6 collective-permute-done.22
  143.9 4.1 collective-permute-start.27
  167.8 5.9 collective-permute-done.43
  178.8 4.5 collective-permute-done.46
  196.7 6.4 %collective-permute-done.34 = bf16[128,1024]{1,0:T(8,128)(2,1)S(1)} collective-permute-done((bf16[128,1024]{1,0:T(8,128)(2,1)S(1)}, bf16[128,1024]{1,0:T(8,128)(2,1)S(1)}, u32[]{:S(2)}, u32[]{:S(2)}) %collective-permute-start.34) | collective-permute-done | bytes 262176 | tf_op jit(solution)/shard_map/ppermute | solution.py:39
  208.8 12.2 %collective-permute-done.36 = bf16[1024,512]{1,0:T(8,128)(2,1)S(1)} collective-permute-done((bf16[1024,512]{1,0:T(8,128)(2,1)S(1)}, bf16[1024,512]{1,0:T(8,128)(2,1)S(1)}, u32[]{:S(2)}, u32[]{:S(2)}) %collective-permute-start.36) | collective-permute-done | bytes 1048608 | tf_op jit(solution)/shard_map/ppermute | solution.py:64
  239.3 7.1 %collective-permute-done.50 = bf16[128,1024]{1,0:T(8,128)(2,1)S(1)} collective-permute-done((bf16[128,1024]{1,0:T(8,128)(2,1)S(1)}, bf16[128,1024]{1,0:T(8,128)(2,1)S(1)}, u32[]{:S(2)}, u32[]{:S(2)}) %collective-permute-start.50) | collective-permute-done | bytes 262176 | tf_op jit(solution)/shard_map/ppermute | solution.py:39
  250.5 6.3 %collective-permute-done.40 = bf16[128,1024]{1,0:T(8,128)(2,1)S(1)} collective-permute-done((bf16[128,1024]{1,0:T(8,128)(2,1)S(1)}, bf16[128,1024]{1,0:T(8,128)(2,1)S(1)}, u32[]{:S(2)}, u32[]{:S(2)}) %collective-permute-start.40) | collective-permute-done | bytes 262176 | tf_op jit(solution)/shard_map/ppermute | solution.py:39
  260.8 7.1 %collective-permute-done.54 = bf16[128,1024]{1,0:T(8,128)(2,1)S(1)} collective-permute-done((bf16[128,1024]{1,0:T(8,128)(2,1)S(1)}, bf16[128,1024]{1,0:T(8,128)(2,1)S(1)}, u32[]{:S(2)}, u32[]{:S(2)}) %collective-permute-start.54) | collective-permute-done | bytes 262176 | tf_op jit(solution)/shard_map/ppermute | solution.py:39
  292.4 3.7 fusion.119
  307.6 6.4 %collective-permute-done.58 = bf16[128,1024]{1,0:T(8,128)(2,1)S(1)} collective-permute-done((bf16[128,1024]{1,0:T(8,128)(2,1)S(1)}, bf16[128,1024]{1,0:T(8,128)(2,1)S(1)}, u32[]{:S(2)}, u32[]{:S(2)}) %collective-permute-start.58) | collective-permute-done | bytes 262176 | tf_op jit(solution)/shard_map/ppermute | solution.py:39
  319.9 5.6 reshape.533
  325.5 4.1 constant_dynamic-slice_fusion.4
  329.5 3.7 copy.84
  355.8 5.6 reshape.531
  361.5 15.1 %constant_dynamic-slice_fusion.3 = (bf16[2,1,128,1024]{2,1,0,3:T(2,128)(2,1)}, bf16[2,1,128,1024]{2,1,0,3:T(2,128)(2,1)}, bf16[2,1,128,1024]{2,1,0,3:T(2,128)(2,...) fusion(f32[2,4,128,1024]{2,1,0,3:T(4,128)} %reshape.533, ...), kind=kLoop, calls=%fused_computation.324 | loop fusion | bytes 6291468 | tf_op jit(solution)/shard_map/jit(dynamic_index_in_dim)/dynamic_slice | solution.py:102
  388.4 3.5 copy.111
  395.9 3.5 copy.108
  399.4 3.5 copy.107
  405.6 4.9 fusion.171
  411.1 4.1 constant_dynamic-slice_fusion.8
  415.2 3.7 copy.80
  427.2 4.9 collective-permute-start.112
  436.6 4.9 collective-permute-start.105
  452.7 3.7 collective-permute-done.66
  458.9 5.2 collective-permute-done.70
  466.9 8.5 %collective-permute-start.71 = (bf16[512,1024]{1,0:T(8,128)(2,1)S(1)}, bf16[512,1024]{1,0:T(8,128)(2,1)S(1)}, u32[]{:S(2)}, u32[]{:S(2)}) collective-permute-start(bf16[512,1024]{1,0:T(8,128)(2,1)S(1)} %pad_maximum_fusion.11), channel_id=1, source_target_pairs={{0,8},{8,0},{1,9},{9,1},{2,10},{10,2},{3,11},{11,3},{4,12},{12,4},... | collective-permute-start | bytes 3145736 | tf_op jit(solution)/shard_map/ppermute | solution.py:43
  496.7 6.8 %constant_dynamic-slice_fusion.12 = (bf16[2,1,128,512]{2,1,0,3:T(2,128)(2,1)}, bf16[2,1,128,512]{2,1,0,3:T(2,128)(2,1)}, bf16[2,1,128,512]{2,1,0,3:T(2,128)(2,1)...) fusion(f32[2,4,128,512]{2,1,0,3:T(4,128)S(1)} %reshape.527, ...), kind=kLoop, calls=%fused_computation.333 | loop fusion | bytes 3145740 | tf_op jit(solution)/shard_map/jit(dynamic_index_in_dim)/dynamic_slice | solution.py:102
  514.6 4.2 collective-permute-start.87
  528.2 4.7 collective-permute-done.96
  533.9 3.8 collective-permute-done.95
  541.5 11.8 %collective-permute-start.97 = (bf16[128,512]{1,0:T(8,128)(2,1)S(1)}, bf16[128,512]{1,0:T(8,128)(2,1)S(1)}, u32[]{:S(2)}, u32[]{:S(2)}) collective-permute-start(bf16[128,512]{1,0:T(8,128)(2,1)S(1)} %get-tuple-element.143), channel_id=1, source_target_pairs={{8,12},{4,64},{72,76},{68,0},{9,13},{5,65},{73,77},{69,1},{10,14},... | collective-permute-start | bytes 393224 | tf_op jit(solution)/shard_map/ppermute | solution.py:117
  554.0 4.9 collective-permute-start.98
  574.0 6.5 %collective-permute-done.73 = bf16[128,1024]{1,0:T(8,128)(2,1)} collective-permute-done((bf16[128,1024]{1,0:T(8,128)(2,1)}, bf16[128,1024]{1,0:T(8,128)(2,1)}, u32[]{:S(2)}, u32[]{:S(2)}) %collective-permute-start.73) | collective-permute-done | bytes 262176 | tf_op jit(solution)/shard_map/ppermute | solution.py:39
  582.1 6.4 %collective-permute-done.74 = bf16[128,1024]{1,0:T(8,128)(2,1)} collective-permute-done((bf16[128,1024]{1,0:T(8,128)(2,1)}, bf16[128,1024]{1,0:T(8,128)(2,1)}, u32[]{:S(2)}, u32[]{:S(2)}) %collective-permute-start.74) | collective-permute-done | bytes 262176 | tf_op jit(solution)/shard_map/ppermute | solution.py:39
  598.5 3.7 collective-permute-start.83
  603.8 4.1 collective-permute-done.82
  611.7 8.7 %collective-permute-start.76 = (f32[128,1024]{1,0:T(8,128)S(1)}, f32[128,1024]{1,0:T(8,128)S(1)}, u32[]{:S(2)}, u32[]{:S(2)}) collective-permute-start(f32[128,1024]{1,0:T(8,128)S(1)} %add_add_fusion.4), channel_id=1, source_target_pairs={{0,0},{4,8},{8,4},{12,12},{1,1},{5,9},{9,5},{13,13},{2,2},{6,10},{... | collective-permute-start | bytes 1572872 | tf_op jit(solution)/shard_map/ppermute | solution.py:47
  (618 shorter events, 345.5 us)
Async XLA Ops:
  2.0 29.0 %collective-permute-start.6 = (f32[12,128]{1,0:T(8,128)S(1)}, f32[12,128]{1,0:T(8,128)S(1)}, u32[]{:S(2)}, u32[]{:S(2)}) collective-permute-start(f32[12,128]{1,0:T(8,128)S(1)} %pad_maximum_fusion.22), channel_id=1, source_target_pairs={{0,4},{8,0},{4,12},{12,72},{64,68},{72,64},{68,76},{76,8},{1,5},{9... | collective-permute-start | bytes 18440 | tf_op jit(solution)/shard_map/ppermute | solution.py:64
  8.4 34.6 %collective-permute-start.7 = (bf16[128,1024]{1,0:T(8,128)(2,1)S(1)}, bf16[128,1024]{1,0:T(8,128)(2,1)S(1)}, u32[]{:S(2)}, u32[]{:S(2)}) collective-permute-start(bf16[128,1024]{1,0:T(8,128)(2,1)S(1)} %get-tuple-element.148), channel_id=1, source_target_pairs={{0,4},{8,0},{4,12},{12,72},{64,68},{72,64},{68,76},{76,8},{1,5},{9... | collective-permute-start | bytes 786440 | tf_op jit(solution)/shard_map/ppermute | solution.py:64
  22.3 12.6 %collective-permute-start.5 = (bf16[1024,384]{0,1:T(8,128)(2,1)}, bf16[1024,384]{0,1:T(8,128)(2,1)S(1)}, u32[]{:S(2)}, u32[]{:S(2)}) collective-permute-start(bf16[1024,384]{0,1:T(8,128)(2,1)} %bitcast.385), channel_id=1, source_target_pairs={{0,68},{8,0},{4,12},{12,8},{64,4},{72,64},{68,76},{76,72},{1,69},{... | collective-permute-start | bytes 2359304 | tf_op jit(solution)/shard_map/ppermute | solution.py:64
  48.6 14.2 %collective-permute-start.9 = (bf16[128,1024]{1,0:T(8,128)(2,1)S(1)}, bf16[128,1024]{1,0:T(8,128)(2,1)S(1)}, u32[]{:S(2)}, u32[]{:S(2)}) collective-permute-start(bf16[128,1024]{1,0:T(8,128)(2,1)S(1)} %get-tuple-element.137), channel_id=1, source_target_pairs={{0,3},{1,0},{2,1},{3,2},{4,7},{5,4},{6,5},{7,6},{8,11},{9,8},{10,9... | collective-permute-start | bytes 786440 | tf_op jit(solution)/shard_map/ppermute | solution.py:39
  52.2 14.9 %collective-permute-start.10 = (bf16[128,1024]{1,0:T(8,128)(2,1)S(1)}, bf16[128,1024]{1,0:T(8,128)(2,1)S(1)}, u32[]{:S(2)}, u32[]{:S(2)}) collective-permute-start(bf16[128,1024]{1,0:T(8,128)(2,1)S(1)} %get-tuple-element.139), channel_id=1, source_target_pairs={{0,1},{1,2},{2,3},{3,0},{4,5},{5,6},{6,7},{7,4},{8,9},{9,10},{10,1... | collective-permute-start | bytes 786440 | tf_op jit(solution)/shard_map/ppermute | solution.py:39
  68.6 14.7 %collective-permute-start.12 = (bf16[128,1024]{1,0:T(8,128)(2,1)S(1)}, bf16[128,1024]{1,0:T(8,128)(2,1)S(1)}, u32[]{:S(2)}, u32[]{:S(2)}) collective-permute-start(bf16[128,1024]{1,0:T(8,128)(2,1)S(1)} %get-tuple-element.81), channel_id=1, source_target_pairs={{0,1},{1,2},{2,3},{3,0},{4,5},{5,6},{6,7},{7,4},{8,9},{9,10},{10,1... | collective-permute-start | bytes 786440 | tf_op jit(solution)/shard_map/ppermute | solution.py:39
  85.1 15.5 %collective-permute-start.16 = (bf16[1024,512]{1,0:T(8,128)(2,1)S(1)}, bf16[1024,512]{1,0:T(8,128)(2,1)S(1)}, u32[]{:S(2)}, u32[]{:S(2)}) collective-permute-start(bf16[1024,512]{1,0:T(8,128)(2,1)S(1)} %get-tuple-element.101), channel_id=1, source_target_pairs={{0,4},{8,0},{4,12},{12,72},{64,68},{72,64},{68,76},{76,8},{1,5},{9... | collective-permute-start | bytes 3145736 | tf_op jit(solution)/shard_map/ppermute | solution.py:64
  86.3 15.5 %collective-permute-start.17 = (bf16[512,1024]{1,0:T(8,128)(2,1)S(1)}, bf16[512,1024]{1,0:T(8,128)(2,1)S(1)}, u32[]{:S(2)}, u32[]{:S(2)}) collective-permute-start(bf16[512,1024]{1,0:T(8,128)(2,1)S(1)} %get-tuple-element.103), channel_id=1, source_target_pairs={{0,68},{8,0},{4,12},{12,8},{64,4},{72,64},{68,76},{76,72},{1,69},{... | collective-permute-start | bytes 3145736 | tf_op jit(solution)/shard_map/ppermute | solution.py:64
  109.5 14.9 %collective-permute-start.20 = (bf16[128,1024]{1,0:T(8,128)(2,1)S(1)}, bf16[128,1024]{1,0:T(8,128)(2,1)S(1)}, u32[]{:S(2)}, u32[]{:S(2)}) collective-permute-start(bf16[128,1024]{1,0:T(8,128)(2,1)S(1)} %get-tuple-element.136), channel_id=1, source_target_pairs={{0,1},{1,2},{2,3},{3,0},{4,5},{5,6},{6,7},{7,4},{8,9},{9,10},{10,1... | collective-permute-start | bytes 786440 | tf_op jit(solution)/shard_map/ppermute | solution.py:39
  126.2 14.9 %collective-permute-start.22 = (bf16[128,1024]{1,0:T(8,128)(2,1)S(1)}, bf16[128,1024]{1,0:T(8,128)(2,1)S(1)}, u32[]{:S(2)}, u32[]{:S(2)}) collective-permute-start(bf16[128,1024]{1,0:T(8,128)(2,1)S(1)} %get-tuple-element.75), channel_id=1, source_target_pairs={{0,1},{1,2},{2,3},{3,0},{4,5},{5,6},{6,7},{7,4},{8,9},{9,10},{10,1... | collective-permute-start | bytes 786440 | tf_op jit(solution)/shard_map/ppermute | solution.py:39
  143.9 18.4 %collective-permute-start.27 = (bf16[128,1024]{1,0:T(8,128)(2,1)}, bf16[128,1024]{1,0:T(8,128)(2,1)S(1)}, u32[]{:S(2)}, u32[]{:S(2)}) collective-permute-start(bf16[128,1024]{1,0:T(8,128)(2,1)} %get-tuple-element.147), channel_id=1, source_target_pairs={{0,4},{8,0},{4,12},{12,72},{64,68},{72,64},{68,76},{76,8},{1,5},{9... | collective-permute-start | bytes 786440 | tf_op jit(solution)/shard_map/ppermute | solution.py:64
  163.2 12.4 %collective-permute-start.28 = (bf16[512,1024]{1,0:T(8,128)(2,1)S(1)}, bf16[512,1024]{1,0:T(8,128)(2,1)S(1)}, u32[]{:S(2)}, u32[]{:S(2)}) collective-permute-start(bf16[512,1024]{1,0:T(8,128)(2,1)S(1)} %slice.583), channel_id=1, source_target_pairs={{0,8},{8,0},{1,9},{9,1},{2,10},{10,2},{3,11},{11,3},{4,12},{12,4},... | collective-permute-start | bytes 3145736 | tf_op jit(solution)/shard_map/ppermute | solution.py:43
  174.2 12.6 %collective-permute-start.45 = (bf16[128,1024]{1,0:T(8,128)(2,1)S(1)}, bf16[128,1024]{1,0:T(8,128)(2,1)S(1)}, u32[]{:S(2)}, u32[]{:S(2)}) collective-permute-start(bf16[128,1024]{1,0:T(8,128)(2,1)S(1)} %collective-permute-done.43), channel_id=1, source_target_pairs={{0,3},{1,0},{2,1},{3,2},{4,7},{5,4},{6,5},{7,6},{8,11},{9,8},{10,9... | collective-permute-start | bytes 786440 | tf_op jit(solution)/shard_map/ppermute | solution.py:39
  175.1 13.7 %collective-permute-start.44 = (bf16[128,1024]{1,0:T(8,128)(2,1)S(1)}, bf16[128,1024]{1,0:T(8,128)(2,1)S(1)}, u32[]{:S(2)}, u32[]{:S(2)}) collective-permute-start(bf16[128,1024]{1,0:T(8,128)(2,1)S(1)} %collective-permute-done.43), channel_id=1, source_target_pairs={{0,1},{1,2},{2,3},{3,0},{4,5},{5,6},{6,7},{7,4},{8,9},{9,10},{10,1... | collective-permute-start | bytes 786440 | tf_op jit(solution)/shard_map/ppermute | solution.py:39
  176.1 13.1 %collective-permute-start.29 = (bf16[128,1024]{1,0:T(8,128)(2,1)S(1)}, bf16[128,1024]{1,0:T(8,128)(2,1)S(1)}, u32[]{:S(2)}, u32[]{:S(2)}) collective-permute-start(bf16[128,1024]{1,0:T(8,128)(2,1)S(1)} %get-tuple-element.131), channel_id=1, source_target_pairs={{0,3},{1,0},{2,1},{3,2},{4,7},{5,4},{6,5},{7,6},{8,11},{9,8},{10,9... | collective-permute-start | bytes 786440 | tf_op jit(solution)/shard_map/ppermute | solution.py:39
  178.4 13.1 %collective-permute-start.31 = (bf16[128,1024]{1,0:T(8,128)(2,1)S(1)}, bf16[128,1024]{1,0:T(8,128)(2,1)S(1)}, u32[]{:S(2)}, u32[]{:S(2)}) collective-permute-start(bf16[128,1024]{1,0:T(8,128)(2,1)S(1)} %get-tuple-element.132), channel_id=1, source_target_pairs={{0,2},{1,3},{2,0},{3,1},{4,6},{5,7},{6,4},{7,5},{8,10},{9,11},{10,... | collective-permute-start | bytes 786440 | tf_op jit(solution)/shard_map/ppermute | solution.py:39
  188.9 18.0 %collective-permute-start.47 = (bf16[512,1024]{1,0:T(8,128)(2,1)S(1)}, bf16[512,1024]{1,0:T(8,128)(2,1)S(1)}, u32[]{:S(2)}, u32[]{:S(2)}) collective-permute-start(bf16[512,1024]{1,0:T(8,128)(2,1)S(1)} %pad_maximum_fusion.8), channel_id=1, source_target_pairs={{0,8},{8,0},{1,9},{9,1},{2,10},{10,2},{3,11},{11,3},{4,12},{12,4},... | collective-permute-start | bytes 3145736 | tf_op jit(solution)/shard_map/ppermute | solution.py:43
  206.0 14.9 %collective-permute-start.36 = (bf16[1024,512]{1,0:T(8,128)(2,1)S(1)}, bf16[1024,512]{1,0:T(8,128)(2,1)S(1)}, u32[]{:S(2)}, u32[]{:S(2)}) collective-permute-start(bf16[1024,512]{1,0:T(8,128)(2,1)S(1)} %copy-done.38), channel_id=1, source_target_pairs={{0,4},{8,0},{4,12},{12,72},{64,68},{72,64},{68,76},{76,8},{1,5},{9... | collective-permute-start | bytes 3145736 | tf_op jit(solution)/shard_map/ppermute | solution.py:64
  206.5 15.7 %collective-permute-start.37 = (bf16[512,1024]{1,0:T(8,128)(2,1)S(1)}, bf16[512,1024]{1,0:T(8,128)(2,1)S(1)}, u32[]{:S(2)}, u32[]{:S(2)}) collective-permute-start(bf16[512,1024]{1,0:T(8,128)(2,1)S(1)} %copy-done.39), channel_id=1, source_target_pairs={{0,68},{8,0},{4,12},{12,8},{64,4},{72,64},{68,76},{76,72},{1,69},{... | collective-permute-start | bytes 3145736 | tf_op jit(solution)/shard_map/ppermute | solution.py:64
  230.6 15.8 %collective-permute-start.50 = (bf16[128,1024]{1,0:T(8,128)(2,1)S(1)}, bf16[128,1024]{1,0:T(8,128)(2,1)S(1)}, u32[]{:S(2)}, u32[]{:S(2)}) collective-permute-start(bf16[128,1024]{1,0:T(8,128)(2,1)S(1)} %get-tuple-element.127), channel_id=1, source_target_pairs={{0,1},{1,2},{2,3},{3,0},{4,5},{5,6},{6,7},{7,4},{8,9},{9,10},{10,1... | collective-permute-start | bytes 786440 | tf_op jit(solution)/shard_map/ppermute | solution.py:39
  232.0 17.0 %collective-permute-start.39 = (bf16[128,1024]{1,0:T(8,128)(2,1)S(1)}, bf16[128,1024]{1,0:T(8,128)(2,1)S(1)}, u32[]{:S(2)}, u32[]{:S(2)}) collective-permute-start(bf16[128,1024]{1,0:T(8,128)(2,1)S(1)} %get-tuple-element.128), channel_id=1, source_target_pairs={{0,3},{1,0},{2,1},{3,2},{4,7},{5,4},{6,5},{7,6},{8,11},{9,8},{10,9... | collective-permute-start | bytes 786440 | tf_op jit(solution)/shard_map/ppermute | solution.py:39
  234.5 16.1 %collective-permute-start.41 = (bf16[128,1024]{1,0:T(8,128)(2,1)S(1)}, bf16[128,1024]{1,0:T(8,128)(2,1)S(1)}, u32[]{:S(2)}, u32[]{:S(2)}) collective-permute-start(bf16[128,1024]{1,0:T(8,128)(2,1)S(1)} %get-tuple-element.129), channel_id=1, source_target_pairs={{0,2},{1,3},{2,0},{3,1},{4,6},{5,7},{6,4},{7,5},{8,10},{9,11},{10,... | collective-permute-start | bytes 786440 | tf_op jit(solution)/shard_map/ppermute | solution.py:39
  237.7 19.2 %collective-permute-start.40 = (bf16[128,1024]{1,0:T(8,128)(2,1)S(1)}, bf16[128,1024]{1,0:T(8,128)(2,1)S(1)}, u32[]{:S(2)}, u32[]{:S(2)}) collective-permute-start(bf16[128,1024]{1,0:T(8,128)(2,1)S(1)} %get-tuple-element.130), channel_id=1, source_target_pairs={{0,1},{1,2},{2,3},{3,0},{4,5},{5,6},{6,7},{7,4},{8,9},{9,10},{10,1... | collective-permute-start | bytes 786440 | tf_op jit(solution)/shard_map/ppermute | solution.py:39
  259.5 14.8 %collective-permute-start.52 = (bf16[128,1024]{1,0:T(8,128)(2,1)S(1)}, bf16[128,1024]{1,0:T(8,128)(2,1)S(1)}, u32[]{:S(2)}, u32[]{:S(2)}) collective-permute-start(bf16[128,1024]{1,0:T(8,128)(2,1)S(1)} %get-tuple-element.45), channel_id=1, source_target_pairs={{0,1},{1,2},{2,3},{3,0},{4,5},{5,6},{6,7},{7,4},{8,9},{9,10},{10,1... | collective-permute-start | bytes 786440 | tf_op jit(solution)/shard_map/ppermute | solution.py:39
  298.9 15.0 %collective-permute-start.58 = (bf16[128,1024]{1,0:T(8,128)(2,1)S(1)}, bf16[128,1024]{1,0:T(8,128)(2,1)S(1)}, u32[]{:S(2)}, u32[]{:S(2)}) collective-permute-start(bf16[128,1024]{1,0:T(8,128)(2,1)S(1)} %get-tuple-element.124), channel_id=1, source_target_pairs={{0,1},{1,2},{2,3},{3,0},{4,5},{5,6},{6,7},{7,4},{8,9},{9,10},{10,1... | collective-permute-start | bytes 786440 | tf_op jit(solution)/shard_map/ppermute | solution.py:39
  301.1 32.2 %collective-permute-start.42 = (f32[128,1024]{1,0:T(8,128)}, f32[128,1024]{1,0:T(8,128)}, u32[]{:S(2)}, u32[]{:S(2)}) collective-permute-start(f32[128,1024]{1,0:T(8,128)} %get-tuple-element.146), channel_id=1, source_target_pairs={{0,0},{4,8},{8,4},{12,12},{1,1},{5,9},{9,5},{13,13},{2,2},{6,10},{... | collective-permute-start | bytes 1572872 | tf_op jit(solution)/shard_map/ppermute | solution.py:47
  315.6 17.7 %collective-permute-start.62 = (bf16[128,1024]{1,0:T(8,128)(2,1)S(1)}, bf16[128,1024]{1,0:T(8,128)(2,1)}, u32[]{:S(2)}, u32[]{:S(2)}) collective-permute-start(bf16[128,1024]{1,0:T(8,128)(2,1)S(1)} %get-tuple-element.42), channel_id=1, source_target_pairs={{0,2},{1,3},{2,0},{3,1},{4,6},{5,7},{6,4},{7,5},{8,10},{9,11},{10,... | collective-permute-start | bytes 786440 | tf_op jit(solution)/shard_map/ppermute | solution.py:39
  315.9 17.4 %collective-permute-start.61 = (bf16[128,1024]{1,0:T(8,128)(2,1)S(1)}, bf16[128,1024]{1,0:T(8,128)(2,1)}, u32[]{:S(2)}, u32[]{:S(2)}) collective-permute-start(bf16[128,1024]{1,0:T(8,128)(2,1)S(1)} %get-tuple-element.42), channel_id=1, source_target_pairs={{0,3},{1,0},{2,1},{3,2},{4,7},{5,4},{6,5},{7,6},{8,11},{9,8},{10,9... | collective-permute-start | bytes 786440 | tf_op jit(solution)/shard_map/ppermute | solution.py:39
  316.1 17.2 %collective-permute-start.60 = (bf16[128,1024]{1,0:T(8,128)(2,1)S(1)}, bf16[128,1024]{1,0:T(8,128)(2,1)}, u32[]{:S(2)}, u32[]{:S(2)}) collective-permute-start(bf16[128,1024]{1,0:T(8,128)(2,1)S(1)} %get-tuple-element.42), channel_id=1, source_target_pairs={{0,1},{1,2},{2,3},{3,0},{4,5},{5,6},{6,7},{7,4},{8,9},{9,10},{10,1... | collective-permute-start | bytes 786440 | tf_op jit(solution)/shard_map/ppermute | solution.py:39
  380.0 30.5 %collective-permute-start.110 = (bf16[2,128,1024]{2,1,0:T(8,128)(2,1)}, bf16[2,128,1024]{2,1,0:T(8,128)(2,1)}, u32[]{:S(2)}, u32[]{:S(2)}) collective-permute-start(bf16[2,128,1024]{2,1,0:T(8,128)(2,1)} %bitcast.270), channel_id=1, source_target_pairs={{0,32},{16,48},{32,0},{48,16},{1,33},{17,49},{33,1},{49,17},{2,34}... | collective-permute-start | bytes 1572872 | tf_op jit(solution)/shard_map/ppermute | solution.py:39
  392.0 28.8 %collective-permute-start.109 = (bf16[2,128,1024]{2,1,0:T(8,128)(2,1)}, bf16[2,128,1024]{2,1,0:T(8,128)(2,1)}, u32[]{:S(2)}, u32[]{:S(2)}) collective-permute-start(bf16[2,128,1024]{2,1,0:T(8,128)(2,1)} %bitcast.271), channel_id=1, source_target_pairs={{0,48},{16,0},{32,16},{48,32},{1,49},{17,1},{33,17},{49,33},{2,50}... | collective-permute-start | bytes 1572872 | tf_op jit(solution)/shard_map/ppermute | solution.py:39
  392.8 29.4 %collective-permute-start.108 = (bf16[2,128,1024]{2,1,0:T(8,128)(2,1)}, bf16[2,128,1024]{2,1,0:T(8,128)(2,1)}, u32[]{:S(2)}, u32[]{:S(2)}) collective-permute-start(bf16[2,128,1024]{2,1,0:T(8,128)(2,1)} %bitcast.272), channel_id=1, source_target_pairs={{0,16},{16,32},{32,48},{48,0},{1,17},{17,33},{33,49},{49,1},{2,18}... | collective-permute-start | bytes 1572872 | tf_op jit(solution)/shard_map/ppermute | solution.py:39
  403.0 23.6 %collective-permute-start.101 = (bf16[2,128,1024]{2,1,0:T(8,128)(2,1)}, bf16[2,128,1024]{2,1,0:T(8,128)(2,1)}, u32[]{:S(2)}, u32[]{:S(2)}) collective-permute-start(bf16[2,128,1024]{2,1,0:T(8,128)(2,1)} %bitcast.389), channel_id=1, source_target_pairs={{0,16},{16,32},{32,48},{48,0},{1,17},{17,33},{33,49},{49,1},{2,18}... | collective-permute-start | bytes 1572872 | tf_op jit(solution)/shard_map/ppermute | solution.py:39
  403.3 23.9 %collective-permute-start.102 = (bf16[2,128,1024]{2,1,0:T(8,128)(2,1)}, bf16[2,128,1024]{2,1,0:T(8,128)(2,1)}, u32[]{:S(2)}, u32[]{:S(2)}) collective-permute-start(bf16[2,128,1024]{2,1,0:T(8,128)(2,1)} %bitcast.388), channel_id=1, source_target_pairs={{0,48},{16,0},{32,16},{48,32},{1,49},{17,1},{33,17},{49,33},{2,50}... | collective-permute-start | bytes 1572872 | tf_op jit(solution)/shard_map/ppermute | solution.py:39
  410.5 21.6 %collective-permute-start.103 = (bf16[2,128,1024]{2,1,0:T(8,128)(2,1)S(1)}, bf16[2,128,1024]{2,1,0:T(8,128)(2,1)}, u32[]{:S(2)}, u32[]{:S(2)}) collective-permute-start(bf16[2,128,1024]{2,1,0:T(8,128)(2,1)S(1)} %bitcast.387), channel_id=1, source_target_pairs={{0,32},{16,48},{32,0},{48,16},{1,33},{17,49},{33,1},{49,17},{2,34}... | collective-permute-start | bytes 1572872 | tf_op jit(solution)/shard_map/ppermute | solution.py:39
  420.7 22.3 %collective-permute-start.64 = (bf16[512,1024]{1,0:T(8,128)(2,1)S(1)}, bf16[512,1024]{1,0:T(8,128)(2,1)S(1)}, u32[]{:S(2)}, u32[]{:S(2)}) collective-permute-start(bf16[512,1024]{1,0:T(8,128)(2,1)S(1)} %slice.579), channel_id=1, source_target_pairs={{0,8},{8,0},{1,9},{9,1},{2,10},{10,2},{3,11},{11,3},{4,12},{12,4},... | collective-permute-start | bytes 3145736 | tf_op jit(solution)/shard_map/ppermute | solution.py:43
  427.2 14.3 %collective-permute-start.112 = (bf16[128,1024]{1,0:T(8,128)(2,1)S(1)}, bf16[128,1024]{1,0:T(8,128)(2,1)S(1)}, u32[]{:S(2)}, u32[]{:S(2)}) collective-permute-start(bf16[128,1024]{1,0:T(8,128)(2,1)S(1)} %get-tuple-element.115), channel_id=1, source_target_pairs={{8,76},{4,0},{72,12},{68,64},{9,77},{5,1},{73,13},{69,65},{10,78},... | collective-permute-start | bytes 786440 | tf_op jit(solution)/shard_map/ppermute | solution.py:122
  441.7 17.1 %collective-permute-start.114 = (f32[64,1024]{1,0:T(8,128)S(1)}, f32[64,1024]{1,0:T(8,128)S(1)}, u32[]{:S(2)}, u32[]{:S(2)}) collective-permute-start(f32[64,1024]{1,0:T(8,128)S(1)} %dynamic-slice_bitcast_fusion), channel_id=1, source_target_pairs={{0,8},{12,4},{1,9},{13,5},{2,10},{14,6},{3,11},{15,7},{16,24},{28,... | collective-permute-start | bytes 786440 | tf_op jit(solution)/shard_map/ppermute | solution.py:137
  514.6 38.7 %collective-permute-start.87 = (bf16[2,128,512]{2,1,0:T(8,128)(2,1)}, bf16[2,128,512]{2,1,0:T(8,128)(2,1)}, u32[]{:S(2)}, u32[]{:S(2)}) collective-permute-start(bf16[2,128,512]{2,1,0:T(8,128)(2,1)} %bitcast.281), channel_id=1, source_target_pairs={{0,16},{16,32},{32,48},{48,0},{1,17},{17,33},{33,49},{49,1},{2,18}... | collective-permute-start | bytes 786440 | tf_op jit(solution)/shard_map/ppermute | solution.py:39
  518.9 35.2 %collective-permute-start.88 = (bf16[2,128,512]{2,1,0:T(8,128)(2,1)}, bf16[2,128,512]{2,1,0:T(8,128)(2,1)}, u32[]{:S(2)}, u32[]{:S(2)}) collective-permute-start(bf16[2,128,512]{2,1,0:T(8,128)(2,1)} %bitcast.280), channel_id=1, source_target_pairs={{0,48},{16,0},{32,16},{48,32},{1,49},{17,1},{33,17},{49,33},{2,50}... | collective-permute-start | bytes 786440 | tf_op jit(solution)/shard_map/ppermute | solution.py:39
  518.9 14.0 %collective-permute-start.96 = (bf16[2,128,512]{2,1,0:T(8,128)(2,1)}, bf16[2,128,512]{2,1,0:T(8,128)(2,1)}, u32[]{:S(2)}, u32[]{:S(2)}) collective-permute-start(bf16[2,128,512]{2,1,0:T(8,128)(2,1)} %bitcast.393), channel_id=1, source_target_pairs={{0,32},{16,48},{32,0},{48,16},{1,33},{17,49},{33,1},{49,17},{2,34}... | collective-permute-start | bytes 786440 | tf_op jit(solution)/shard_map/ppermute | solution.py:39
  521.9 15.9 %collective-permute-start.95 = (bf16[2,128,512]{2,1,0:T(8,128)(2,1)}, bf16[2,128,512]{2,1,0:T(8,128)(2,1)}, u32[]{:S(2)}, u32[]{:S(2)}) collective-permute-start(bf16[2,128,512]{2,1,0:T(8,128)(2,1)} %bitcast.392), channel_id=1, source_target_pairs={{0,48},{16,0},{32,16},{48,32},{1,49},{17,1},{33,17},{49,33},{2,50}... | collective-permute-start | bytes 786440 | tf_op jit(solution)/shard_map/ppermute | solution.py:39
  522.9 17.4 %collective-permute-start.94 = (bf16[2,128,512]{2,1,0:T(8,128)(2,1)}, bf16[2,128,512]{2,1,0:T(8,128)(2,1)}, u32[]{:S(2)}, u32[]{:S(2)}) collective-permute-start(bf16[2,128,512]{2,1,0:T(8,128)(2,1)} %bitcast.391), channel_id=1, source_target_pairs={{0,16},{16,32},{32,48},{48,0},{1,17},{17,33},{33,49},{49,1},{2,18}... | collective-permute-start | bytes 786440 | tf_op jit(solution)/shard_map/ppermute | solution.py:39
  532.8 26.1 %collective-permute-start.89 = (bf16[2,128,512]{2,1,0:T(8,128)(2,1)S(1)}, bf16[2,128,512]{2,1,0:T(8,128)(2,1)S(1)}, u32[]{:S(2)}, u32[]{:S(2)}) collective-permute-start(bf16[2,128,512]{2,1,0:T(8,128)(2,1)S(1)} %bitcast.390), channel_id=1, source_target_pairs={{0,32},{16,48},{32,0},{48,16},{1,33},{17,49},{33,1},{49,17},{2,34}... | collective-permute-start | bytes 786440 | tf_op jit(solution)/shard_map/ppermute | solution.py:39
  537.7 33.3 %collective-permute-start.72 = (bf16[512,1024]{1,0:T(8,128)(2,1)S(1)}, bf16[512,1024]{1,0:T(8,128)(2,1)S(1)}, u32[]{:S(2)}, u32[]{:S(2)}) collective-permute-start(bf16[512,1024]{1,0:T(8,128)(2,1)S(1)} %slice.578), channel_id=1, source_target_pairs={{0,8},{8,0},{1,9},{9,1},{2,10},{10,2},{3,11},{11,3},{4,12},{12,4},... | collective-permute-start | bytes 3145736 | tf_op jit(solution)/shard_map/ppermute | solution.py:43
  541.5 20.3 %collective-permute-start.97 = (bf16[128,512]{1,0:T(8,128)(2,1)S(1)}, bf16[128,512]{1,0:T(8,128)(2,1)S(1)}, u32[]{:S(2)}, u32[]{:S(2)}) collective-permute-start(bf16[128,512]{1,0:T(8,128)(2,1)S(1)} %get-tuple-element.143), channel_id=1, source_target_pairs={{8,12},{4,64},{72,76},{68,0},{9,13},{5,65},{73,77},{69,1},{10,14},... | collective-permute-start | bytes 393224 | tf_op jit(solution)/shard_map/ppermute | solution.py:117
  573.2 15.2 %collective-permute-start.74 = (bf16[128,1024]{1,0:T(8,128)(2,1)}, bf16[128,1024]{1,0:T(8,128)(2,1)}, u32[]{:S(2)}, u32[]{:S(2)}) collective-permute-start(bf16[128,1024]{1,0:T(8,128)(2,1)} %get-tuple-element.118), channel_id=1, source_target_pairs={{0,1},{1,2},{2,3},{3,0},{4,5},{5,6},{6,7},{7,4},{8,9},{9,10},{10,1... | collective-permute-start | bytes 786440 | tf_op jit(solution)/shard_map/ppermute | solution.py:39
  611.7 15.5 %collective-permute-start.76 = (f32[128,1024]{1,0:T(8,128)S(1)}, f32[128,1024]{1,0:T(8,128)S(1)}, u32[]{:S(2)}, u32[]{:S(2)}) collective-permute-start(f32[128,1024]{1,0:T(8,128)S(1)} %add_add_fusion.4), channel_id=1, source_target_pairs={{0,0},{4,8},{8,4},{12,12},{1,1},{5,9},{9,5},{13,13},{2,2},{6,10},{... | collective-permute-start | bytes 1572872 | tf_op jit(solution)/shard_map/ppermute | solution.py:47
  (145 other events, 1111.0 us)

commit v2 on v1

--- a/solution.py
+++ b/solution.py
@@ -85,35 +85,36 @@
     from_after = ring(low[rows : 2 * rows], "z", -1)
     from_before = ring(low[2 * rows : 3 * rows], "z", 1)
     from_across = ring(low[3 * rows :], "z", 2)
-    return (
+    total = (
         both[:rows]
         + from_after.astype(F32)
         + from_before.astype(F32)
         + from_across.astype(F32)
     )
-
-
-def scatter_grads(grad):
-    columns = grad.shape[1]
-    blocks = grad.reshape(2, 4, 128, columns)
+    return total, low
+
+
+def scatter_grads(grads):
+    count, _, columns = grads.shape
+    blocks = grads.reshape(count, 2, 4, 128, columns)
     place = lax.axis_index("x")
 
     def pick(step):
-        return lax.dynamic_index_in_dim(blocks, (place + step) % 4, 1, keepdims=False)
+        return lax.dynamic_index_in_dim(blocks, (place + step) % 4, 2, keepdims=False)
 
     summed = (
         pick(0).astype(F32)
-        + ring(pick(1).astype(BF), "x", 1).astype(F32)
-        + ring(pick(3).astype(BF), "x", -1).astype(F32)
-        + ring(pick(2).astype(BF), "x", 2).astype(F32)
-    )
-    high = lax.axis_index("yh")
-    y = high * 2 + lax.axis_index("yl")
+        + ring(pick(1), "x", 1).astype(F32)
+        + ring(pick(3), "x", -1).astype(F32)
+        + ring(pick(2), "x", 2).astype(F32)
+    )
+    high, low_place, core = lax.axis_index("yh"), lax.axis_index("yl"), lax.axis_index("c")
 
     def pick_high(index):
-        return lax.dynamic_index_in_dim(summed, index, 0, keepdims=False)
+        return jnp.where(index == 0, summed[:, 0], summed[:, 1])
 
     axes = ("yh", "c", "yl")
+    y = high * 2 + low_place
     up = lax.ppermute(
         pick_high(((y + 1) % 4) // 2).astype(BF),
         axes,
@@ -130,12 +131,11 @@
         y_pairs(lambda y, c: (y + 2, c) if c == y % 2 else None),
     )
     total = pick_high(high) + up.astype(F32) + down.astype(F32) + far.astype(F32)
-    core = lax.axis_index("c")
-    halves = total.reshape(2, 64, columns)
-    keep = lax.dynamic_index_in_dim(halves, core, 0, keepdims=False)
-    give = lax.dynamic_index_in_dim(halves, 1 - core, 0, keepdims=False)
+    first, second = total[:, :64], total[:, 64:]
+    keep = jnp.where(core == 0, first, second)
+    give = jnp.where(core == 0, second, first)
     got = lax.ppermute(give, ("c", "yl"), [(0, 2), (3, 1)])
-    return jnp.where(core == lax.axis_index("yl"), keep, got)
+    return jnp.where(core == low_place, keep, got)
 
 
 def sum_everywhere(values):
@@ -230,7 +230,7 @@
         values = (projected[:, 2 * columns :] + bias_in[layer, 1]).astype(BF)
         attended, log_totals = attend_forward(queries, keys, values, mask)
         middle = stream + (
-            scatter_rows(jnp.dot(attended, w_out[layer], preferred_element_type=F32))
+            scatter_rows(jnp.dot(attended, w_out[layer], preferred_element_type=F32))[0]
             + outward_bias[layer]
         )
         normed_mid = layer_norm(middle, norm_gain[layer, 1], norm_shift[layer, 1]).astype(BF)
@@ -240,7 +240,7 @@
         )
         activated = gelu_tanh(hidden_pre).astype(BF)
         result = middle + (
-            scatter_rows(jnp.dot(activated, w_down[layer], preferred_element_type=F32))
+            scatter_rows(jnp.dot(activated, w_down[layer], preferred_element_type=F32))[0]
             + shrink_bias[layer]
         )
         saved.append(
@@ -262,10 +262,11 @@
         grad_act = against_rows(dy_all, w_down[layer])
         du = jax.vjp(gelu_tanh, hidden_pre)[1](grad_act)[0].astype(BF)
         sums_up[layer] = jnp.sum(du, 0, dtype=F32)
-        dh = scatter_rows(against_rows(du, w_up[layer]))
+        dh, sent = scatter_rows(against_rows(du, w_up[layer]))
+        du, dy_all, sent = lax.optimization_barrier((du, dy_all, sent))
         grads_mlp[layer] = scatter_grads(
-            jnp.concatenate(
-                [tokens_inner(dy_all, activated), tokens_inner(mid_all, du)], 1
+            jnp.stack(
+                [tokens_inner(dy_all, activated).astype(BF), tokens_inner(mid_all, du).astype(BF)]
             )
         )
         back_mid = jax.vjp(layer_norm, middle, norm_gain[layer, 1], norm_shift[layer, 1])[1]
@@ -278,11 +279,16 @@
         dq, dk, dv = attend_backward(queries, keys, values, do, log_totals, mask)
         sums_in[layer] = jnp.stack([jnp.sum(dq, 0, dtype=F32), jnp.sum(dv, 0, dtype=F32)])
         dqkv = jnp.concatenate([dq, dk, dv], 1)
-        da = scatter_rows(against_rows(dqkv, w_in[layer]))
+        da, sent = scatter_rows(against_rows(dqkv, w_in[layer]))
+        dqkv, dz_all, sent = lax.optimization_barrier((dqkv, dz_all, sent))
         grads_attn[layer] = scatter_grads(
             jnp.concatenate(
-                [tokens_inner(dz_all, attended), tokens_inner(normed_all, dqkv)], 1
-            )
+                [
+                    tokens_inner(dz_all, attended).astype(BF),
+                    tokens_inner(normed_all, dqkv).astype(BF),
+                ],
+                1,
+            )[None]
         )
         back_in = jax.vjp(layer_norm, stream, norm_gain[layer, 0], norm_shift[layer, 0])[1]
         grad_first, gains[layer, 0], shifts[layer, 0] = back_in(da)
@@ -318,19 +324,18 @@
     grad_up_bias = lax.dynamic_index_in_dim(up, own, 1, keepdims=False)
     grad_in_bias = lax.dynamic_index_in_dim(qv, own, 2, keepdims=False)
 
-    width = activated.shape[1]
     return (
         hidden_out,
         grad_hidden,
         grad_gain,
         grad_shift,
-        jnp.stack([g[:, columns:].reshape(-1, 3, columns) for g in grads_attn]),
+        jnp.stack([g[0, :, columns:].reshape(-1, 3, columns) for g in grads_attn]),
         grad_in_bias,
-        jnp.stack([g[:, :columns].T for g in grads_attn]),
+        jnp.stack([g[0, :, :columns].T for g in grads_attn]),
         grad_out_bias,
-        jnp.stack([g[:, width:] for g in grads_mlp]),
+        jnp.stack([g[1] for g in grads_mlp]),
         grad_up_bias,
-        jnp.stack([g[:, :width].T for g in grads_mlp]),
+        jnp.stack([g[0].T for g in grads_mlp]),
         grad_down_bias,
     )
 

time: 641 us -> 561 us (0.88)
  the two profiles are of different devices: /device:TPU:1 before, /device:TPU:0 now
where the time goes in v2:
time: 561 us; the launch traced here: 551 us
  waiting for transfers between devices  215 us (38%)
  starting transfers between devices  157 us (28%)
  local copies, waits for them, and re-layouts  64.7 us (12%)
  matrix products  60.4 us (11%)
  other arithmetic  50.6 us (9%)
    ppermute x69, waiting for transfers between devices, ring(): lax.ppermute(values, RINGS[axis], [(i, (i + step) % 4) for i in range(4)])  166 us
    ppermute x69, starting transfers between devices, ring(): lax.ppermute(values, RINGS[axis], [(i, (i + step) % 4) for i in range(4)])  88.5 us
    ppermute x9, waiting for transfers between devices, fetch_weights(): lax.ppermute(values, ('yh', 'c', 'yl'), y_pairs(lambda y, c: (y - step, y...  29 us
    unnamed x285, local copies, waits for them, and re-layouts  25 us
    ppermute x17, starting transfers between devices, swap_cores(): return lax.ppermute(values, 'c', [(0, 1), (1, 0)])  16.3 us
    ppermute x9, starting transfers between devices, fetch_weights(): lax.ppermute(values, ('yh', 'c', 'yl'), y_pairs(lambda y, c: (y - step, y...  15.7 us
    ppermute x4, starting transfers between devices, scatter_grads(): lax.ppermute(pick_high(1 - high).astype(BF), axes, y_pairs(lambda y, c: (...  15.2 us
    dot_general x8, matrix products, against_rows(): lax.dot_general(left, right, (((1,), (1,)), ((), ())), preferred_element_...  13.7 us
  transfers between devices with their start and end apart: 115, of which 66 were waited for; matrix products, arithmetic and copies ran while one was open for 22% of the time, Pallas kernels for 0%

profile of v2, /device:TPU:0, one launch (start us, length us, event | category | flops | bytes accessed | tf_op | source)
XLA Modules:
  0.0 550.9 jit_solution(267407279123788836)
XLA Ops:
  12.3 4.0 collective-permute-start.3
  19.6 3.9 collective-permute-done.3
  25.4 3.4 collective-permute-done.2
  31.7 3.5 collective-permute-done.5
  47.6 3.7 collective-permute-start.9
  52.8 10.0 %collective-permute-done.9 = bf16[128,1024]{1,0:T(8,128)(2,1)S(1)} collective-permute-done((bf16[128,1024]{1,0:T(8,128)(2,1)S(1)}, bf16[128,1024]{1,0:T(8,128)(2,1)S(1)}, u32[]{:S(2)}, u32[]{:S(2)}) %collective-permute-start.9) | collective-permute-done | bytes 262176 | tf_op jit(solution)/shard_map/ppermute | solution.py:39
  62.8 3.7 collective-permute-done.10
  69.8 8.2 %collective-permute-done.14 = bf16[128,1024]{1,0:T(8,128)(2,1)S(1)} collective-permute-done((bf16[128,1024]{1,0:T(8,128)(2,1)S(1)}, bf16[128,1024]{1,0:T(8,128)(2,1)S(1)}, u32[]{:S(2)}, u32[]{:S(2)}) %collective-permute-start.14) | collective-permute-done | bytes 262176 | tf_op jit(solution)/shard_map/ppermute | solution.py:39
  89.4 8.5 %collective-permute-done.16 = bf16[1024,512]{1,0:T(8,128)(2,1)S(1)} collective-permute-done((bf16[1024,512]{1,0:T(8,128)(2,1)S(1)}, bf16[1024,512]{1,0:T(8,128)(2,1)S(1)}, u32[]{:S(2)}, u32[]{:S(2)}) %collective-permute-start.16) | collective-permute-done | bytes 1048608 | tf_op jit(solution)/shard_map/ppermute | solution.py:64
  109.7 7.0 %collective-permute-done.19 = bf16[128,1024]{1,0:T(8,128)(2,1)S(1)} collective-permute-done((bf16[128,1024]{1,0:T(8,128)(2,1)S(1)}, bf16[128,1024]{1,0:T(8,128)(2,1)S(1)}, u32[]{:S(2)}, u32[]{:S(2)}) %collective-permute-start.19) | collective-permute-done | bytes 262176 | tf_op jit(solution)/shard_map/ppermute | solution.py:39
  118.9 4.4 collective-permute-done.20
  127.5 8.0 %collective-permute-done.24 = bf16[128,1024]{1,0:T(8,128)(2,1)S(1)} collective-permute-done((bf16[128,1024]{1,0:T(8,128)(2,1)S(1)}, bf16[128,1024]{1,0:T(8,128)(2,1)S(1)}, u32[]{:S(2)}, u32[]{:S(2)}) %collective-permute-start.24) | collective-permute-done | bytes 262176 | tf_op jit(solution)/shard_map/ppermute | solution.py:39
  142.3 3.7 collective-permute-start.26
  151.9 4.0 collective-permute-done.26
  176.5 11.6 %collective-permute-start.47 = (bf16[512,1024]{1,0:T(8,128)(2,1)S(1)}, bf16[512,1024]{1,0:T(8,128)(2,1)S(1)}, u32[]{:S(2)}, u32[]{:S(2)}) collective-permute-start(bf16[512,1024]{1,0:T(8,128)(2,1)S(1)} %pad_maximum_fusion.4), channel_id=1, source_target_pairs={{0,8},{8,0},{1,9},{9,1},{2,10},{10,2},{3,11},{11,3},{4,12},{12,4},... | collective-permute-start | bytes 3145736 | tf_op jit(solution)/shard_map/ppermute | solution.py:43
  191.4 5.4 collective-permute-done.34
  196.8 2.9 collective-permute-done.33
  199.7 3.4 collective-permute-done.32
  205.1 3.0 collective-permute-start.37
  208.5 9.0 %collective-permute-done.36 = bf16[1024,512]{1,0:T(8,128)(2,1)S(1)} collective-permute-done((bf16[1024,512]{1,0:T(8,128)(2,1)S(1)}, bf16[1024,512]{1,0:T(8,128)(2,1)S(1)}, u32[]{:S(2)}, u32[]{:S(2)}) %collective-permute-start.36) | collective-permute-done | bytes 1048608 | tf_op jit(solution)/shard_map/ppermute | solution.py:64
  220.4 3.4 convert_reduce_fusion
  240.5 5.7 %collective-permute-done.50 = bf16[128,1024]{1,0:T(8,128)(2,1)S(1)} collective-permute-done((bf16[128,1024]{1,0:T(8,128)(2,1)S(1)}, bf16[128,1024]{1,0:T(8,128)(2,1)S(1)}, u32[]{:S(2)}, u32[]{:S(2)}) %collective-permute-start.50) | collective-permute-done | bytes 262176 | tf_op jit(solution)/shard_map/ppermute | solution.py:39
  251.8 4.7 collective-permute-done.40
  261.7 8.2 %collective-permute-done.54 = bf16[128,1024]{1,0:T(8,128)(2,1)S(1)} collective-permute-done((bf16[128,1024]{1,0:T(8,128)(2,1)S(1)}, bf16[128,1024]{1,0:T(8,128)(2,1)S(1)}, u32[]{:S(2)}, u32[]{:S(2)}) %collective-permute-start.54) | collective-permute-done | bytes 262176 | tf_op jit(solution)/shard_map/ppermute | solution.py:39
  292.4 3.8 convolution_convert_fusion.1
  302.0 3.1 collective-permute-start.110
  309.7 4.7 collective-permute-done.58
  318.5 10.1 %collective-permute-done.109 = bf16[2,2,128,512]{3,2,0,1:T(8,128)(2,1)S(1)} collective-permute-done((bf16[2,2,128,512]{3,2,0,1:T(8,128)(2,1)S(1)}, bf16[2,2,128,512]{3,2,0,1:T(8,128)(2,1)S(1)}, u32[]{:S(2)}, u32[]{:S(2)}) %collective-permute-start.109) | collective-permute-done | bytes 524320 | tf_op jit(solution)/shard_map/ppermute | solution.py:39
  337.3 3.2 collective-permute-start.113
  352.1 3.5 convert_reduce_fusion.1
  370.3 3.3 collective-permute-start.65
  380.0 2.9 collective-permute-start.103
  391.9 7.6 %collective-permute-done.70 = bf16[128,1024]{1,0:T(8,128)(2,1)S(1)} collective-permute-done((bf16[128,1024]{1,0:T(8,128)(2,1)S(1)}, bf16[128,1024]{1,0:T(8,128)(2,1)S(1)}, u32[]{:S(2)}, u32[]{:S(2)}) %collective-permute-start.70) | collective-permute-done | bytes 262176 | tf_op jit(solution)/shard_map/ppermute | solution.py:39
  402.5 6.4 %collective-permute-done.68 = bf16[128,1024]{1,0:T(8,128)(2,1)} collective-permute-done((bf16[128,1024]{1,0:T(8,128)(2,1)S(1)}, bf16[128,1024]{1,0:T(8,128)(2,1)}, u32[]{:S(2)}, u32[]{:S(2)}) %collective-permute-start.68) | collective-permute-done | bytes 262176 | tf_op jit(solution)/shard_map/ppermute | solution.py:39
  415.0 4.3 collective-permute-start.106
  427.8 5.9 %convert_reduce_fusion.6 = (f32[2,64]{1,0:T(2,128)}, bf16[2,64,1024]{2,1,0:T(8,128)(2,1)S(1)}) fusion(bf16[1024,2,64]{0,2,1:T(8,128)(2,1)S(1)} %bitcast.317, f32[2,1024,1024]{1,2,0:T(8,128)} %copy-done, f32[2,1024]{1,0:T(2,128)S(1)} %log_add_fusion), kind=kOutput, calls=%fused_computation.220 | convolution fusion | flops 273022848 | bytes 8921600 | tf_op jit(solution)/shard_map/hqk,qhd->khd/dot_general | solution.py:187
  447.2 4.0 fusion.127
  456.7 5.4 constant_dynamic-slice_fusion.5
  472.1 2.8 collective-permute-start.89
  482.3 6.4 %collective-permute-done.94 = bf16[1,2,128,512]{3,2,1,0:T(8,128)(2,1)S(1)} collective-permute-done((bf16[1,2,128,512]{3,2,1,0:T(8,128)(2,1)S(1)}, bf16[1,2,128,512]{3,2,1,0:T(8,128)(2,1)S(1)}, u32[]{:S(2)}, u32[]{:S(2)}) %collective-permute-start.94) | collective-permute-done | bytes 262176 | tf_op jit(solution)/shard_map/ppermute | solution.py:39
  489.9 4.4 collective-permute-done.95
  498.5 3.8 collective-permute-start.99
  505.1 3.3 collective-permute-done.98
  508.4 3.8 collective-permute-start.92
  512.2 2.8 collective-permute-start.80
  515.2 3.4 collective-permute-start.78
  523.1 7.0 %collective-permute-start.83 = (f32[192,128]{1,0:T(8,128)S(1)}, f32[192,128]{1,0:T(8,128)S(1)}, u32[]{:S(2)}, u32[]{:S(2)}) collective-permute-start(f32[192,128]{1,0:T(8,128)S(1)} %add_add_fusion.9), channel_id=1, source_target_pairs={{0,48},{16,0},{32,16},{48,32},{1,49},{17,1},{33,17},{49,33},{2,50}... | collective-permute-start | bytes 294920 | tf_op jit(solution)/shard_map/ppermute | solution.py:39
  533.4 3.7 collective-permute-done.82
  (685 shorter events, 304.5 us)
Async XLA Ops:
  2.0 27.6 %collective-permute-start.6 = (f32[12,128]{1,0:T(8,128)S(1)}, f32[12,128]{1,0:T(8,128)S(1)}, u32[]{:S(2)}, u32[]{:S(2)}) collective-permute-start(f32[12,128]{1,0:T(8,128)S(1)} %pad_maximum_fusion.16), channel_id=1, source_target_pairs={{0,4},{8,0},{4,12},{12,72},{64,68},{72,64},{68,76},{76,8},{1,5},{9... | collective-permute-start | bytes 18440 | tf_op jit(solution)/shard_map/ppermute | solution.py:64
  7.0 36.3 %collective-permute-start.7 = (bf16[128,1024]{1,0:T(8,128)(2,1)S(1)}, bf16[128,1024]{1,0:T(8,128)(2,1)S(1)}, u32[]{:S(2)}, u32[]{:S(2)}) collective-permute-start(bf16[128,1024]{1,0:T(8,128)(2,1)S(1)} %get-tuple-element.168), channel_id=1, source_target_pairs={{0,4},{8,0},{4,12},{12,72},{64,68},{72,64},{68,76},{76,8},{1,5},{9... | collective-permute-start | bytes 786440 | tf_op jit(solution)/shard_map/ppermute | solution.py:64
  16.3 12.5 %collective-permute-start.2 = (bf16[128,1024]{1,0:T(8,128)(2,1)S(1)}, bf16[128,1024]{1,0:T(8,128)(2,1)S(1)}, u32[]{:S(2)}, u32[]{:S(2)}) collective-permute-start(bf16[128,1024]{1,0:T(8,128)(2,1)S(1)} %get-tuple-element.103), channel_id=1, source_target_pairs={{0,3},{1,0},{2,1},{3,2},{4,7},{5,4},{6,5},{7,6},{8,11},{9,8},{10,9... | collective-permute-start | bytes 786440 | tf_op jit(solution)/shard_map/ppermute | solution.py:39
  47.6 15.2 %collective-permute-start.9 = (bf16[128,1024]{1,0:T(8,128)(2,1)S(1)}, bf16[128,1024]{1,0:T(8,128)(2,1)S(1)}, u32[]{:S(2)}, u32[]{:S(2)}) collective-permute-start(bf16[128,1024]{1,0:T(8,128)(2,1)S(1)} %get-tuple-element.157), channel_id=1, source_target_pairs={{0,3},{1,0},{2,1},{3,2},{4,7},{5,4},{6,5},{7,6},{8,11},{9,8},{10,9... | collective-permute-start | bytes 786440 | tf_op jit(solution)/shard_map/ppermute | solution.py:39
  51.5 15.0 %collective-permute-start.10 = (bf16[128,1024]{1,0:T(8,128)(2,1)S(1)}, bf16[128,1024]{1,0:T(8,128)(2,1)S(1)}, u32[]{:S(2)}, u32[]{:S(2)}) collective-permute-start(bf16[128,1024]{1,0:T(8,128)(2,1)S(1)} %get-tuple-element.159), channel_id=1, source_target_pairs={{0,1},{1,2},{2,3},{3,0},{4,5},{5,6},{6,7},{7,4},{8,9},{9,10},{10,1... | collective-permute-start | bytes 786440 | tf_op jit(solution)/shard_map/ppermute | solution.py:39
  69.0 13.4 %collective-permute-start.12 = (bf16[128,1024]{1,0:T(8,128)(2,1)S(1)}, bf16[128,1024]{1,0:T(8,128)(2,1)S(1)}, u32[]{:S(2)}, u32[]{:S(2)}) collective-permute-start(bf16[128,1024]{1,0:T(8,128)(2,1)S(1)} %get-tuple-element.97), channel_id=1, source_target_pairs={{0,1},{1,2},{2,3},{3,0},{4,5},{5,6},{6,7},{7,4},{8,9},{9,10},{10,1... | collective-permute-start | bytes 786440 | tf_op jit(solution)/shard_map/ppermute | solution.py:39
  83.8 14.1 %collective-permute-start.16 = (bf16[1024,512]{1,0:T(8,128)(2,1)S(1)}, bf16[1024,512]{1,0:T(8,128)(2,1)S(1)}, u32[]{:S(2)}, u32[]{:S(2)}) collective-permute-start(bf16[1024,512]{1,0:T(8,128)(2,1)S(1)} %get-tuple-element.113), channel_id=1, source_target_pairs={{0,4},{8,0},{4,12},{12,72},{64,68},{72,64},{68,76},{76,8},{1,5},{9... | collective-permute-start | bytes 3145736 | tf_op jit(solution)/shard_map/ppermute | solution.py:64
  86.7 14.8 %collective-permute-start.17 = (bf16[512,1024]{1,0:T(8,128)(2,1)S(1)}, bf16[512,1024]{1,0:T(8,128)(2,1)S(1)}, u32[]{:S(2)}, u32[]{:S(2)}) collective-permute-start(bf16[512,1024]{1,0:T(8,128)(2,1)S(1)} %get-tuple-element.115), channel_id=1, source_target_pairs={{0,68},{8,0},{4,12},{12,8},{64,4},{72,64},{68,76},{76,72},{1,69},{... | collective-permute-start | bytes 3145736 | tf_op jit(solution)/shard_map/ppermute | solution.py:64
  108.9 14.5 %collective-permute-start.20 = (bf16[128,1024]{1,0:T(8,128)(2,1)S(1)}, bf16[128,1024]{1,0:T(8,128)(2,1)S(1)}, u32[]{:S(2)}, u32[]{:S(2)}) collective-permute-start(bf16[128,1024]{1,0:T(8,128)(2,1)S(1)} %get-tuple-element.156), channel_id=1, source_target_pairs={{0,1},{1,2},{2,3},{3,0},{4,5},{5,6},{6,7},{7,4},{8,9},{9,10},{10,1... | collective-permute-start | bytes 786440 | tf_op jit(solution)/shard_map/ppermute | solution.py:39
  126.7 13.4 %collective-permute-start.22 = (bf16[128,1024]{1,0:T(8,128)(2,1)S(1)}, bf16[128,1024]{1,0:T(8,128)(2,1)S(1)}, u32[]{:S(2)}, u32[]{:S(2)}) collective-permute-start(bf16[128,1024]{1,0:T(8,128)(2,1)S(1)} %get-tuple-element.91), channel_id=1, source_target_pairs={{0,1},{1,2},{2,3},{3,0},{4,5},{5,6},{6,7},{7,4},{8,9},{9,10},{10,1... | collective-permute-start | bytes 786440 | tf_op jit(solution)/shard_map/ppermute | solution.py:39
  142.3 13.5 %collective-permute-start.26 = (bf16[1024,384]{0,1:T(8,128)(2,1)}, bf16[1024,384]{0,1:T(8,128)(2,1)S(1)}, u32[]{:S(2)}, u32[]{:S(2)}) collective-permute-start(bf16[1024,384]{0,1:T(8,128)(2,1)} %bitcast.348), channel_id=1, source_target_pairs={{0,68},{8,0},{4,12},{12,8},{64,4},{72,64},{68,76},{76,72},{1,69},{... | collective-permute-start | bytes 2359304 | tf_op jit(solution)/shard_map/ppermute | solution.py:64
  146.0 17.2 %collective-permute-start.27 = (bf16[128,1024]{1,0:T(8,128)(2,1)}, bf16[128,1024]{1,0:T(8,128)(2,1)S(1)}, u32[]{:S(2)}, u32[]{:S(2)}) collective-permute-start(bf16[128,1024]{1,0:T(8,128)(2,1)} %get-tuple-element.167), channel_id=1, source_target_pairs={{0,4},{8,0},{4,12},{12,72},{64,68},{72,64},{68,76},{76,8},{1,5},{9... | collective-permute-start | bytes 786440 | tf_op jit(solution)/shard_map/ppermute | solution.py:64
  169.0 19.0 %collective-permute-start.29 = (bf16[128,1024]{1,0:T(8,128)(2,1)S(1)}, bf16[128,1024]{1,0:T(8,128)(2,1)S(1)}, u32[]{:S(2)}, u32[]{:S(2)}) collective-permute-start(bf16[128,1024]{1,0:T(8,128)(2,1)S(1)} %get-tuple-element.151), channel_id=1, source_target_pairs={{0,3},{1,0},{2,1},{3,2},{4,7},{5,4},{6,5},{7,6},{8,11},{9,8},{10,9... | collective-permute-start | bytes 786440 | tf_op jit(solution)/shard_map/ppermute | solution.py:39
  171.5 16.5 %collective-permute-start.31 = (bf16[128,1024]{1,0:T(8,128)(2,1)S(1)}, bf16[128,1024]{1,0:T(8,128)(2,1)S(1)}, u32[]{:S(2)}, u32[]{:S(2)}) collective-permute-start(bf16[128,1024]{1,0:T(8,128)(2,1)S(1)} %get-tuple-element.152), channel_id=1, source_target_pairs={{0,2},{1,3},{2,0},{3,1},{4,6},{5,7},{6,4},{7,5},{8,10},{9,11},{10,... | collective-permute-start | bytes 786440 | tf_op jit(solution)/shard_map/ppermute | solution.py:39
  173.7 14.4 %collective-permute-start.30 = (bf16[128,1024]{1,0:T(8,128)(2,1)S(1)}, bf16[128,1024]{1,0:T(8,128)(2,1)S(1)}, u32[]{:S(2)}, u32[]{:S(2)}) collective-permute-start(bf16[128,1024]{1,0:T(8,128)(2,1)S(1)} %get-tuple-element.153), channel_id=1, source_target_pairs={{0,1},{1,2},{2,3},{3,0},{4,5},{5,6},{6,7},{7,4},{8,9},{9,10},{10,1... | collective-permute-start | bytes 786440 | tf_op jit(solution)/shard_map/ppermute | solution.py:39
  176.5 31.7 %collective-permute-start.47 = (bf16[512,1024]{1,0:T(8,128)(2,1)S(1)}, bf16[512,1024]{1,0:T(8,128)(2,1)S(1)}, u32[]{:S(2)}, u32[]{:S(2)}) collective-permute-start(bf16[512,1024]{1,0:T(8,128)(2,1)S(1)} %pad_maximum_fusion.4), channel_id=1, source_target_pairs={{0,8},{8,0},{1,9},{9,1},{2,10},{10,2},{3,11},{11,3},{4,12},{12,4},... | collective-permute-start | bytes 3145736 | tf_op jit(solution)/shard_map/ppermute | solution.py:43
  190.3 12.8 %collective-permute-start.32 = (bf16[128,1024]{1,0:T(8,128)(2,1)S(1)}, bf16[128,1024]{1,0:T(8,128)(2,1)S(1)}, u32[]{:S(2)}, u32[]{:S(2)}) collective-permute-start(bf16[128,1024]{1,0:T(8,128)(2,1)S(1)} %get-tuple-element.85), channel_id=1, source_target_pairs={{0,1},{1,2},{2,3},{3,0},{4,5},{5,6},{6,7},{7,4},{8,9},{9,10},{10,1... | collective-permute-start | bytes 786440 | tf_op jit(solution)/shard_map/ppermute | solution.py:39
  205.1 15.3 %collective-permute-start.37 = (bf16[512,1024]{1,0:T(8,128)(2,1)S(1)}, bf16[512,1024]{1,0:T(8,128)(2,1)S(1)}, u32[]{:S(2)}, u32[]{:S(2)}) collective-permute-start(bf16[512,1024]{1,0:T(8,128)(2,1)S(1)} %copy-done.41), channel_id=1, source_target_pairs={{0,68},{8,0},{4,12},{12,8},{64,4},{72,64},{68,76},{76,72},{1,69},{... | collective-permute-start | bytes 3145736 | tf_op jit(solution)/shard_map/ppermute | solution.py:64
  230.4 15.8 %collective-permute-start.50 = (bf16[128,1024]{1,0:T(8,128)(2,1)S(1)}, bf16[128,1024]{1,0:T(8,128)(2,1)S(1)}, u32[]{:S(2)}, u32[]{:S(2)}) collective-permute-start(bf16[128,1024]{1,0:T(8,128)(2,1)S(1)} %get-tuple-element.147), channel_id=1, source_target_pairs={{0,1},{1,2},{2,3},{3,0},{4,5},{5,6},{6,7},{7,4},{8,9},{9,10},{10,1... | collective-permute-start | bytes 786440 | tf_op jit(solution)/shard_map/ppermute | solution.py:39
  231.8 17.8 %collective-permute-start.39 = (bf16[128,1024]{1,0:T(8,128)(2,1)S(1)}, bf16[128,1024]{1,0:T(8,128)(2,1)S(1)}, u32[]{:S(2)}, u32[]{:S(2)}) collective-permute-start(bf16[128,1024]{1,0:T(8,128)(2,1)S(1)} %get-tuple-element.148), channel_id=1, source_target_pairs={{0,3},{1,0},{2,1},{3,2},{4,7},{5,4},{6,5},{7,6},{8,11},{9,8},{10,9... | collective-permute-start | bytes 786440 | tf_op jit(solution)/shard_map/ppermute | solution.py:39
  234.6 17.2 %collective-permute-start.41 = (bf16[128,1024]{1,0:T(8,128)(2,1)S(1)}, bf16[128,1024]{1,0:T(8,128)(2,1)S(1)}, u32[]{:S(2)}, u32[]{:S(2)}) collective-permute-start(bf16[128,1024]{1,0:T(8,128)(2,1)S(1)} %get-tuple-element.149), channel_id=1, source_target_pairs={{0,2},{1,3},{2,0},{3,1},{4,6},{5,7},{6,4},{7,5},{8,10},{9,11},{10,... | collective-permute-start | bytes 786440 | tf_op jit(solution)/shard_map/ppermute | solution.py:39
  238.3 18.2 %collective-permute-start.40 = (bf16[128,1024]{1,0:T(8,128)(2,1)S(1)}, bf16[128,1024]{1,0:T(8,128)(2,1)S(1)}, u32[]{:S(2)}, u32[]{:S(2)}) collective-permute-start(bf16[128,1024]{1,0:T(8,128)(2,1)S(1)} %get-tuple-element.150), channel_id=1, source_target_pairs={{0,1},{1,2},{2,3},{3,0},{4,5},{5,6},{6,7},{7,4},{8,9},{9,10},{10,1... | collective-permute-start | bytes 786440 | tf_op jit(solution)/shard_map/ppermute | solution.py:39
  259.6 12.6 %collective-permute-start.53 = (bf16[128,1024]{1,0:T(8,128)(2,1)S(1)}, bf16[128,1024]{1,0:T(8,128)(2,1)S(1)}, u32[]{:S(2)}, u32[]{:S(2)}) collective-permute-start(bf16[128,1024]{1,0:T(8,128)(2,1)S(1)} %get-tuple-element.61), channel_id=1, source_target_pairs={{0,3},{1,0},{2,1},{3,2},{4,7},{5,4},{6,5},{7,6},{8,11},{9,8},{10,9... | collective-permute-start | bytes 786440 | tf_op jit(solution)/shard_map/ppermute | solution.py:39
  260.9 13.6 %collective-permute-start.52 = (bf16[128,1024]{1,0:T(8,128)(2,1)S(1)}, bf16[128,1024]{1,0:T(8,128)(2,1)S(1)}, u32[]{:S(2)}, u32[]{:S(2)}) collective-permute-start(bf16[128,1024]{1,0:T(8,128)(2,1)S(1)} %get-tuple-element.61), channel_id=1, source_target_pairs={{0,1},{1,2},{2,3},{3,0},{4,5},{5,6},{6,7},{7,4},{8,9},{9,10},{10,1... | collective-permute-start | bytes 786440 | tf_op jit(solution)/shard_map/ppermute | solution.py:39
  299.5 14.9 %collective-permute-start.58 = (bf16[128,1024]{1,0:T(8,128)(2,1)S(1)}, bf16[128,1024]{1,0:T(8,128)(2,1)S(1)}, u32[]{:S(2)}, u32[]{:S(2)}) collective-permute-start(bf16[128,1024]{1,0:T(8,128)(2,1)S(1)} %get-tuple-element.144), channel_id=1, source_target_pairs={{0,1},{1,2},{2,3},{3,0},{4,5},{5,6},{6,7},{7,4},{8,9},{9,10},{10,1... | collective-permute-start | bytes 786440 | tf_op jit(solution)/shard_map/ppermute | solution.py:39
  302.0 16.4 %collective-permute-start.110 = (bf16[2,2,128,512]{3,2,0,1:T(8,128)(2,1)S(1)}, bf16[2,2,128,512]{3,2,0,1:T(8,128)(2,1)S(1)}, u32[]{:S(2)}, u32[]{:S(2)}) collective-permute-start(bf16[2,2,128,512]{3,2,0,1:T(8,128)(2,1)S(1)} %bitcast.351), channel_id=1, source_target_pairs={{0,32},{16,48},{32,0},{48,16},{1,33},{17,49},{33,1},{49,17},{2,34}... | collective-permute-start | bytes 1572872 | tf_op jit(solution)/shard_map/ppermute | solution.py:39
  305.1 23.5 %collective-permute-start.109 = (bf16[2,2,128,512]{3,2,0,1:T(8,128)(2,1)S(1)}, bf16[2,2,128,512]{3,2,0,1:T(8,128)(2,1)S(1)}, u32[]{:S(2)}, u32[]{:S(2)}) collective-permute-start(bf16[2,2,128,512]{3,2,0,1:T(8,128)(2,1)S(1)} %bitcast.350), channel_id=1, source_target_pairs={{0,48},{16,0},{32,16},{48,32},{1,49},{17,1},{33,17},{49,33},{2,50}... | collective-permute-start | bytes 1572872 | tf_op jit(solution)/shard_map/ppermute | solution.py:39
  307.5 21.1 %collective-permute-start.108 = (bf16[2,2,128,512]{3,2,0,1:T(8,128)(2,1)S(1)}, bf16[2,2,128,512]{3,2,0,1:T(8,128)(2,1)S(1)}, u32[]{:S(2)}, u32[]{:S(2)}) collective-permute-start(bf16[2,2,128,512]{3,2,0,1:T(8,128)(2,1)S(1)} %bitcast.349), channel_id=1, source_target_pairs={{0,16},{16,32},{32,48},{48,0},{1,17},{17,33},{33,49},{49,1},{2,18}... | collective-permute-start | bytes 1572872 | tf_op jit(solution)/shard_map/ppermute | solution.py:39
  317.1 20.1 %collective-permute-start.62 = (bf16[128,1024]{1,0:T(8,128)(2,1)S(1)}, bf16[128,1024]{1,0:T(8,128)(2,1)S(1)}, u32[]{:S(2)}, u32[]{:S(2)}) collective-permute-start(bf16[128,1024]{1,0:T(8,128)(2,1)S(1)} %get-tuple-element.58), channel_id=1, source_target_pairs={{0,2},{1,3},{2,0},{3,1},{4,6},{5,7},{6,4},{7,5},{8,10},{9,11},{10,... | collective-permute-start | bytes 786440 | tf_op jit(solution)/shard_map/ppermute | solution.py:39
  343.3 14.9 %collective-permute-start.42 = (f32[128,1024]{1,0:T(8,128)}, f32[128,1024]{1,0:T(8,128)S(1)}, u32[]{:S(2)}, u32[]{:S(2)}) collective-permute-start(f32[128,1024]{1,0:T(8,128)} %get-tuple-element.166), channel_id=1, source_target_pairs={{0,0},{4,8},{8,4},{12,12},{1,1},{5,9},{9,5},{13,13},{2,2},{6,10},{... | collective-permute-start | bytes 1572872 | tf_op jit(solution)/shard_map/ppermute | solution.py:47
  370.3 14.3 %collective-permute-start.65 = (bf16[128,1024]{1,0:T(8,128)(2,1)S(1)}, bf16[128,1024]{1,0:T(8,128)(2,1)S(1)}, u32[]{:S(2)}, u32[]{:S(2)}) collective-permute-start(bf16[128,1024]{1,0:T(8,128)(2,1)S(1)} %get-tuple-element.139), channel_id=1, source_target_pairs={{0,3},{1,0},{2,1},{3,2},{4,7},{5,4},{6,5},{7,6},{8,11},{9,8},{10,9... | collective-permute-start | bytes 786440 | tf_op jit(solution)/shard_map/ppermute | solution.py:39
  373.7 14.6 %collective-permute-start.66 = (bf16[128,1024]{1,0:T(8,128)(2,1)S(1)}, bf16[128,1024]{1,0:T(8,128)(2,1)S(1)}, u32[]{:S(2)}, u32[]{:S(2)}) collective-permute-start(bf16[128,1024]{1,0:T(8,128)(2,1)S(1)} %get-tuple-element.141), channel_id=1, source_target_pairs={{0,1},{1,2},{2,3},{3,0},{4,5},{5,6},{6,7},{7,4},{8,9},{9,10},{10,1... | collective-permute-start | bytes 786440 | tf_op jit(solution)/shard_map/ppermute | solution.py:39
  380.0 30.1 %collective-permute-start.103 = (bf16[2,2,128,512]{3,2,0,1:T(8,128)(2,1)}, bf16[2,2,128,512]{3,2,0,1:T(8,128)(2,1)}, u32[]{:S(2)}, u32[]{:S(2)}) collective-permute-start(bf16[2,2,128,512]{3,2,0,1:T(8,128)(2,1)} %bitcast.305), channel_id=1, source_target_pairs={{0,32},{16,48},{32,0},{48,16},{1,33},{17,49},{33,1},{49,17},{2,34}... | collective-permute-start | bytes 1572872 | tf_op jit(solution)/shard_map/ppermute | solution.py:39
  382.9 27.2 %collective-permute-start.102 = (bf16[2,2,128,512]{3,2,0,1:T(8,128)(2,1)}, bf16[2,2,128,512]{3,2,0,1:T(8,128)(2,1)}, u32[]{:S(2)}, u32[]{:S(2)}) collective-permute-start(bf16[2,2,128,512]{3,2,0,1:T(8,128)(2,1)} %bitcast.306), channel_id=1, source_target_pairs={{0,48},{16,0},{32,16},{48,32},{1,49},{17,1},{33,17},{49,33},{2,50}... | collective-permute-start | bytes 1572872 | tf_op jit(solution)/shard_map/ppermute | solution.py:39
  384.7 25.5 %collective-permute-start.101 = (bf16[2,2,128,512]{3,2,0,1:T(8,128)(2,1)}, bf16[2,2,128,512]{3,2,0,1:T(8,128)(2,1)}, u32[]{:S(2)}, u32[]{:S(2)}) collective-permute-start(bf16[2,2,128,512]{3,2,0,1:T(8,128)(2,1)} %bitcast.307), channel_id=1, source_target_pairs={{0,16},{16,32},{32,48},{48,0},{1,17},{17,33},{33,49},{49,1},{2,18}... | collective-permute-start | bytes 1572872 | tf_op jit(solution)/shard_map/ppermute | solution.py:39
  410.0 16.8 %collective-permute-start.71 = (bf16[512,1024]{1,0:T(8,128)(2,1)S(1)}, bf16[512,1024]{1,0:T(8,128)(2,1)S(1)}, u32[]{:S(2)}, u32[]{:S(2)}) collective-permute-start(bf16[512,1024]{1,0:T(8,128)(2,1)S(1)} %pad_maximum_fusion.7), channel_id=1, source_target_pairs={{0,8},{8,0},{1,9},{9,1},{2,10},{10,2},{3,11},{11,3},{4,12},{12,4},... | collective-permute-start | bytes 3145736 | tf_op jit(solution)/shard_map/ppermute | solution.py:43
  425.4 17.8 %collective-permute-start.107 = (f32[2,64,512]{2,1,0:T(8,128)S(1)}, f32[2,64,512]{2,1,0:T(8,128)S(1)}, u32[]{:S(2)}, u32[]{:S(2)}) collective-permute-start(f32[2,64,512]{2,1,0:T(8,128)S(1)} %slice_select_fusion.1), channel_id=1, source_target_pairs={{0,8},{12,4},{1,9},{13,5},{2,10},{14,6},{3,11},{15,7},{16,24},{28,... | collective-permute-start | bytes 786440 | tf_op jit(solution)/shard_map/ppermute | solution.py:137
  454.4 21.6 %collective-permute-start.73 = (bf16[128,1024]{1,0:T(8,128)(2,1)}, bf16[128,1024]{1,0:T(8,128)(2,1)}, u32[]{:S(2)}, u32[]{:S(2)}) collective-permute-start(bf16[128,1024]{1,0:T(8,128)(2,1)} %get-tuple-element.136), channel_id=1, source_target_pairs={{0,3},{1,0},{2,1},{3,2},{4,7},{5,4},{6,5},{7,6},{8,11},{9,8},{10,9... | collective-permute-start | bytes 786440 | tf_op jit(solution)/shard_map/ppermute | solution.py:39
  454.8 22.1 %collective-permute-start.75 = (bf16[128,1024]{1,0:T(8,128)(2,1)}, bf16[128,1024]{1,0:T(8,128)(2,1)}, u32[]{:S(2)}, u32[]{:S(2)}) collective-permute-start(bf16[128,1024]{1,0:T(8,128)(2,1)} %get-tuple-element.137), channel_id=1, source_target_pairs={{0,2},{1,3},{2,0},{3,1},{4,6},{5,7},{6,4},{7,5},{8,10},{9,11},{10,... | collective-permute-start | bytes 786440 | tf_op jit(solution)/shard_map/ppermute | solution.py:39
  455.6 23.7 %collective-permute-start.74 = (bf16[128,1024]{1,0:T(8,128)(2,1)}, bf16[128,1024]{1,0:T(8,128)(2,1)}, u32[]{:S(2)}, u32[]{:S(2)}) collective-permute-start(bf16[128,1024]{1,0:T(8,128)(2,1)} %get-tuple-element.138), channel_id=1, source_target_pairs={{0,1},{1,2},{2,3},{3,0},{4,5},{5,6},{6,7},{7,4},{8,9},{9,10},{10,1... | collective-permute-start | bytes 786440 | tf_op jit(solution)/shard_map/ppermute | solution.py:39
  472.1 23.2 %collective-permute-start.89 = (bf16[1,2,128,512]{3,2,1,0:T(8,128)(2,1)}, bf16[1,2,128,512]{3,2,1,0:T(8,128)(2,1)S(1)}, u32[]{:S(2)}, u32[]{:S(2)}) collective-permute-start(bf16[1,2,128,512]{3,2,1,0:T(8,128)(2,1)} %bitcast.84), channel_id=1, source_target_pairs={{0,32},{16,48},{32,0},{48,16},{1,33},{17,49},{33,1},{49,17},{2,34}... | collective-permute-start | bytes 786440 | tf_op jit(solution)/shard_map/ppermute | solution.py:39
  474.8 21.7 %collective-permute-start.88 = (bf16[1,2,128,512]{3,2,1,0:T(8,128)(2,1)S(1)}, bf16[1,2,128,512]{3,2,1,0:T(8,128)(2,1)S(1)}, u32[]{:S(2)}, u32[]{:S(2)}) collective-permute-start(bf16[1,2,128,512]{3,2,1,0:T(8,128)(2,1)S(1)} %bitcast.353), channel_id=1, source_target_pairs={{0,48},{16,0},{32,16},{48,32},{1,49},{17,1},{33,17},{49,33},{2,50}... | collective-permute-start | bytes 786440 | tf_op jit(solution)/shard_map/ppermute | solution.py:39
  476.0 12.7 %collective-permute-start.94 = (bf16[1,2,128,512]{3,2,1,0:T(8,128)(2,1)S(1)}, bf16[1,2,128,512]{3,2,1,0:T(8,128)(2,1)S(1)}, u32[]{:S(2)}, u32[]{:S(2)}) collective-permute-start(bf16[1,2,128,512]{3,2,1,0:T(8,128)(2,1)S(1)} %bitcast.356), channel_id=1, source_target_pairs={{0,16},{16,32},{32,48},{48,0},{1,17},{17,33},{33,49},{49,1},{2,18}... | collective-permute-start | bytes 786440 | tf_op jit(solution)/shard_map/ppermute | solution.py:39
  476.9 17.5 %collective-permute-start.95 = (bf16[1,2,128,512]{3,2,1,0:T(8,128)(2,1)S(1)}, bf16[1,2,128,512]{3,2,1,0:T(8,128)(2,1)S(1)}, u32[]{:S(2)}, u32[]{:S(2)}) collective-permute-start(bf16[1,2,128,512]{3,2,1,0:T(8,128)(2,1)S(1)} %bitcast.355), channel_id=1, source_target_pairs={{0,48},{16,0},{32,16},{48,32},{1,49},{17,1},{33,17},{49,33},{2,50}... | collective-permute-start | bytes 786440 | tf_op jit(solution)/shard_map/ppermute | solution.py:39
  479.3 15.1 %collective-permute-start.96 = (bf16[1,2,128,512]{3,2,1,0:T(8,128)(2,1)}, bf16[1,2,128,512]{3,2,1,0:T(8,128)(2,1)S(1)}, u32[]{:S(2)}, u32[]{:S(2)}) collective-permute-start(bf16[1,2,128,512]{3,2,1,0:T(8,128)(2,1)} %bitcast.354), channel_id=1, source_target_pairs={{0,32},{16,48},{32,0},{48,16},{1,33},{17,49},{33,1},{49,17},{2,34}... | collective-permute-start | bytes 786440 | tf_op jit(solution)/shard_map/ppermute | solution.py:39
  494.4 54.6 %collective-permute-start.76 = (f32[128,1024]{1,0:T(8,128)S(1)}, f32[128,1024]{1,0:T(8,128)S(1)}, u32[]{:S(2)}, u32[]{:S(2)}) collective-permute-start(f32[128,1024]{1,0:T(8,128)S(1)} %add_add_fusion.4), channel_id=1, source_target_pairs={{0,0},{4,8},{8,4},{12,12},{1,1},{5,9},{9,5},{13,13},{2,2},{6,10},{... | collective-permute-start | bytes 1572872 | tf_op jit(solution)/shard_map/ppermute | solution.py:47
  498.5 13.7 %collective-permute-start.99 = (bf16[1,128,512]{2,1,0:T(8,128)(2,1)S(1)}, bf16[1,128,512]{2,1,0:T(8,128)(2,1)S(1)}, u32[]{:S(2)}, u32[]{:S(2)}) collective-permute-start(bf16[1,128,512]{2,1,0:T(8,128)(2,1)S(1)} %get-tuple-element.165), channel_id=1, source_target_pairs={{0,64},{12,76},{64,0},{76,12},{1,65},{13,77},{65,1},{77,13},{2,66}... | collective-permute-start | bytes 393224 | tf_op jit(solution)/shard_map/ppermute | solution.py:128
  502.4 12.7 %collective-permute-start.90 = (bf16[1,128,512]{2,1,0:T(8,128)(2,1)S(1)}, bf16[1,128,512]{2,1,0:T(8,128)(2,1)S(1)}, u32[]{:S(2)}, u32[]{:S(2)}) collective-permute-start(bf16[1,128,512]{2,1,0:T(8,128)(2,1)S(1)} %get-tuple-element.160), channel_id=1, source_target_pairs={{8,12},{4,64},{72,76},{68,0},{9,13},{5,65},{73,77},{69,1},{10,14},... | collective-permute-start | bytes 393224 | tf_op jit(solution)/shard_map/ppermute | solution.py:118
  (182 other events, 1850.6 us)

commit v3 on v1

v3 whole, which is shorter than its diff:
```python
import jax
import jax.numpy as jnp
from jax import lax
from jax.experimental import pallas as pl
from jax.experimental.pallas import tpu as pltpu
from jax.sharding import Mesh
from jax.sharding import PartitionSpec as P

HEAD_DIM = 64
LAYERS = 2
EPS_NORM = 1e-05
NEG_FILL = -1000000000.0
BF = jnp.bfloat16
F32 = jnp.float32
RINGS = {"z": ("z",), "x": ("x",), "y": ("yh", "yl")}


def layer_norm(stream, norm_gain, norm_shift):
    center = stream - jnp.mean(stream, -1, keepdims=True)
    spread = jnp.mean(center * center, -1, keepdims=True)
    return center * lax.rsqrt(spread + EPS_NORM) * norm_gain + norm_shift


def gelu_tanh(values):
    return (
        0.5
        * values
        * (1.0 + jnp.tanh(0.7978845608028654 * (values + 0.044715 * values * values * values)))
    )


def tokens_inner(left, right):
    return lax.dot_general(left, right, (((0,), (0,)), ((), ())), preferred_element_type=F32)


def against_rows(left, right):
    return lax.dot_general(left, right, (((1,), (1,)), ((), ())), preferred_element_type=F32)


def ring(values, axis, step):
    return lax.ppermute(values, RINGS[axis], [(i, (i + step) % 4) for i in range(4)])


def swap_cores(values):
    return lax.ppermute(values, "c", [(0, 1), (1, 0)])


def swap_halves(values):
    return lax.ppermute(values, ("c", "yl"), [(0, 0), (1, 2), (2, 1), (3, 3)])


def y_pairs(rule):
    pairs = []
    for y in range(4):
        for core in range(2):
            target = rule(y, core)
            if target is not None:
                y2, core2 = target[0] % 4, target[1]
                pairs.append(
                    ((y // 2) * 4 + core * 2 + y % 2, (y2 // 2) * 4 + core2 * 2 + y2 % 2)
                )
    return pairs


def fetch_weights(values, step):
    return lax.ppermute(
        values,
        ("yh", "c", "yl"),
        y_pairs(lambda y, c: (y - step, y % 2) if c == y % 2 else (y, y % 2)),
    )


def after(token, *values):
    return lax.optimization_barrier((token,) + values)[1:]


def run_beside(token, chain, tasks):
    results = [task(*after(token, *operands)) for task, operands in tasks]
    return lax.optimization_barrier((chain, results))


def gather_ring(values, tasks=()):
    before = ring(values, "z", 1)
    behind = ring(values, "z", -1)
    across = ring(values, "z", 2)
    return run_beside(values, jnp.concatenate([values, before, behind, across]), tasks)


def gather_pair(mine):
    return jnp.concatenate([mine, swap_cores(mine)])


def gather_rows(values, tasks=()):
    mine, results = gather_ring(values, tasks)
    return gather_pair(mine), results


def scatter_pair(partial):
    half = partial.shape[0] // 2
    return partial[:half] + swap_cores(partial[half:].astype(BF)).astype(F32)


def scatter_rows(partial, tasks=()):
    both = scatter_pair(partial)
    low = both.astype(BF)
    rows = low.shape[0] // 4
    total = (
        both[:rows]
        + ring(low[rows : 2 * rows], "z", -1).astype(F32)
        + ring(low[2 * rows : 3 * rows], "z", 1).astype(F32)
        + ring(low[3 * rows :], "z", 2).astype(F32)
    )
    return run_beside(low, total, tasks)


def grad_blocks(pairs):
    place = lax.axis_index("x").astype(jnp.int32).reshape(1)
    tokens = pairs[0][0].shape[0]
    widths = [right.shape[1] for _, right in pairs]
    total = sum(widths)
    count = len(pairs)

    def kernel(place_ref, *refs):
        lefts, rights, outs = refs[: 2 * count], refs[2 * count : 3 * count], refs[3 * count :]
        step = pl.program_id(0)
        for d in range(4):

            @pl.when(step == d)
            def _():
                start = 0
                for i in range(count):
                    for high in range(2):
                        outs[d][high, :, start : start + widths[i]] = tokens_inner(
                            lefts[2 * i + high][...], rights[i][...]
                        ).astype(BF)
                    start += widths[i]

    def left_spec(high):
        return pl.BlockSpec((tokens, 128), lambda d, p: (0, high * 4 + lax.rem(p[0] + d, 4)))

    return pl.pallas_call(
        kernel,
        grid_spec=pltpu.PrefetchScalarGridSpec(
            num_scalar_prefetch=1,
            grid=(4,),
            in_specs=[left_spec(high) for _ in pairs for high in range(2)]
            + [pl.BlockSpec((tokens, width), lambda d, p: (0, 0)) for width in widths],
            out_specs=[pl.BlockSpec((2, 128, total), lambda d, p: (0, 0, 0))] * 4,
        ),
        out_shape=[jax.ShapeDtypeStruct((2, 128, total), BF)] * 4,
        compiler_params=pltpu.CompilerParams(vmem_limit_bytes=24 * 1024 * 1024),
        cost_estimate=pl.CostEstimate(
            flops=2 * tokens * 1024 * total, bytes_accessed=8 * 1024 * 1024, transcendentals=0
        ),
    )(place, *[left for left, _ in pairs for _ in range(2)], *[right for _, right in pairs])


def send_x(blocks):
    return blocks[0], ring(blocks[1], "x", 1), ring(blocks[3], "x", -1), ring(blocks[2], "x", 2)


def add_x(own, before, behind, across):
    summed = own.astype(F32) + before.astype(F32) + behind.astype(F32) + across.astype(F32)
    high, low_place = lax.axis_index("yh"), lax.axis_index("yl")
    y = high * 2 + low_place

    def pick(index):
        return jnp.where(index == 0, summed[0], summed[1])

    return (
        pick(high),
        pick(((y + 1) % 4) // 2).astype(BF),
        pick(((y + 3) % 4) // 2).astype(BF),
        pick(1 - high).astype(BF),
    )


def send_y(own, up, down, far):
    axes = ("yh", "c", "yl")
    return (
        own,
        lax.ppermute(up, axes, y_pairs(lambda y, c: (y + 1, c) if c != y % 2 else None)),
        lax.ppermute(down, axes, y_pairs(lambda y, c: (y + 3, c) if c != y % 2 else None)),
        lax.ppermute(far, axes, y_pairs(lambda y, c: (y + 2, c) if c == y % 2 else None)),
    )


def add_y(own, up, down, far):
    total = own + up.astype(F32) + down.astype(F32) + far.astype(F32)
    core = lax.axis_index("c")
    first, second = total[:64], total[64:]
    return jnp.where(core == 0, first, second), jnp.where(core == 0, second, first)


def send_core(keep, give):
    got = lax.ppermute(give, ("c", "yl"), [(0, 2), (3, 1)])
    return jnp.where(lax.axis_index("c") == lax.axis_index("yl"), keep, got)


def sum_everywhere(values):
    values = values + swap_cores(values)
    for axis in ("z", "x", "y"):
        values = (values + ring(values, axis, 2)) + (
            ring(values, axis, 1) + ring(values, axis, -1)
        )
    return values


def row_places():
    core, z = lax.axis_index("c"), lax.axis_index("z")
    blocks = jnp.stack([cc * 4 + (z + dz) % 4 for cc in (core, 1 - core) for dz in (0, 3, 1, 2)])
    return (blocks[:, None] * 128 + lax.iota(jnp.int32, 128)[None, :]).reshape(-1)


QUERY_ROWS = 256
VMEM_BYTES = 32 * 1024 * 1024


def attend_forward_kernel(query_place, key_place, q_ref, k_ref, v_ref, out_ref, log_ref):
    mask = query_place[...] >= key_place[...]
    for head in range(q_ref.shape[1] // HEAD_DIM):
        cut = slice(head * HEAD_DIM, (head + 1) * HEAD_DIM)
        scores = against_rows(k_ref[:, cut], q_ref[:, cut]) * HEAD_DIM ** (-0.5)
        scores = jnp.where(mask, scores, NEG_FILL)
        peak = jnp.max(scores, 0, keepdims=True)
        weights = jnp.exp(scores - peak)
        total = jnp.sum(weights, 0, keepdims=True)
        weights = (weights / total).astype(BF)
        out_ref[:, cut] = tokens_inner(v_ref[:, cut], weights).T.astype(BF)
        log_ref[head : head + 1, :] = peak + jnp.log(total)


def attend_forward(qkv, places):
    tokens, width = qkv.shape[0], qkv.shape[1] // 3
    heads = width // HEAD_DIM
    return pl.pallas_call(
        attend_forward_kernel,
        grid=(tokens // QUERY_ROWS,),
        in_specs=[
            pl.BlockSpec((1, QUERY_ROWS), lambda i: (0, i)),
            pl.BlockSpec((tokens, 1), lambda i: (0, 0)),
            pl.BlockSpec((QUERY_ROWS, width), lambda i: (i, 0)),
            pl.BlockSpec((tokens, width), lambda i: (0, 1)),
            pl.BlockSpec((tokens, width), lambda i: (0, 2)),
        ],
        out_specs=[
            pl.BlockSpec((QUERY_ROWS, width), lambda i: (i, 0)),
            pl.BlockSpec((heads, QUERY_ROWS), lambda i: (0, i)),
        ],
        out_shape=[
            jax.ShapeDtypeStruct((tokens, width), BF),
            jax.ShapeDtypeStruct((heads, tokens), F32),
        ],
        compiler_params=pltpu.CompilerParams(vmem_limit_bytes=VMEM_BYTES),
        cost_estimate=pl.CostEstimate(
            flops=8 * tokens * tokens * width, bytes_accessed=2 ** 21, transcendentals=tokens * tokens * heads
        ),
    )(places[None, :], places[:, None], qkv, qkv, qkv)


def attend_backward_kernel(
    query_place, key_place, log_ref, q_ref, k_ref, v_ref, do_ref, out_ref, dk_ref, dv_ref
):
    step = pl.program_id(0)
    width = q_ref.shape[1]
    rows = pl.ds(pl.multiple_of(step * QUERY_ROWS, QUERY_ROWS), QUERY_ROWS)
    mask = query_place[...] >= key_place[...]
    scale = HEAD_DIM ** (-0.5)

    @pl.when(step == 0)
    def _():
        dk_ref[...] = jnp.zeros_like(dk_ref)
        dv_ref[...] = jnp.zeros_like(dv_ref)

    for head in range(width // HEAD_DIM):
        cut = slice(head * HEAD_DIM, (head + 1) * HEAD_DIM)
        q, k, v, do = q_ref[:, cut], k_ref[:, cut], v_ref[:, cut], do_ref[:, cut]
        scores = jnp.where(mask, against_rows(k, q) * scale, NEG_FILL)
        weights = jnp.exp(scores - log_ref[head : head + 1, :])
        grad_weights = against_rows(v, do)
        mean = jnp.sum(weights * grad_weights, 0, keepdims=True)
        grad_scores = (weights * (grad_weights - mean)).astype(BF)
        out_ref[rows, cut] = (tokens_inner(k, grad_scores).T * scale).astype(BF)
        dk_ref[:, cut] += jnp.dot(grad_scores, q, preferred_element_type=F32)
        dv_ref[:, cut] += jnp.dot(weights.astype(BF), do, preferred_element_type=F32)

    @pl.when(step == pl.num_programs(0) - 1)
    def _():
        out_ref[:, width : 2 * width] = (dk_ref[...] * scale).astype(BF)
        out_ref[:, 2 * width :] = dv_ref[...].astype(BF)


def attend_backward(qkv, grad_out, log_totals, places):
    tokens, width = qkv.shape[0], qkv.shape[1] // 3
    heads = width // HEAD_DIM
    return pl.pallas_call(
        attend_backward_kernel,
        grid=(tokens // QUERY_ROWS,),
        in_specs=[
            pl.BlockSpec((1, QUERY_ROWS), lambda i: (0, i)),
            pl.BlockSpec((tokens, 1), lambda i: (0, 0)),
            pl.BlockSpec((heads, QUERY_ROWS), lambda i: (0, i)),
            pl.BlockSpec((QUERY_ROWS, width), lambda i: (i, 0)),
            pl.BlockSpec((tokens, width), lambda i: (0, 1)),
            pl.BlockSpec((tokens, width), lambda i: (0, 2)),
            pl.BlockSpec((QUERY_ROWS, width), lambda i: (i, 0)),
        ],
        out_specs=pl.BlockSpec((tokens, 3 * width), lambda i: (0, 0)),
        out_shape=jax.ShapeDtypeStruct((tokens, 3 * width), BF),
        scratch_shapes=[pltpu.VMEM((tokens, width), F32), pltpu.VMEM((tokens, width), F32)],
        compiler_params=pltpu.CompilerParams(vmem_limit_bytes=VMEM_BYTES),
        cost_estimate=pl.CostEstimate(
            flops=20 * tokens * tokens * width, bytes_accessed=2 ** 22, transcendentals=tokens * tokens * heads
        ),
    )(places[None, :], places[:, None], log_totals, qkv, qkv, qkv, grad_out)


def per_device(
    hidden_in,
    cotangent,
    norm_gain,
    norm_shift,
    inward,
    inward_bias,
    outward,
    outward_bias,
    expand,
    expand_bias,
    shrink,
    shrink_bias,
):
    stream = swap_halves(hidden_in).astype(F32)
    columns = inward.shape[3]
    w_in, w_out, w_up, w_down = [], [], [], []
    for layer in range(LAYERS):
        w_in.append(fetch_weights(inward[layer].reshape(-1, 3 * columns), 1))
        if layer == 0:
            biases = fetch_weights(
                jnp.concatenate([inward_bias.reshape(-1, 128), expand_bias.reshape(-1, 128)]), -1
            )
            bias_in = biases[:4].reshape(LAYERS, 2, columns)
            bias_up = biases[4:].reshape(LAYERS, -1)
        w_out.append(fetch_weights(outward[layer], -1))
        w_up.append(fetch_weights(expand[layer], -1))
        w_down.append(fetch_weights(shrink[layer], 1))
    cotangent = swap_halves(cotangent)

    places = row_places()
    saved = []
    pieces = {}

    def cotangent_task(step):
        def task(values):
            pieces[step] = ring(values, "z", step)
            return pieces[step]

        return [(task, (cotangent,))]

    for layer in range(LAYERS):
        normed = layer_norm(stream, norm_gain[layer, 0], norm_shift[layer, 0]).astype(BF)
        normed_all, _ = gather_rows(normed)
        qkv_bias = jnp.concatenate(
            [bias_in[layer, 0], jnp.zeros((columns,), F32), bias_in[layer, 1]]
        )
        qkv = (
            jnp.dot(normed_all, w_in[layer], preferred_element_type=F32) + qkv_bias
        ).astype(BF)
        attended, log_totals = attend_forward(qkv, places)
        attended, (piece,) = run_beside(
            normed_all, attended, cotangent_task(1 if layer == 0 else 2)
        )
        pieces[1 if layer == 0 else 2] = piece
        if layer == 1:
            attended, w_up[1], w_down[1] = lax.optimization_barrier(
                (attended, w_up[1], w_down[1])
            )
        middle = stream + (
            scatter_rows(jnp.dot(attended, w_out[layer], preferred_element_type=F32))[0]
            + outward_bias[layer]
        )
        normed_mid = layer_norm(middle, norm_gain[layer, 1], norm_shift[layer, 1]).astype(BF)
        if layer == 0:
            normed_mid, w_up[0], w_down[0] = lax.optimization_barrier(
                (normed_mid, w_up[0], w_down[0])
            )
        mid_mine, _ = gather_ring(normed_mid)
        mid_all = gather_pair(mid_mine)
        hidden_pre = (
            jnp.dot(mid_all, w_up[layer], preferred_element_type=F32) + bias_up[layer]
        )
        activated = gelu_tanh(hidden_pre).astype(BF)
        saved.append(
            (stream, normed_all, qkv, attended, log_totals, middle, mid_all, hidden_pre,
             activated)
        )
        if layer == 0:
            activated, (pieces[-1],) = run_beside(mid_mine, activated, cotangent_task(-1))
            activated, w_in[1], w_out[1] = lax.optimization_barrier(
                (activated, w_in[1], w_out[1])
            )
            stream = middle + (
                scatter_rows(jnp.dot(activated, w_down[layer], preferred_element_type=F32))[0]
                + shrink_bias[layer]
            )
    cotangent_ring = jnp.concatenate([cotangent, pieces[1], pieces[-1], pieces[2]])

    grad_stream = cotangent.astype(F32)
    gains, shifts, sums_out, sums_down, sums_in, sums_up = {}, {}, {}, {}, {}, {}
    grads_mlp, grads_attn = [None] * LAYERS, [None] * LAYERS

    _, normed_all, qkv, attended, log_totals, middle, mid_all, hidden_pre, activated = saved[1]
    sums_down[1] = jnp.sum(cotangent, 0, dtype=F32)
    dy_all = gather_pair(cotangent_ring)

    def mlp_back(layer, dy_all):
        hidden_pre = saved[layer][7]
        grad_act = against_rows(dy_all, w_down[layer])
        du = jax.vjp(gelu_tanh, hidden_pre)[1](grad_act)[0].astype(BF)
        return du

    def mlp_sum(layer, du, dy_all, tasks):
        _, _, _, _, _, middle, mid_all, hidden_pre, activated = saved[layer]
        sums_up[layer] = jnp.sum(du, 0, dtype=F32)

        def make(dy_all, activated, mid_all, du):
            return grad_blocks([(dy_all, activated), (mid_all, du)])

        dh, results = scatter_rows(
            against_rows(du, w_up[layer]), [(make, (dy_all, activated, mid_all, du))] + tasks
        )
        back_mid = jax.vjp(layer_norm, middle, norm_gain[layer, 1], norm_shift[layer, 1])[1]
        grad_part, gains[layer, 1], shifts[layer, 1] = back_mid(dh)
        return grad_part, results

    def attn_sum(layer, dqkv, dz_all, tasks):
        stream, normed_all, _, attended, _, _, _, _, _ = saved[layer]
        sums = jnp.sum(dqkv, 0, dtype=F32)
        sums_in[layer] = jnp.stack([sums[:columns], sums[2 * columns :]])

        def make(dz_all, attended, normed_all, dqkv):
            return grad_blocks([(dz_all, attended), (normed_all, dqkv)])

        da, results = scatter_rows(
            against_rows(dqkv, w_in[layer]), [(make, (dz_all, attended, normed_all, dqkv))] + tasks
        )
        back_in = jax.vjp(layer_norm, stream, norm_gain[layer, 0], norm_shift[layer, 0])[1]
        grad_first, gains[layer, 0], shifts[layer, 0] = back_in(da)
        return grad_first, results

    du = mlp_back(1, dy_all)
    grad_part, (mlp1,) = mlp_sum(1, du, dy_all, [])
    grad_middle = grad_stream + grad_part
    mlp1 = send_x(mlp1)
    dz = grad_middle.astype(BF)
    sums_out[1] = jnp.sum(dz, 0, dtype=F32)
    dz_all, _ = gather_rows(dz)
    do = against_rows(dz_all, w_out[1]).astype(BF)
    dqkv = attend_backward(qkv, do, log_totals, places)

    def last_pairs(activated):
        both = scatter_pair(jnp.dot(activated, w_down[1], preferred_element_type=F32))
        low = both.astype(BF)
        rows = low.shape[0] // 4
        near = (
            both[:rows]
            + ring(low[rows : 2 * rows], "z", -1).astype(F32)
            + ring(low[2 * rows : 3 * rows], "z", 1).astype(F32)
        )
        return near, low[3 * rows :]

    dqkv, ((last_near, last_far),) = run_beside(dz_all, dqkv, [(last_pairs, (activated,))])
    grad_first, (attn1, mlp1) = attn_sum(1, dqkv, dz_all, [(add_x, mlp1)])
    grad_stream = grad_middle + grad_first
    attn1, mlp1 = send_x(attn1), send_y(*mlp1)

    _, normed_all, qkv, attended, log_totals, middle, mid_all, hidden_pre, activated = saved[0]
    dy = grad_stream.astype(BF)
    sums_down[0] = jnp.sum(dy, 0, dtype=F32)
    dy_mine, (mlp1,) = gather_ring(dy, [(add_y, mlp1)])
    grads_mlp[1] = send_core(*mlp1)
    dy_all = gather_pair(dy_mine)
    du = mlp_back(0, dy_all)
    du, (last_across,) = run_beside(
        dy_mine, du, [(lambda values: ring(values, "z", 2), (last_far,))]
    )
    hidden_out = swap_halves(
        saved[1][5] + (last_near + last_across.astype(F32) + shrink_bias[1])
    )
    grad_part, (mlp0, attn1) = mlp_sum(0, du, dy_all, [(add_x, attn1)])
    grad_middle = grad_stream + grad_part
    mlp0, attn1 = send_x(mlp0), send_y(*attn1)
    dz = grad_middle.astype(BF)
    sums_out[0] = jnp.sum(dz, 0, dtype=F32)
    dz_all, (attn1,) = gather_rows(dz, [(add_y, attn1)])
    grads_attn[1] = send_core(*attn1)
    do = against_rows(dz_all, w_out[0]).astype(BF)
    dqkv = attend_backward(qkv, do, log_totals, places)
    grad_first, (attn0, mlp0) = attn_sum(0, dqkv, dz_all, [(add_x, mlp0)])
    grad_stream = grad_middle + grad_first
    grad_hidden = swap_halves(grad_stream)
    attn0 = add_x(*send_x(attn0))
    grads_mlp[0] = send_core(*add_y(*send_y(*mlp0)))
    grads_attn[0] = send_core(*add_y(*send_y(*attn0)))

    shard = lax.axis_index("c") * 4 + lax.axis_index("z")
    own = lax.axis_index("yl") * 4 + lax.axis_index("z")
    both = range(LAYERS)
    up = jnp.stack([sums_up[n] for n in both])[:, None]
    qv = jnp.stack([sums_in[n] for n in both])[:, :, None]
    up = lax.dynamic_update_slice_in_dim(jnp.zeros((LAYERS, 8, up.shape[2]), F32), up, shard, 1)
    qv = lax.dynamic_update_slice_in_dim(jnp.zeros((LAYERS, 2, 8, columns), F32), qv, shard, 2)
    vectors = jnp.concatenate(
        [
            m.reshape(-1, 128)
            for m in (
                [gains[n, i] for n in both for i in (0, 1)]
                + [shifts[n, i] for n in both for i in (0, 1)]
                + [sums_out[n] for n in both]
                + [sums_down[n] for n in both]
                + [up, qv]
            )
        ]
    )
    vectors = sum_everywhere(vectors)
    grad_gain = vectors[:32].reshape(LAYERS, 2, 1024)
    grad_shift = vectors[32:64].reshape(LAYERS, 2, 1024)
    grad_out_bias = vectors[64:80].reshape(LAYERS, 1024)
    grad_down_bias = vectors[80:96].reshape(LAYERS, 1024)
    up = vectors[96:160].reshape(LAYERS, 8, -1)
    qv = vectors[160:].reshape(LAYERS, 2, 8, columns)
    grad_up_bias = lax.dynamic_index_in_dim(up, own, 1, keepdims=False)
    grad_in_bias = lax.dynamic_index_in_dim(qv, own, 2, keepdims=False)

    width = shrink.shape[1]
    return (
        hidden_out,
        grad_hidden,
        grad_gain,
        grad_shift,
        jnp.stack([g[:, columns:].reshape(-1, 3, columns) for g in grads_attn]),
        grad_in_bias,
        jnp.stack([g[:, :columns].T for g in grads_attn]),
        grad_out_bias,
        jnp.stack([g[:, width:] for g in grads_mlp]),
        grad_up_bias,
        jnp.stack([g[:, :width].T for g in grads_mlp]),
        grad_down_bias,
    )


def solution(mesh):
    fine = Mesh(mesh.devices.reshape(2, 4, 2, 2, 4), ("yh", "x", "c", "yl", "z"))
    dp, tensor = ("yh", "x", "c"), ("yl", "z")
    rows = P(dp + tensor, None)
    return jax.shard_map(
        per_device,
        mesh=fine,
        in_specs=(
            rows,
            rows,
            P(),
            P(),
            P(None, None, None, tensor),
            P(None, None, tensor),
            P(None, tensor, None),
            P(),
            P(None, None, tensor),
            P(None, tensor),
            P(None, tensor, None),
            P(),
        ),
        out_specs=(
            rows,
            rows,
            P(),
            P(),
            P(None, dp, None, tensor),
            P(None, None, tensor),
            P(None, tensor, dp),
            P(),
            P(None, dp, tensor),
            P(None, tensor),
            P(None, tensor, dp),
            P(),
        ),
        check_vma=False,
    )
```

time: 641 us -> 520 us (0.81)
  the two profiles are of different devices: /device:TPU:1 before, /device:TPU:2 now
where the time goes in v3:
time: 520 us; the launch traced here: 511 us
  waiting for transfers between devices  202 us (39%)
  starting transfers between devices  144 us (28%)
  Pallas kernels  53.5 us (10%)
  other arithmetic  43.5 us (8%)
  local copies, waits for them, and re-layouts  36.8 us (7%)
  matrix products  28.1 us (5%)
    ppermute x69, waiting for transfers between devices, ring(): lax.ppermute(values, RINGS[axis], [(i, (i + step) % 4) for i in range(4)])  164 us
    ppermute x69, starting transfers between devices, ring(): lax.ppermute(values, RINGS[axis], [(i, (i + step) % 4) for i in range(4)])  83.1 us
    pallas_call x2, Pallas kernels, attend_backward(): pl.pallas_call(attend_backward_kernel, grid=(tokens // QUERY_ROWS,), in_s...  20.2 us
    ppermute x17, waiting for transfers between devices, swap_cores(): return lax.ppermute(values, 'c', [(0, 1), (1, 0)])  19.2 us
    unnamed x255, local copies, waits for them, and re-layouts  18.1 us
    pallas_call x4, Pallas kernels, grad_blocks(): pl.pallas_call(kernel, grid_spec=pltpu.PrefetchScalarGridSpec(num_scalar_...  16.8 us
    pallas_call x2, Pallas kernels, attend_forward(): pl.pallas_call(attend_forward_kernel, grid=(tokens // QUERY_ROWS,), in_sp...  16.5 us
    ppermute x4, starting transfers between devices, send_y(): lax.ppermute(far, axes, y_pairs(lambda y, c: (y + 2, c) if c == y % 2 els...  15 us
  transfers between devices with their start and end apart: 115, of which 59 were waited for; matrix products, arithmetic and copies ran while one was open for 13% of the time, Pallas kernels for 10%

profile of v3, /device:TPU:2, one launch (start us, length us, event | category | flops | bytes accessed | tf_op | source)
XLA Modules:
  0.0 510.6 jit_solution(1125474127895177228)
XLA Ops:
  5.0 4.0 collective-permute-start.3
  13.7 7.7 %collective-permute-start.5 = (bf16[1024,384]{0,1:T(8,128)(2,1)}, bf16[1024,384]{0,1:T(8,128)(2,1)}, u32[]{:S(2)}, u32[]{:S(2)}) collective-permute-start(bf16[1024,384]{0,1:T(8,128)(2,1)} %bitcast.12), channel_id=1, source_target_pairs={{0,68},{8,0},{4,12},{12,8},{64,4},{72,64},{68,76},{76,72},{1,69},{... | collective-permute-start | bytes 2359304 | tf_op jit(solution)/shard_map/ppermute | solution.py:66
  21.5 3.6 collective-permute-start.7
  29.1 2.9 pad_maximum_fusion.refs_2_.refs_3_
  33.0 2.7 add_convert_fusion.1.q_ref.k_ref.v_ref
  35.7 8.2 %shard_map.211 = (bf16[1024,128]{1,0:T(8,128)(2,1)S(1)}, f32[2,1024]{1,0:T(2,128)S(1)}) custom-call(s32[1,1024]{1,0:T(1,128)S(1)} %bitcast.184, s32[1024,1]{1,0:T(8,128)S(1)} %copy.29.key_place, bf16[1024,384]{1,0:T(8,128)(2,1)S(1)} %add_convert_fusion.1.q_ref.k_ref.v_ref, bf16[1024,384]{1,0:T(8,128)(2,1)S(1)} %add_convert_fusion.1.q_ref.k_ref.v_ref, ...), custom_call_target="tpu_custom_call" | custom-call | flops 1073741824 | bytes 2097152 | tf_op jit(solution)/shard_map/pallas_call | solution.py:236
  59.3 4.7 collective-permute-done.12
  64.8 4.8 collective-permute-done.15
  71.9 8.5 %collective-permute-done.18 = bf16[128,1024]{1,0:T(8,128)(2,1)S(1)} collective-permute-done((bf16[128,1024]{1,0:T(8,128)(2,1)S(1)}, bf16[128,1024]{1,0:T(8,128)(2,1)S(1)}, u32[]{:S(2)}, u32[]{:S(2)}) %collective-permute-start.18) | collective-permute-done | bytes 262176 | tf_op jit(solution)/shard_map/ppermute | solution.py:41
  87.1 4.6 multiply_convert_fusion.1
  91.6 3.2 collective-permute-done.20
  105.1 7.1 %collective-permute-done.26 = bf16[128,1024]{1,0:T(8,128)(2,1)S(1)} collective-permute-done((bf16[128,1024]{1,0:T(8,128)(2,1)S(1)}, bf16[128,1024]{1,0:T(8,128)(2,1)S(1)}, u32[]{:S(2)}, u32[]{:S(2)}) %collective-permute-start.26) | collective-permute-done | bytes 262176 | tf_op jit(solution)/shard_map/ppermute | solution.py:41
  112.2 4.8 collective-permute-done.25
  120.3 8.2 %collective-permute-done.29 = bf16[128,1024]{1,0:T(8,128)(2,1)S(1)} collective-permute-done((bf16[128,1024]{1,0:T(8,128)(2,1)S(1)}, bf16[128,1024]{1,0:T(8,128)(2,1)S(1)}, u32[]{:S(2)}, u32[]{:S(2)}) %collective-permute-start.29) | collective-permute-done | bytes 262176 | tf_op jit(solution)/shard_map/ppermute | solution.py:41
  128.6 2.8 collective-permute-done.28
  138.5 8.2 %shard_map.212 = (bf16[1024,128]{1,0:T(8,128)(2,1)S(1)}, f32[2,1024]{1,0:T(2,128)S(1)}) custom-call(s32[1,1024]{1,0:T(1,128)S(1)} %bitcast.185, s32[1024,1]{1,0:T(8,128)S(1)} %copy.29.key_place, bf16[1024,384]{1,0:T(8,128)(2,1)S(1)} %add_convert_fusion.q_ref.k_ref.v_ref, bf16[1024,384]{1,0:T(8,128)(2,1)S(1)} %add_convert_fusion.q_ref.k_ref.v_ref, ...), custom_call_target="tpu_custom_call" | custom-call | flops 1073741824 | bytes 2097152 | tf_op jit(solution)/shard_map/pallas_call | solution.py:236
  157.2 6.2 %collective-permute-done.37 = bf16[128,1024]{1,0:T(8,128)(2,1)S(1)} collective-permute-done((bf16[128,1024]{1,0:T(8,128)(2,1)S(1)}, bf16[128,1024]{1,0:T(8,128)(2,1)S(1)}, u32[]{:S(2)}, u32[]{:S(2)}) %collective-permute-start.37) | collective-permute-done | bytes 262176 | tf_op jit(solution)/shard_map/ppermute | solution.py:41
  163.4 4.8 collective-permute-done.36
  173.4 6.3 %collective-permute-done.40 = bf16[128,1024]{1,0:T(8,128)(2,1)S(1)} collective-permute-done((bf16[128,1024]{1,0:T(8,128)(2,1)S(1)}, bf16[128,1024]{1,0:T(8,128)(2,1)S(1)}, u32[]{:S(2)}, u32[]{:S(2)}) %collective-permute-start.40) | collective-permute-done | bytes 262176 | tf_op jit(solution)/shard_map/ppermute | solution.py:41
  179.7 3.0 collective-permute-done.39
  188.4 4.0 convert_reduce_fusion
  196.2 2.9 collective-permute-done.43
  206.6 4.4 shard_map.213
  212.6 4.8 collective-permute-done.45
  223.9 7.4 %collective-permute-done.49 = bf16[128,1024]{1,0:T(8,128)(2,1)S(1)} collective-permute-done((bf16[128,1024]{1,0:T(8,128)(2,1)S(1)}, bf16[128,1024]{1,0:T(8,128)(2,1)S(1)}, u32[]{:S(2)}, u32[]{:S(2)}) %collective-permute-start.49) | collective-permute-done | bytes 262176 | tf_op jit(solution)/shard_map/ppermute | solution.py:41
  231.3 3.0 collective-permute-done.48
  245.8 3.6 collective-permute-start.52
  250.1 10.1 %shard_map.214.refs_5_ = bf16[1024,384]{1,0:T(8,128)(2,1)S(1)} custom-call(s32[1,1024]{1,0:T(1,128)S(1)} %bitcast.186, s32[1024,1]{1,0:T(8,128)S(1)} %copy-done.12, f32[2,1024]{1,0:T(2,128)S(1)} %get-tuple-element.146.log_ref, bf16[1024,384]{1,0:T(8,128)(2,1)S(1)} %copy-done.38, bf16[1024,384]{1,0:T(8,128)(2,1)S(1)} %copy-done.38, ...), custom_call_target="tpu_custom_call" | custom-call | flops 2684354560 | bytes 4194304 | tf_op jit(solution)/shard_map/pallas_call | solution.py:296
  273.6 7.3 %collective-permute-done.58 = bf16[2,128,1024]{2,1,0:T(8,128)(2,1)S(1)} collective-permute-done((bf16[2,128,1024]{2,1,0:T(8,128)(2,1)}, bf16[2,128,1024]{2,1,0:T(8,128)(2,1)S(1)}, u32[]{:S(2)}, u32[]{:S(2)}) %collective-permute-start.58) | collective-permute-done | bytes 524320 | tf_op jit(solution)/shard_map/ppermute | solution.py:41
  281.8 11.8 %collective-permute-done.60 = bf16[2,128,1024]{2,1,0:T(8,128)(2,1)S(1)} collective-permute-done((bf16[2,128,1024]{2,1,0:T(8,128)(2,1)}, bf16[2,128,1024]{2,1,0:T(8,128)(2,1)S(1)}, u32[]{:S(2)}, u32[]{:S(2)}) %collective-permute-start.60) | collective-permute-done | bytes 524320 | tf_op jit(solution)/shard_map/ppermute | solution.py:41
  294.0 3.9 shard_map.215
  303.1 3.4 collective-permute-start.66
  314.2 5.6 %collective-permute-done.63 = bf16[128,1024]{1,0:T(8,128)(2,1)S(1)} collective-permute-done((bf16[128,1024]{1,0:T(8,128)(2,1)S(1)}, bf16[128,1024]{1,0:T(8,128)(2,1)S(1)}, u32[]{:S(2)}, u32[]{:S(2)}) %collective-permute-start.63) | collective-permute-done | bytes 262176 | tf_op jit(solution)/shard_map/ppermute | solution.py:41
  319.8 2.9 collective-permute-done.62
  328.1 2.8 fusion.3.refs_5_
  330.9 4.7 collective-permute-done.68
  350.5 3.2 collective-permute-start.71
  353.7 3.2 collective-permute-done.76
  357.1 4.5 shard_map.216
  366.9 3.7 collective-permute-start.82
  375.4 6.7 %collective-permute-done.79 = bf16[128,1024]{1,0:T(8,128)(2,1)S(1)} collective-permute-done((bf16[128,1024]{1,0:T(8,128)(2,1)S(1)}, bf16[128,1024]{1,0:T(8,128)(2,1)S(1)}, u32[]{:S(2)}, u32[]{:S(2)}) %collective-permute-start.79) | collective-permute-done | bytes 262176 | tf_op jit(solution)/shard_map/ppermute | solution.py:41
  389.0 5.5 %collective-permute-start.69 = (f32[128,1024]{1,0:T(8,128)}, f32[128,1024]{1,0:T(8,128)}, u32[]{:S(2)}, u32[]{:S(2)}) collective-permute-start(f32[128,1024]{1,0:T(8,128)} %add_add_fusion.6), channel_id=1, source_target_pairs={{0,0},{4,8},{8,4},{12,12},{1,1},{5,9},{9,5},{13,13},{2,2},{6,10},{... | collective-permute-start | bytes 1572872 | tf_op jit(solution)/shard_map/ppermute | solution.py:49
  397.8 10.1 %shard_map.217.refs_5_ = bf16[1024,384]{1,0:T(8,128)(2,1)S(1)} custom-call(s32[1,1024]{1,0:T(1,128)S(1)} %bitcast.187, s32[1024,1]{1,0:T(8,128)S(1)} %copy-done.13, f32[2,1024]{1,0:T(2,128)S(1)} %get-tuple-element.211.log_ref, bf16[1024,384]{1,0:T(8,128)(2,1)S(1)} %copy-done.36, bf16[1024,384]{1,0:T(8,128)(2,1)S(1)} %copy-done.36, ...), custom_call_target="tpu_custom_call" | custom-call | flops 2684354560 | bytes 4194304 | tf_op jit(solution)/shard_map/pallas_call | solution.py:296
  423.4 15.0 %collective-permute-done.88 = bf16[2,128,1024]{2,1,0:T(8,128)(2,1)} collective-permute-done((bf16[2,128,1024]{2,1,0:T(8,128)(2,1)}, bf16[2,128,1024]{2,1,0:T(8,128)(2,1)}, u32[]{:S(2)}, u32[]{:S(2)}) %collective-permute-start.88) | collective-permute-done | bytes 524320 | tf_op jit(solution)/shard_map/ppermute | solution.py:41
  443.1 3.9 shard_map.218
  463.9 3.3 collective-permute-start.112
  470.4 6.3 %collective-permute-done.112 = bf16[128,1024]{1,0:T(8,128)(2,1)S(1)} collective-permute-done((bf16[128,1024]{1,0:T(8,128)(2,1)}, bf16[128,1024]{1,0:T(8,128)(2,1)S(1)}, u32[]{:S(2)}, u32[]{:S(2)}) %collective-permute-start.112) | collective-permute-done | bytes 262176 | tf_op jit(solution)/shard_map/ppermute | solution.py:184
  480.4 4.6 collective-permute-start.107
  (632 shorter events, 247.8 us)
Async XLA Ops:
  5.0 16.5 %collective-permute-start.3 = (bf16[128,1024]{1,0:T(8,128)(2,1)S(1)}, bf16[128,1024]{1,0:T(8,128)(2,1)S(1)}, u32[]{:S(2)}, u32[]{:S(2)}) collective-permute-start(bf16[128,1024]{1,0:T(8,128)(2,1)S(1)} %fusion.19), channel_id=1, source_target_pairs={{0,2},{1,3},{2,0},{3,1},{4,6},{5,7},{6,4},{7,5},{8,10},{9,11},{10,... | collective-permute-start | bytes 786440 | tf_op jit(solution)/shard_map/ppermute | solution.py:41
  9.0 16.1 %collective-permute-start.2 = (bf16[128,1024]{1,0:T(8,128)(2,1)S(1)}, bf16[128,1024]{1,0:T(8,128)(2,1)S(1)}, u32[]{:S(2)}, u32[]{:S(2)}) collective-permute-start(bf16[128,1024]{1,0:T(8,128)(2,1)S(1)} %fusion.19), channel_id=1, source_target_pairs={{0,3},{1,0},{2,1},{3,2},{4,7},{5,4},{6,5},{7,6},{8,11},{9,8},{10,9... | collective-permute-start | bytes 786440 | tf_op jit(solution)/shard_map/ppermute | solution.py:41
  9.7 15.4 %collective-permute-start.1 = (bf16[128,1024]{1,0:T(8,128)(2,1)S(1)}, bf16[128,1024]{1,0:T(8,128)(2,1)}, u32[]{:S(2)}, u32[]{:S(2)}) collective-permute-start(bf16[128,1024]{1,0:T(8,128)(2,1)S(1)} %fusion.19), channel_id=1, source_target_pairs={{0,1},{1,2},{2,3},{3,0},{4,5},{5,6},{6,7},{7,4},{8,9},{9,10},{10,1... | collective-permute-start | bytes 786440 | tf_op jit(solution)/shard_map/ppermute | solution.py:41
  13.7 19.3 %collective-permute-start.5 = (bf16[1024,384]{0,1:T(8,128)(2,1)}, bf16[1024,384]{0,1:T(8,128)(2,1)}, u32[]{:S(2)}, u32[]{:S(2)}) collective-permute-start(bf16[1024,384]{0,1:T(8,128)(2,1)} %bitcast.12), channel_id=1, source_target_pairs={{0,68},{8,0},{4,12},{12,8},{64,4},{72,64},{68,76},{76,72},{1,69},{... | collective-permute-start | bytes 2359304 | tf_op jit(solution)/shard_map/ppermute | solution.py:66
  27.1 16.9 %collective-permute-start.9 = (bf16[128,1024]{1,0:T(8,128)(2,1)}, bf16[128,1024]{1,0:T(8,128)(2,1)S(1)}, u32[]{:S(2)}, u32[]{:S(2)}) collective-permute-start(bf16[128,1024]{1,0:T(8,128)(2,1)} %get-tuple-element.358), channel_id=1, source_target_pairs={{0,4},{8,0},{4,12},{12,72},{64,68},{72,64},{68,76},{76,8},{1,5},{9... | collective-permute-start | bytes 786440 | tf_op jit(solution)/shard_map/ppermute | solution.py:66
  47.5 17.3 %collective-permute-start.14 = (bf16[1024,512]{1,0:T(8,128)(2,1)S(1)}, bf16[1024,512]{1,0:T(8,128)(2,1)S(1)}, u32[]{:S(2)}, u32[]{:S(2)}) collective-permute-start(bf16[1024,512]{1,0:T(8,128)(2,1)S(1)} %get-tuple-element.316), channel_id=1, source_target_pairs={{0,4},{8,0},{4,12},{12,72},{64,68},{72,64},{68,76},{76,8},{1,5},{9... | collective-permute-start | bytes 3145736 | tf_op jit(solution)/shard_map/ppermute | solution.py:66
  51.0 13.0 %collective-permute-start.12 = (bf16[128,1024]{1,0:T(8,128)(2,1)S(1)}, bf16[128,1024]{1,0:T(8,128)(2,1)S(1)}, u32[]{:S(2)}, u32[]{:S(2)}) collective-permute-start(bf16[128,1024]{1,0:T(8,128)(2,1)S(1)} %get-tuple-element.348), channel_id=1, source_target_pairs={{0,1},{1,2},{2,3},{3,0},{4,5},{5,6},{6,7},{7,4},{8,9},{9,10},{10,1... | collective-permute-start | bytes 786440 | tf_op jit(solution)/shard_map/ppermute | solution.py:41
  55.4 14.2 %collective-permute-start.15 = (bf16[512,1024]{1,0:T(8,128)(2,1)S(1)}, bf16[512,1024]{1,0:T(8,128)(2,1)S(1)}, u32[]{:S(2)}, u32[]{:S(2)}) collective-permute-start(bf16[512,1024]{1,0:T(8,128)(2,1)S(1)} %get-tuple-element.314), channel_id=1, source_target_pairs={{0,68},{8,0},{4,12},{12,8},{64,4},{72,64},{68,76},{76,72},{1,69},{... | collective-permute-start | bytes 3145736 | tf_op jit(solution)/shard_map/ppermute | solution.py:66
  101.8 15.2 %collective-permute-start.25 = (bf16[128,1024]{1,0:T(8,128)(2,1)S(1)}, bf16[128,1024]{1,0:T(8,128)(2,1)S(1)}, u32[]{:S(2)}, u32[]{:S(2)}) collective-permute-start(bf16[128,1024]{1,0:T(8,128)(2,1)S(1)} %get-tuple-element.345), channel_id=1, source_target_pairs={{0,1},{1,2},{2,3},{3,0},{4,5},{5,6},{6,7},{7,4},{8,9},{9,10},{10,1... | collective-permute-start | bytes 786440 | tf_op jit(solution)/shard_map/ppermute | solution.py:41
  103.0 14.0 %collective-permute-start.24 = (bf16[128,1024]{1,0:T(8,128)(2,1)S(1)}, bf16[128,1024]{1,0:T(8,128)(2,1)S(1)}, u32[]{:S(2)}, u32[]{:S(2)}) collective-permute-start(bf16[128,1024]{1,0:T(8,128)(2,1)S(1)} %get-tuple-element.343), channel_id=1, source_target_pairs={{0,3},{1,0},{2,1},{3,2},{4,7},{5,4},{6,5},{7,6},{8,11},{9,8},{10,9... | collective-permute-start | bytes 786440 | tf_op jit(solution)/shard_map/ppermute | solution.py:41
  118.3 13.0 %collective-permute-start.28 = (bf16[128,1024]{1,0:T(8,128)(2,1)S(1)}, bf16[128,1024]{1,0:T(8,128)(2,1)S(1)}, u32[]{:S(2)}, u32[]{:S(2)}) collective-permute-start(bf16[128,1024]{1,0:T(8,128)(2,1)S(1)} %add_convert_fusion.3), channel_id=1, source_target_pairs={{0,3},{1,0},{2,1},{3,2},{4,7},{5,4},{6,5},{7,6},{8,11},{9,8},{10,9... | collective-permute-start | bytes 786440 | tf_op jit(solution)/shard_map/ppermute | solution.py:41
  120.2 12.8 %collective-permute-start.27 = (bf16[128,1024]{1,0:T(8,128)(2,1)S(1)}, bf16[128,1024]{1,0:T(8,128)(2,1)S(1)}, u32[]{:S(2)}, u32[]{:S(2)}) collective-permute-start(bf16[128,1024]{1,0:T(8,128)(2,1)S(1)} %add_convert_fusion.3), channel_id=1, source_target_pairs={{0,1},{1,2},{2,3},{3,0},{4,5},{5,6},{6,7},{7,4},{8,9},{9,10},{10,1... | collective-permute-start | bytes 786440 | tf_op jit(solution)/shard_map/ppermute | solution.py:41
  133.1 13.6 %collective-permute-start.32 = (bf16[1024,512]{1,0:T(8,128)(2,1)S(1)}, bf16[1024,512]{1,0:T(8,128)(2,1)S(1)}, u32[]{:S(2)}, u32[]{:S(2)}) collective-permute-start(bf16[1024,512]{1,0:T(8,128)(2,1)S(1)} %copy-done.67), channel_id=1, source_target_pairs={{0,4},{8,0},{4,12},{12,72},{64,68},{72,64},{68,76},{76,8},{1,5},{9... | collective-permute-start | bytes 3145736 | tf_op jit(solution)/shard_map/ppermute | solution.py:66
  134.0 14.4 %collective-permute-start.33 = (bf16[512,1024]{1,0:T(8,128)(2,1)S(1)}, bf16[512,1024]{1,0:T(8,128)(2,1)S(1)}, u32[]{:S(2)}, u32[]{:S(2)}) collective-permute-start(bf16[512,1024]{1,0:T(8,128)(2,1)S(1)} %copy-done.68), channel_id=1, source_target_pairs={{0,68},{8,0},{4,12},{12,8},{64,4},{72,64},{68,76},{76,72},{1,69},{... | collective-permute-start | bytes 3145736 | tf_op jit(solution)/shard_map/ppermute | solution.py:66
  153.9 14.2 %collective-permute-start.36 = (bf16[128,1024]{1,0:T(8,128)(2,1)S(1)}, bf16[128,1024]{1,0:T(8,128)(2,1)S(1)}, u32[]{:S(2)}, u32[]{:S(2)}) collective-permute-start(bf16[128,1024]{1,0:T(8,128)(2,1)S(1)} %get-tuple-element.342), channel_id=1, source_target_pairs={{0,1},{1,2},{2,3},{3,0},{4,5},{5,6},{6,7},{7,4},{8,9},{9,10},{10,1... | collective-permute-start | bytes 786440 | tf_op jit(solution)/shard_map/ppermute | solution.py:41
  154.5 13.6 %collective-permute-start.35 = (bf16[128,1024]{1,0:T(8,128)(2,1)S(1)}, bf16[128,1024]{1,0:T(8,128)(2,1)S(1)}, u32[]{:S(2)}, u32[]{:S(2)}) collective-permute-start(bf16[128,1024]{1,0:T(8,128)(2,1)S(1)} %get-tuple-element.340), channel_id=1, source_target_pairs={{0,3},{1,0},{2,1},{3,2},{4,7},{5,4},{6,5},{7,6},{8,11},{9,8},{10,9... | collective-permute-start | bytes 786440 | tf_op jit(solution)/shard_map/ppermute | solution.py:41
  171.6 12.7 %collective-permute-start.38 = (bf16[128,1024]{1,0:T(8,128)(2,1)S(1)}, bf16[128,1024]{1,0:T(8,128)(2,1)S(1)}, u32[]{:S(2)}, u32[]{:S(2)}) collective-permute-start(bf16[128,1024]{1,0:T(8,128)(2,1)S(1)} %add_convert_fusion.2), channel_id=1, source_target_pairs={{0,1},{1,2},{2,3},{3,0},{4,5},{5,6},{6,7},{7,4},{8,9},{9,10},{10,1... | collective-permute-start | bytes 786440 | tf_op jit(solution)/shard_map/ppermute | solution.py:41
  203.1 14.2 %collective-permute-start.45 = (bf16[128,1024]{1,0:T(8,128)(2,1)S(1)}, bf16[128,1024]{1,0:T(8,128)(2,1)S(1)}, u32[]{:S(2)}, u32[]{:S(2)}) collective-permute-start(bf16[128,1024]{1,0:T(8,128)(2,1)S(1)} %get-tuple-element.339), channel_id=1, source_target_pairs={{0,1},{1,2},{2,3},{3,0},{4,5},{5,6},{6,7},{7,4},{8,9},{9,10},{10,1... | collective-permute-start | bytes 786440 | tf_op jit(solution)/shard_map/ppermute | solution.py:41
  203.7 13.6 %collective-permute-start.44 = (bf16[128,1024]{1,0:T(8,128)(2,1)S(1)}, bf16[128,1024]{1,0:T(8,128)(2,1)S(1)}, u32[]{:S(2)}, u32[]{:S(2)}) collective-permute-start(bf16[128,1024]{1,0:T(8,128)(2,1)S(1)} %get-tuple-element.337), channel_id=1, source_target_pairs={{0,3},{1,0},{2,1},{3,2},{4,7},{5,4},{6,5},{7,6},{8,11},{9,8},{10,9... | collective-permute-start | bytes 786440 | tf_op jit(solution)/shard_map/ppermute | solution.py:41
  223.2 12.7 %collective-permute-start.47 = (bf16[128,1024]{1,0:T(8,128)(2,1)S(1)}, bf16[128,1024]{1,0:T(8,128)(2,1)S(1)}, u32[]{:S(2)}, u32[]{:S(2)}) collective-permute-start(bf16[128,1024]{1,0:T(8,128)(2,1)S(1)} %get-tuple-element.281), channel_id=1, source_target_pairs={{0,1},{1,2},{2,3},{3,0},{4,5},{5,6},{6,7},{7,4},{8,9},{9,10},{10,1... | collective-permute-start | bytes 786440 | tf_op jit(solution)/shard_map/ppermute | solution.py:41
  245.8 14.5 %collective-permute-start.53 = (bf16[128,1024]{1,0:T(8,128)(2,1)S(1)}, bf16[128,1024]{1,0:T(8,128)(2,1)S(1)}, u32[]{:S(2)}, u32[]{:S(2)}) collective-permute-start(bf16[128,1024]{1,0:T(8,128)(2,1)S(1)} %get-tuple-element.335), channel_id=1, source_target_pairs={{0,1},{1,2},{2,3},{3,0},{4,5},{5,6},{6,7},{7,4},{8,9},{9,10},{10,1... | collective-permute-start | bytes 786440 | tf_op jit(solution)/shard_map/ppermute | solution.py:41
  245.8 14.5 %collective-permute-start.52 = (bf16[128,1024]{1,0:T(8,128)(2,1)S(1)}, bf16[128,1024]{1,0:T(8,128)(2,1)S(1)}, u32[]{:S(2)}, u32[]{:S(2)}) collective-permute-start(bf16[128,1024]{1,0:T(8,128)(2,1)S(1)} %get-tuple-element.336), channel_id=1, source_target_pairs={{0,3},{1,0},{2,1},{3,2},{4,7},{5,4},{6,5},{7,6},{8,11},{9,8},{10,9... | collective-permute-start | bytes 786440 | tf_op jit(solution)/shard_map/ppermute | solution.py:41
  266.0 14.9 %collective-permute-start.58 = (bf16[2,128,1024]{2,1,0:T(8,128)(2,1)}, bf16[2,128,1024]{2,1,0:T(8,128)(2,1)S(1)}, u32[]{:S(2)}, u32[]{:S(2)}) collective-permute-start(bf16[2,128,1024]{2,1,0:T(8,128)(2,1)} %copy-done.22), channel_id=1, source_target_pairs={{0,16},{16,32},{32,48},{48,0},{1,17},{17,33},{33,49},{49,1},{2,18}... | collective-permute-start | bytes 1572872 | tf_op jit(solution)/shard_map/ppermute | solution.py:41
  267.5 14.3 %collective-permute-start.59 = (bf16[2,128,1024]{2,1,0:T(8,128)(2,1)}, bf16[2,128,1024]{2,1,0:T(8,128)(2,1)S(1)}, u32[]{:S(2)}, u32[]{:S(2)}) collective-permute-start(bf16[2,128,1024]{2,1,0:T(8,128)(2,1)} %copy-done.21), channel_id=1, source_target_pairs={{0,48},{16,0},{32,16},{48,32},{1,49},{17,1},{33,17},{49,33},{2,50}... | collective-permute-start | bytes 1572872 | tf_op jit(solution)/shard_map/ppermute | solution.py:41
  268.0 25.6 %collective-permute-start.60 = (bf16[2,128,1024]{2,1,0:T(8,128)(2,1)}, bf16[2,128,1024]{2,1,0:T(8,128)(2,1)S(1)}, u32[]{:S(2)}, u32[]{:S(2)}) collective-permute-start(bf16[2,128,1024]{2,1,0:T(8,128)(2,1)} %copy-done.20), channel_id=1, source_target_pairs={{0,32},{16,48},{32,0},{48,16},{1,33},{17,49},{33,1},{49,17},{2,34}... | collective-permute-start | bytes 1572872 | tf_op jit(solution)/shard_map/ppermute | solution.py:41
  272.6 25.5 %collective-permute-start.57 = (bf16[128,1024]{1,0:T(8,128)(2,1)S(1)}, bf16[128,1024]{1,0:T(8,128)(2,1)S(1)}, u32[]{:S(2)}, u32[]{:S(2)}) collective-permute-start(bf16[128,1024]{1,0:T(8,128)(2,1)S(1)} %get-tuple-element.332), channel_id=1, source_target_pairs={{0,2},{1,3},{2,0},{3,1},{4,6},{5,7},{6,4},{7,5},{8,10},{9,11},{10,... | collective-permute-start | bytes 786440 | tf_op jit(solution)/shard_map/ppermute | solution.py:41
  272.7 25.5 %collective-permute-start.56 = (bf16[128,1024]{1,0:T(8,128)(2,1)S(1)}, bf16[128,1024]{1,0:T(8,128)(2,1)S(1)}, u32[]{:S(2)}, u32[]{:S(2)}) collective-permute-start(bf16[128,1024]{1,0:T(8,128)(2,1)S(1)} %get-tuple-element.333), channel_id=1, source_target_pairs={{0,1},{1,2},{2,3},{3,0},{4,5},{5,6},{6,7},{7,4},{8,9},{9,10},{10,1... | collective-permute-start | bytes 786440 | tf_op jit(solution)/shard_map/ppermute | solution.py:41
  280.9 17.2 %collective-permute-start.55 = (bf16[128,1024]{1,0:T(8,128)(2,1)S(1)}, bf16[128,1024]{1,0:T(8,128)(2,1)S(1)}, u32[]{:S(2)}, u32[]{:S(2)}) collective-permute-start(bf16[128,1024]{1,0:T(8,128)(2,1)S(1)} %get-tuple-element.331), channel_id=1, source_target_pairs={{0,3},{1,0},{2,1},{3,2},{4,7},{5,4},{6,5},{7,6},{8,11},{9,8},{10,9... | collective-permute-start | bytes 786440 | tf_op jit(solution)/shard_map/ppermute | solution.py:41
  309.4 13.2 %collective-permute-start.62 = (bf16[128,1024]{1,0:T(8,128)(2,1)S(1)}, bf16[128,1024]{1,0:T(8,128)(2,1)S(1)}, u32[]{:S(2)}, u32[]{:S(2)}) collective-permute-start(bf16[128,1024]{1,0:T(8,128)(2,1)S(1)} %get-tuple-element.278), channel_id=1, source_target_pairs={{0,3},{1,0},{2,1},{3,2},{4,7},{5,4},{6,5},{7,6},{8,11},{9,8},{10,9... | collective-permute-start | bytes 786440 | tf_op jit(solution)/shard_map/ppermute | solution.py:41
  310.6 14.5 %collective-permute-start.61 = (bf16[128,1024]{1,0:T(8,128)(2,1)S(1)}, bf16[128,1024]{1,0:T(8,128)(2,1)S(1)}, u32[]{:S(2)}, u32[]{:S(2)}) collective-permute-start(bf16[128,1024]{1,0:T(8,128)(2,1)S(1)} %get-tuple-element.278), channel_id=1, source_target_pairs={{0,1},{1,2},{2,3},{3,0},{4,5},{5,6},{6,7},{7,4},{8,9},{9,10},{10,1... | collective-permute-start | bytes 786440 | tf_op jit(solution)/shard_map/ppermute | solution.py:41
  343.4 13.5 %collective-permute-start.76 = (bf16[2,128,512]{2,1,0:T(8,128)(2,1)S(1)}, bf16[2,128,512]{2,1,0:T(8,128)(2,1)S(1)}, u32[]{:S(2)}, u32[]{:S(2)}) collective-permute-start(bf16[2,128,512]{2,1,0:T(8,128)(2,1)S(1)} %copy-done.27), channel_id=1, source_target_pairs={{0,32},{16,48},{32,0},{48,16},{1,33},{17,49},{33,1},{49,17},{2,34}... | collective-permute-start | bytes 786440 | tf_op jit(solution)/shard_map/ppermute | solution.py:41
  344.8 42.4 %collective-permute-start.114 = (f32[64,1024]{1,0:T(8,128)}, f32[64,1024]{1,0:T(8,128)S(1)}, u32[]{:S(2)}, u32[]{:S(2)}) collective-permute-start(f32[64,1024]{1,0:T(8,128)} %get-tuple-element.249), channel_id=1, source_target_pairs={{0,8},{12,4},{1,9},{13,5},{2,10},{14,6},{3,11},{15,7},{16,24},{28,... | collective-permute-start | bytes 786440 | tf_op jit(solution)/shard_map/ppermute | solution.py:196
  348.2 13.5 %collective-permute-start.73 = (bf16[128,1024]{1,0:T(8,128)(2,1)S(1)}, bf16[128,1024]{1,0:T(8,128)(2,1)S(1)}, u32[]{:S(2)}, u32[]{:S(2)}) collective-permute-start(bf16[128,1024]{1,0:T(8,128)(2,1)S(1)} %get-tuple-element.326), channel_id=1, source_target_pairs={{0,2},{1,3},{2,0},{3,1},{4,6},{5,7},{6,4},{7,5},{8,10},{9,11},{10,... | collective-permute-start | bytes 786440 | tf_op jit(solution)/shard_map/ppermute | solution.py:41
  373.1 13.5 %collective-permute-start.77 = (bf16[128,1024]{1,0:T(8,128)(2,1)S(1)}, bf16[128,1024]{1,0:T(8,128)(2,1)S(1)}, u32[]{:S(2)}, u32[]{:S(2)}) collective-permute-start(bf16[128,1024]{1,0:T(8,128)(2,1)S(1)} %get-tuple-element.283), channel_id=1, source_target_pairs={{0,1},{1,2},{2,3},{3,0},{4,5},{5,6},{6,7},{7,4},{8,9},{9,10},{10,1... | collective-permute-start | bytes 786440 | tf_op jit(solution)/shard_map/ppermute | solution.py:41
  389.0 24.4 %collective-permute-start.69 = (f32[128,1024]{1,0:T(8,128)}, f32[128,1024]{1,0:T(8,128)}, u32[]{:S(2)}, u32[]{:S(2)}) collective-permute-start(f32[128,1024]{1,0:T(8,128)} %add_add_fusion.6), channel_id=1, source_target_pairs={{0,0},{4,8},{8,4},{12,12},{1,1},{5,9},{9,5},{13,13},{2,2},{6,10},{... | collective-permute-start | bytes 1572872 | tf_op jit(solution)/shard_map/ppermute | solution.py:49
  394.5 22.8 %collective-permute-start.109 = (f32[64,512]{1,0:T(8,128)S(1)}, f32[64,512]{1,0:T(8,128)}, u32[]{:S(2)}, u32[]{:S(2)}) collective-permute-start(f32[64,512]{1,0:T(8,128)S(1)} %get-tuple-element.243), channel_id=1, source_target_pairs={{0,8},{12,4},{1,9},{13,5},{2,10},{14,6},{3,11},{15,7},{16,24},{28,... | collective-permute-start | bytes 393224 | tf_op jit(solution)/shard_map/ppermute | solution.py:196
  413.4 25.0 %collective-permute-start.88 = (bf16[2,128,1024]{2,1,0:T(8,128)(2,1)}, bf16[2,128,1024]{2,1,0:T(8,128)(2,1)}, u32[]{:S(2)}, u32[]{:S(2)}) collective-permute-start(bf16[2,128,1024]{2,1,0:T(8,128)(2,1)} %copy-done.25), channel_id=1, source_target_pairs={{0,16},{16,32},{32,48},{48,0},{1,17},{17,33},{33,49},{49,1},{2,18}... | collective-permute-start | bytes 1572872 | tf_op jit(solution)/shard_map/ppermute | solution.py:41
  415.8 24.8 %collective-permute-start.89 = (bf16[2,128,1024]{2,1,0:T(8,128)(2,1)}, bf16[2,128,1024]{2,1,0:T(8,128)(2,1)}, u32[]{:S(2)}, u32[]{:S(2)}) collective-permute-start(bf16[2,128,1024]{2,1,0:T(8,128)(2,1)} %copy-done.24), channel_id=1, source_target_pairs={{0,48},{16,0},{32,16},{48,32},{1,49},{17,1},{33,17},{49,33},{2,50}... | collective-permute-start | bytes 1572872 | tf_op jit(solution)/shard_map/ppermute | solution.py:41
  415.8 24.8 %collective-permute-start.90 = (bf16[2,128,1024]{2,1,0:T(8,128)(2,1)}, bf16[2,128,1024]{2,1,0:T(8,128)(2,1)}, u32[]{:S(2)}, u32[]{:S(2)}) collective-permute-start(bf16[2,128,1024]{2,1,0:T(8,128)(2,1)} %copy-done.23), channel_id=1, source_target_pairs={{0,32},{16,48},{32,0},{48,16},{1,33},{17,49},{33,1},{49,17},{2,34}... | collective-permute-start | bytes 1572872 | tf_op jit(solution)/shard_map/ppermute | solution.py:41
  420.9 27.1 %collective-permute-start.87 = (bf16[128,1024]{1,0:T(8,128)(2,1)S(1)}, bf16[128,1024]{1,0:T(8,128)(2,1)S(1)}, u32[]{:S(2)}, u32[]{:S(2)}) collective-permute-start(bf16[128,1024]{1,0:T(8,128)(2,1)S(1)} %get-tuple-element.323), channel_id=1, source_target_pairs={{0,2},{1,3},{2,0},{3,1},{4,6},{5,7},{6,4},{7,5},{8,10},{9,11},{10,... | collective-permute-start | bytes 786440 | tf_op jit(solution)/shard_map/ppermute | solution.py:41
  422.5 25.5 %collective-permute-start.86 = (bf16[128,1024]{1,0:T(8,128)(2,1)S(1)}, bf16[128,1024]{1,0:T(8,128)(2,1)S(1)}, u32[]{:S(2)}, u32[]{:S(2)}) collective-permute-start(bf16[128,1024]{1,0:T(8,128)(2,1)S(1)} %get-tuple-element.324), channel_id=1, source_target_pairs={{0,1},{1,2},{2,3},{3,0},{4,5},{5,6},{6,7},{7,4},{8,9},{9,10},{10,1... | collective-permute-start | bytes 786440 | tf_op jit(solution)/shard_map/ppermute | solution.py:41
  450.8 16.5 %collective-permute-start.104 = (bf16[2,128,512]{2,1,0:T(8,128)(2,1)}, bf16[2,128,512]{2,1,0:T(8,128)(2,1)S(1)}, u32[]{:S(2)}, u32[]{:S(2)}) collective-permute-start(bf16[2,128,512]{2,1,0:T(8,128)(2,1)} %copy-done.34), channel_id=1, source_target_pairs={{0,32},{16,48},{32,0},{48,16},{1,33},{17,49},{33,1},{49,17},{2,34}... | collective-permute-start | bytes 786440 | tf_op jit(solution)/shard_map/ppermute | solution.py:41
  452.6 16.0 %collective-permute-start.103 = (bf16[2,128,512]{2,1,0:T(8,128)(2,1)}, bf16[2,128,512]{2,1,0:T(8,128)(2,1)S(1)}, u32[]{:S(2)}, u32[]{:S(2)}) collective-permute-start(bf16[2,128,512]{2,1,0:T(8,128)(2,1)} %copy-done.33), channel_id=1, source_target_pairs={{0,48},{16,0},{32,16},{48,32},{1,49},{17,1},{33,17},{49,33},{2,50}... | collective-permute-start | bytes 786440 | tf_op jit(solution)/shard_map/ppermute | solution.py:41
  455.4 14.5 %collective-permute-start.102 = (bf16[2,128,512]{2,1,0:T(8,128)(2,1)}, bf16[2,128,512]{2,1,0:T(8,128)(2,1)S(1)}, u32[]{:S(2)}, u32[]{:S(2)}) collective-permute-start(bf16[2,128,512]{2,1,0:T(8,128)(2,1)} %copy-done.32), channel_id=1, source_target_pairs={{0,16},{16,32},{32,48},{48,0},{1,17},{17,33},{33,49},{49,1},{2,18}... | collective-permute-start | bytes 786440 | tf_op jit(solution)/shard_map/ppermute | solution.py:41
  461.2 46.3 %collective-permute-start.91 = (f32[128,1024]{1,0:T(8,128)S(1)}, f32[128,1024]{1,0:T(8,128)S(1)}, u32[]{:S(2)}, u32[]{:S(2)}) collective-permute-start(f32[128,1024]{1,0:T(8,128)S(1)} %add_add_fusion.4), channel_id=1, source_target_pairs={{0,0},{4,8},{8,4},{12,12},{1,1},{5,9},{9,5},{13,13},{2,2},{6,10},{... | collective-permute-start | bytes 1572872 | tf_op jit(solution)/shard_map/ppermute | solution.py:49
  463.9 12.8 %collective-permute-start.112 = (bf16[128,1024]{1,0:T(8,128)(2,1)}, bf16[128,1024]{1,0:T(8,128)(2,1)S(1)}, u32[]{:S(2)}, u32[]{:S(2)}) collective-permute-start(bf16[128,1024]{1,0:T(8,128)(2,1)} %get-tuple-element.247), channel_id=1, source_target_pairs={{0,64},{12,76},{64,0},{76,12},{1,65},{13,77},{65,1},{77,13},{2,66}... | collective-permute-start | bytes 786440 | tf_op jit(solution)/shard_map/ppermute | solution.py:184
  469.9 15.3 %collective-permute-start.97 = (f32[192,128]{1,0:T(8,128)S(1)}, f32[192,128]{1,0:T(8,128)S(1)}, u32[]{:S(2)}, u32[]{:S(2)}) collective-permute-start(f32[192,128]{1,0:T(8,128)S(1)} %add_add_fusion.12), channel_id=1, source_target_pairs={{0,16},{16,32},{32,48},{48,0},{1,17},{17,33},{33,49},{49,1},{2,18}... | collective-permute-start | bytes 294920 | tf_op jit(solution)/shard_map/ppermute | solution.py:41
  487.8 16.8 %collective-permute-start.113 = (f32[64,1024]{1,0:T(8,128)S(1)}, f32[64,1024]{1,0:T(8,128)S(1)}, u32[]{:S(2)}, u32[]{:S(2)}) collective-permute-start(f32[64,1024]{1,0:T(8,128)S(1)} %slice_select_fusion), channel_id=1, source_target_pairs={{0,8},{12,4},{1,9},{13,5},{2,10},{14,6},{3,11},{15,7},{16,24},{28,... | collective-permute-start | bytes 786440 | tf_op jit(solution)/shard_map/ppermute | solution.py:196
  (182 other events, 1699.5 us)

commit v4 on v3

--- a/solution.py
+++ b/solution.py
@@ -95,13 +95,14 @@
     return gather_pair(mine), results
 
 
-def scatter_pair(partial):
-    half = partial.shape[0] // 2
-    return partial[:half] + swap_cores(partial[half:].astype(BF)).astype(F32)
-
-
-def scatter_rows(partial, tasks=()):
-    both = scatter_pair(partial)
+def scatter_pair(left, product):
+    half = left.shape[0] // 2
+    other = swap_cores(product(left[half:]).astype(BF))
+    return product(left[:half]) + other.astype(F32)
+
+
+def scatter_rows(left, product, tasks=()):
+    both = scatter_pair(left, product)
     low = both.astype(BF)
     rows = low.shape[0] // 4
     total = (
@@ -111,6 +112,14 @@
         + ring(low[3 * rows :], "z", 2).astype(F32)
     )
     return run_beside(low, total, tasks)
+
+
+def times(weight):
+    return lambda left: jnp.dot(left, weight, preferred_element_type=F32)
+
+
+def times_rows(weight):
+    return lambda left: against_rows(left, weight)
 
 
 def grad_blocks(pairs):
@@ -197,13 +206,20 @@
     return jnp.where(lax.axis_index("c") == lax.axis_index("yl"), keep, got)
 
 
-def sum_everywhere(values):
-    values = values + swap_cores(values)
-    for axis in ("z", "x", "y"):
+def sum_everywhere(common, shard, steps, state):
+    rows = common.shape[0]
+    values = common
+    for axis, step in zip(("z", "x", "y"), steps):
+        if axis == "x":
+            values = jnp.concatenate([values, shard])
         values = (values + ring(values, axis, 2)) + (
             ring(values, axis, 1) + ring(values, axis, -1)
         )
-    return values
+        values, state = lax.optimization_barrier((values, state))
+        state = step(*state)
+    other = swap_cores(values)
+    own = lax.axis_index("c") == lax.axis_index("yl")
+    return values[:rows] + other[:rows], jnp.where(own, values[rows:], other[rows:]), state
 
 
 def row_places():
@@ -220,12 +236,12 @@
     mask = query_place[...] >= key_place[...]
     for head in range(q_ref.shape[1] // HEAD_DIM):
         cut = slice(head * HEAD_DIM, (head + 1) * HEAD_DIM)
-        scores = against_rows(k_ref[:, cut], q_ref[:, cut]) * HEAD_DIM ** (-0.5)
+        scores = against_rows(k_ref[:, cut], q_ref[:, cut] * HEAD_DIM ** (-0.5))
         scores = jnp.where(mask, scores, NEG_FILL)
         peak = jnp.max(scores, 0, keepdims=True)
         weights = jnp.exp(scores - peak)
         total = jnp.sum(weights, 0, keepdims=True)
-        weights = (weights / total).astype(BF)
+        weights = (weights * (1.0 / total)).astype(BF)
         out_ref[:, cut] = tokens_inner(v_ref[:, cut], weights).T.astype(BF)
         log_ref[head : head + 1, :] = peak + jnp.log(total)
 
@@ -274,8 +290,8 @@
 
     for head in range(width // HEAD_DIM):
         cut = slice(head * HEAD_DIM, (head + 1) * HEAD_DIM)
-        q, k, v, do = q_ref[:, cut], k_ref[:, cut], v_ref[:, cut], do_ref[:, cut]
-        scores = jnp.where(mask, against_rows(k, q) * scale, NEG_FILL)
+        q, k, v, do = q_ref[:, cut] * scale, k_ref[:, cut], v_ref[:, cut], do_ref[:, cut]
+        scores = jnp.where(mask, against_rows(k, q), NEG_FILL)
         weights = jnp.exp(scores - log_ref[head : head + 1, :])
         grad_weights = against_rows(v, do)
         mean = jnp.sum(weights * grad_weights, 0, keepdims=True)
@@ -286,7 +302,7 @@
 
     @pl.when(step == pl.num_programs(0) - 1)
     def _():
-        out_ref[:, width : 2 * width] = (dk_ref[...] * scale).astype(BF)
+        out_ref[:, width : 2 * width] = dk_ref[...].astype(BF)
         out_ref[:, 2 * width :] = dv_ref[...].astype(BF)
 
 
@@ -358,7 +374,12 @@
 
     for layer in range(LAYERS):
         normed = layer_norm(stream, norm_gain[layer, 0], norm_shift[layer, 0]).astype(BF)
-        normed_all, _ = gather_rows(normed)
+        mine, _ = gather_ring(normed)
+        if layer == 1:
+            mine, w_up[1], w_down[1] = lax.optimization_barrier((mine, w_up[1], w_down[1]))
+        normed_all = gather_pair(mine)
+        if layer == 0:
+            normed_all, w_up[0] = lax.optimization_barrier((normed_all, w_up[0]))
         qkv_bias = jnp.concatenate(
             [bias_in[layer, 0], jnp.zeros((columns,), F32), bias_in[layer, 1]]
         )
@@ -370,20 +391,16 @@
             normed_all, attended, cotangent_task(1 if layer == 0 else 2)
         )
         pieces[1 if layer == 0 else 2] = piece
-        if layer == 1:
-            attended, w_up[1], w_down[1] = lax.optimization_barrier(
-                (attended, w_up[1], w_down[1])
-            )
+        if layer == 0:
+            attended, w_down[0] = lax.optimization_barrier((attended, w_down[0]))
         middle = stream + (
-            scatter_rows(jnp.dot(attended, w_out[layer], preferred_element_type=F32))[0]
+            scatter_rows(attended, times(w_out[layer]))[0]
             + outward_bias[layer]
         )
         normed_mid = layer_norm(middle, norm_gain[layer, 1], norm_shift[layer, 1]).astype(BF)
+        mid_mine, _ = gather_ring(normed_mid)
         if layer == 0:
-            normed_mid, w_up[0], w_down[0] = lax.optimization_barrier(
-                (normed_mid, w_up[0], w_down[0])
-            )
-        mid_mine, _ = gather_ring(normed_mid)
+            mid_mine, w_in[1], w_out[1] = lax.optimization_barrier((mid_mine, w_in[1], w_out[1]))
         mid_all = gather_pair(mid_mine)
         hidden_pre = (
             jnp.dot(mid_all, w_up[layer], preferred_element_type=F32) + bias_up[layer]
@@ -395,11 +412,8 @@
         )
         if layer == 0:
             activated, (pieces[-1],) = run_beside(mid_mine, activated, cotangent_task(-1))
-            activated, w_in[1], w_out[1] = lax.optimization_barrier(
-                (activated, w_in[1], w_out[1])
-            )
             stream = middle + (
-                scatter_rows(jnp.dot(activated, w_down[layer], preferred_element_type=F32))[0]
+                scatter_rows(activated, times(w_down[layer]))[0]
                 + shrink_bias[layer]
             )
     cotangent_ring = jnp.concatenate([cotangent, pieces[1], pieces[-1], pieces[2]])
@@ -426,7 +440,7 @@
             return grad_blocks([(dy_all, activated), (mid_all, du)])
 
         dh, results = scatter_rows(
-            against_rows(du, w_up[layer]), [(make, (dy_all, activated, mid_all, du))] + tasks
+            du, times_rows(w_up[layer]), [(make, (dy_all, activated, mid_all, du))] + tasks
         )
         back_mid = jax.vjp(layer_norm, middle, norm_gain[layer, 1], norm_shift[layer, 1])[1]
         grad_part, gains[layer, 1], shifts[layer, 1] = back_mid(dh)
@@ -441,7 +455,7 @@
             return grad_blocks([(dz_all, attended), (normed_all, dqkv)])
 
         da, results = scatter_rows(
-            against_rows(dqkv, w_in[layer]), [(make, (dz_all, attended, normed_all, dqkv))] + tasks
+            dqkv, times_rows(w_in[layer]), [(make, (dz_all, attended, normed_all, dqkv))] + tasks
         )
         back_in = jax.vjp(layer_norm, stream, norm_gain[layer, 0], norm_shift[layer, 0])[1]
         grad_first, gains[layer, 0], shifts[layer, 0] = back_in(da)
@@ -453,12 +467,14 @@
     mlp1 = send_x(mlp1)
     dz = grad_middle.astype(BF)
     sums_out[1] = jnp.sum(dz, 0, dtype=F32)
-    dz_all, _ = gather_rows(dz)
+    dz_mine, _ = gather_ring(dz)
+    dz_mine, near1 = lax.optimization_barrier((dz_mine, mlp1[:3]))
+    dz_all = gather_pair(dz_mine)
     do = against_rows(dz_all, w_out[1]).astype(BF)
     dqkv = attend_backward(qkv, do, log_totals, places)
 
     def last_pairs(activated):
-        both = scatter_pair(jnp.dot(activated, w_down[1], preferred_element_type=F32))
+        both = scatter_pair(activated, times(w_down[1]))
         low = both.astype(BF)
         rows = low.shape[0] // 4
         near = (
@@ -469,47 +485,47 @@
         return near, low[3 * rows :]
 
     dqkv, ((last_near, last_far),) = run_beside(dz_all, dqkv, [(last_pairs, (activated,))])
-    grad_first, (attn1, mlp1) = attn_sum(1, dqkv, dz_all, [(add_x, mlp1)])
+    dqkv, mlp1 = lax.optimization_barrier((dqkv, (*near1, mlp1[3])))
+    mlp1 = send_y(*add_x(*mlp1))
+    grad_first, (attn1, mlp1) = attn_sum(1, dqkv, dz_all, [(add_y, mlp1)])
     grad_stream = grad_middle + grad_first
-    attn1, mlp1 = send_x(attn1), send_y(*mlp1)
+    attn1 = send_x(attn1)
+    grads_mlp[1] = send_core(*mlp1)
 
     _, normed_all, qkv, attended, log_totals, middle, mid_all, hidden_pre, activated = saved[0]
     dy = grad_stream.astype(BF)
     sums_down[0] = jnp.sum(dy, 0, dtype=F32)
-    dy_mine, (mlp1,) = gather_ring(dy, [(add_y, mlp1)])
-    grads_mlp[1] = send_core(*mlp1)
+    dy_mine, _ = gather_ring(dy)
+    dy_mine, attn1 = lax.optimization_barrier((dy_mine, attn1))
+    attn1 = send_y(*add_x(*attn1))
     dy_all = gather_pair(dy_mine)
     du = mlp_back(0, dy_all)
     du, (last_across,) = run_beside(
         dy_mine, du, [(lambda values: ring(values, "z", 2), (last_far,))]
     )
-    hidden_out = swap_halves(
-        saved[1][5] + (last_near + last_across.astype(F32) + shrink_bias[1])
-    )
-    grad_part, (mlp0, attn1) = mlp_sum(0, du, dy_all, [(add_x, attn1)])
+    hidden_out = saved[1][5] + (last_near + last_across.astype(F32) + shrink_bias[1])
+    hidden_out = swap_halves(hidden_out.astype(BF)).astype(F32)
+    du, attn1 = lax.optimization_barrier((du, attn1))
+    grad_part, (mlp0, attn1) = mlp_sum(0, du, dy_all, [(add_y, attn1)])
     grad_middle = grad_stream + grad_part
-    mlp0, attn1 = send_x(mlp0), send_y(*attn1)
+    mlp0 = send_x(mlp0)
+    grads_attn[1] = send_core(*attn1)
     dz = grad_middle.astype(BF)
     sums_out[0] = jnp.sum(dz, 0, dtype=F32)
-    dz_all, (attn1,) = gather_rows(dz, [(add_y, attn1)])
-    grads_attn[1] = send_core(*attn1)
+    dz_mine, _ = gather_ring(dz)
+    dz_mine, near0 = lax.optimization_barrier((dz_mine, mlp0[:3]))
+    dz_all = gather_pair(dz_mine)
     do = against_rows(dz_all, w_out[0]).astype(BF)
     dqkv = attend_backward(qkv, do, log_totals, places)
-    grad_first, (attn0, mlp0) = attn_sum(0, dqkv, dz_all, [(add_x, mlp0)])
+    dqkv, mlp0 = lax.optimization_barrier((dqkv, (*near0, mlp0[3])))
+    mlp0 = send_y(*add_x(*mlp0))
+    grad_first, (attn0, mlp0) = attn_sum(0, dqkv, dz_all, [(add_y, mlp0)])
     grad_stream = grad_middle + grad_first
-    grad_hidden = swap_halves(grad_stream)
-    attn0 = add_x(*send_x(attn0))
-    grads_mlp[0] = send_core(*add_y(*send_y(*mlp0)))
-    grads_attn[0] = send_core(*add_y(*send_y(*attn0)))
-
-    shard = lax.axis_index("c") * 4 + lax.axis_index("z")
-    own = lax.axis_index("yl") * 4 + lax.axis_index("z")
+    grad_hidden = swap_halves(grad_stream.astype(BF)).astype(F32)
+    grads_mlp[0] = send_core(*mlp0)
+
     both = range(LAYERS)
-    up = jnp.stack([sums_up[n] for n in both])[:, None]
-    qv = jnp.stack([sums_in[n] for n in both])[:, :, None]
-    up = lax.dynamic_update_slice_in_dim(jnp.zeros((LAYERS, 8, up.shape[2]), F32), up, shard, 1)
-    qv = lax.dynamic_update_slice_in_dim(jnp.zeros((LAYERS, 2, 8, columns), F32), qv, shard, 2)
-    vectors = jnp.concatenate(
+    common = jnp.concatenate(
         [
             m.reshape(-1, 128)
             for m in (
@@ -517,19 +533,28 @@
                 + [shifts[n, i] for n in both for i in (0, 1)]
                 + [sums_out[n] for n in both]
                 + [sums_down[n] for n in both]
-                + [up, qv]
             )
         ]
     )
-    vectors = sum_everywhere(vectors)
-    grad_gain = vectors[:32].reshape(LAYERS, 2, 1024)
-    grad_shift = vectors[32:64].reshape(LAYERS, 2, 1024)
-    grad_out_bias = vectors[64:80].reshape(LAYERS, 1024)
-    grad_down_bias = vectors[80:96].reshape(LAYERS, 1024)
-    up = vectors[96:160].reshape(LAYERS, 8, -1)
-    qv = vectors[160:].reshape(LAYERS, 2, 8, columns)
-    grad_up_bias = lax.dynamic_index_in_dim(up, own, 1, keepdims=False)
-    grad_in_bias = lax.dynamic_index_in_dim(qv, own, 2, keepdims=False)
+    shard = jnp.concatenate(
+        [m.reshape(-1, 128) for m in [sums_up[n] for n in both] + [sums_in[n] for n in both]]
+    )
+    common, shard, grads_attn[0] = sum_everywhere(
+        common,
+        shard,
+        (
+            lambda *m: m,
+            lambda *m: send_y(*add_x(*m)),
+            lambda *m: send_core(*add_y(*m)),
+        ),
+        send_x(attn0),
+    )
+    grad_gain = common[:32].reshape(LAYERS, 2, 1024)
+    grad_shift = common[32:64].reshape(LAYERS, 2, 1024)
+    grad_out_bias = common[64:80].reshape(LAYERS, 1024)
+    grad_down_bias = common[80:96].reshape(LAYERS, 1024)
+    grad_up_bias = shard[:8].reshape(LAYERS, -1)
+    grad_in_bias = shard[8:].reshape(LAYERS, 2, columns)
 
     width = shrink.shape[1]
     return (

time: 520 us -> 482 us (0.927)
  the two profiles are of different devices: /device:TPU:2 before, /device:TPU:1 now
where the time goes in v4:
time: 482 us; the launch traced here: 472 us
  starting transfers between devices  174 us (36%)
  waiting for transfers between devices  141 us (29%)
  Pallas kernels  53.7 us (11%)
  matrix products  41.6 us (9%)
  local copies, waits for them, and re-layouts  30.8 us (6%)
  other arithmetic  28.3 us (6%)
    ppermute x69, waiting for transfers between devices, ring(): lax.ppermute(values, RINGS[axis], [(i, (i + step) % 4) for i in range(4)])  115 us
    ppermute x69, starting transfers between devices, ring(): lax.ppermute(values, RINGS[axis], [(i, (i + step) % 4) for i in range(4)])  94.4 us
    dot_general x12, matrix products, against_rows(): lax.dot_general(left, right, (((1,), (1,)), ((), ())), preferred_element_...  25.3 us
    ppermute x17, starting transfers between devices, swap_cores(): return lax.ppermute(values, 'c', [(0, 1), (1, 0)])  23.8 us
    pallas_call x2, Pallas kernels, attend_backward(): pl.pallas_call(attend_backward_kernel, grid=(tokens // QUERY_ROWS,), in_s...  19.9 us
    ppermute x17, waiting for transfers between devices, swap_cores(): return lax.ppermute(values, 'c', [(0, 1), (1, 0)])  18.9 us
    pallas_call x4, Pallas kernels, grad_blocks(): pl.pallas_call(kernel, grid_spec=pltpu.PrefetchScalarGridSpec(num_scalar_...  17.6 us
    ppermute x4, starting transfers between devices, swap_halves(): return lax.ppermute(values, ('c', 'yl'), [(0, 0), (1, 2), (2, 1), (3, 3)])  16.7 us
  transfers between devices with their start and end apart: 115, of which 48 were waited for; matrix products, arithmetic and copies ran while one was open for 14% of the time, Pallas kernels for 11%

profile of v4, /device:TPU:1, one launch (start us, length us, event | category | flops | bytes accessed | tf_op | source)
XLA Modules:
  0.0 472.4 jit_solution(16488617229437299304)
XLA Ops:
  0.7 4.7 %collective-permute-start = (bf16[128,1024]{1,0:T(8,128)(2,1)}, bf16[128,1024]{1,0:T(8,128)(2,1)S(1)}, u32[]{:S(2)}, u32[]{:S(2)}) collective-permute-start(bf16[128,1024]{1,0:T(8,128)(2,1)} %param.12), channel_id=1, source_target_pairs={{0,0},{4,8},{8,4},{12,12},{1,1},{5,9},{9,5},{13,13},{2,2},{6,10},{... | collective-permute-start | bytes 786440 | tf_op jit(solution)/shard_map/ppermute | solution.py:49
  5.4 3.0 slice_bitcast_fusion.1
  11.9 3.7 collective-permute-start.3
  17.1 3.1 slice_bitcast_fusion
  20.6 4.2 collective-permute-start.7
  24.7 2.9 collective-permute-done.2
  27.7 5.3 %collective-permute-start.8 = (bf16[128,1024]{1,0:T(8,128)(2,1)S(1)}, bf16[128,1024]{1,0:T(8,128)(2,1)S(1)}, u32[]{:S(2)}, u32[]{:S(2)}) collective-permute-start(bf16[128,1024]{1,0:T(8,128)(2,1)S(1)} %copy-done.119), channel_id=1, source_target_pairs={{0,0},{4,8},{8,4},{12,12},{1,1},{5,9},{9,5},{13,13},{2,2},{6,10},{... | collective-permute-start | bytes 786440 | tf_op jit(solution)/shard_map/ppermute | solution.py:49
  37.8 2.9 add_convert_fusion.1.q_ref.k_ref.v_ref
  40.7 8.1 %shard_map.211 = (bf16[1024,128]{1,0:T(8,128)(2,1)S(1)}, f32[2,1024]{1,0:T(2,128)S(1)}) custom-call(s32[1,1024]{1,0:T(1,128)S(1)} %bitcast.170, s32[1024,1]{1,0:T(8,128)S(1)} %copy.27.key_place, bf16[1024,384]{1,0:T(8,128)(2,1)S(1)} %add_convert_fusion.1.q_ref.k_ref.v_ref, bf16[1024,384]{1,0:T(8,128)(2,1)S(1)} %add_convert_fusion.1.q_ref.k_ref.v_ref, ...), custom_call_target="tpu_custom_call" | custom-call | flops 1073741824 | bytes 2097152 | tf_op jit(solution)/shard_map/pallas_call | solution.py:252
  54.7 3.0 collective-permute-start.15
  64.1 6.1 %collective-permute-done.14 = bf16[128,1024]{1,0:T(8,128)(2,1)S(1)} collective-permute-done((bf16[128,1024]{1,0:T(8,128)(2,1)}, bf16[128,1024]{1,0:T(8,128)(2,1)S(1)}, u32[]{:S(2)}, u32[]{:S(2)}) %collective-permute-start.14) | collective-permute-done | bytes 262176 | tf_op jit(solution)/shard_map/ppermute | solution.py:41
  77.1 4.0 collective-permute-done.18
  81.1 5.5 %collective-permute-done.17 = bf16[128,1024]{1,0:T(8,128)(2,1)S(1)} collective-permute-done((bf16[128,1024]{1,0:T(8,128)(2,1)S(1)}, bf16[128,1024]{1,0:T(8,128)(2,1)S(1)}, u32[]{:S(2)}, u32[]{:S(2)}) %collective-permute-start.17) | collective-permute-done | bytes 262176 | tf_op jit(solution)/shard_map/ppermute | solution.py:41
  90.8 5.1 %multiply_convert_fusion.1 = (bf16[1024,512]{1,0:T(8,128)(2,1)S(1)}, f32[1024,512]{1,0:T(8,128)}) fusion(f32[512]{0:T(512)S(1)} %get-tuple-element.415, bf16[1024,1024]{1,0:T(8,128)(2,1)S(1)} %constant_dynamic-update-slice_fusion.refs_2_.refs_3_, bf16[1024,512]{1,0:T(8,128)(2,1)} %collective-permute-done.5), kind=kOutput, calls=%fused_computation.32 | convolution fusion | flops 1078984704 | bytes 6293504 | tf_op jit(solution)/shard_map/dot_general | solution.py:406
  110.1 6.3 %collective-permute-done.25 = bf16[128,1024]{1,0:T(8,128)(2,1)S(1)} collective-permute-done((bf16[128,1024]{1,0:T(8,128)(2,1)S(1)}, bf16[128,1024]{1,0:T(8,128)(2,1)S(1)}, u32[]{:S(2)}, u32[]{:S(2)}) %collective-permute-start.25) | collective-permute-done | bytes 262176 | tf_op jit(solution)/shard_map/ppermute | solution.py:41
  121.2 4.5 collective-permute-done.29
  125.6 7.1 %collective-permute-done.28 = bf16[128,1024]{1,0:T(8,128)(2,1)S(1)} collective-permute-done((bf16[128,1024]{1,0:T(8,128)(2,1)S(1)}, bf16[128,1024]{1,0:T(8,128)(2,1)S(1)}, u32[]{:S(2)}, u32[]{:S(2)}) %collective-permute-start.28) | collective-permute-done | bytes 262176 | tf_op jit(solution)/shard_map/ppermute | solution.py:41
  140.4 8.1 %shard_map.212 = (bf16[1024,128]{1,0:T(8,128)(2,1)S(1)}, f32[2,1024]{1,0:T(2,128)S(1)}) custom-call(s32[1,1024]{1,0:T(1,128)S(1)} %bitcast.171, s32[1024,1]{1,0:T(8,128)S(1)} %copy.27.key_place, bf16[1024,384]{1,0:T(8,128)(2,1)S(1)} %add_convert_fusion.q_ref.k_ref.v_ref, bf16[1024,384]{1,0:T(8,128)(2,1)S(1)} %add_convert_fusion.q_ref.k_ref.v_ref, ...), custom_call_target="tpu_custom_call" | custom-call | flops 1073741824 | bytes 2097152 | tf_op jit(solution)/shard_map/pallas_call | solution.py:252
  157.4 4.3 collective-permute-done.37
  161.6 6.3 %collective-permute-done.36 = bf16[128,1024]{1,0:T(8,128)(2,1)S(1)} collective-permute-done((bf16[128,1024]{1,0:T(8,128)(2,1)S(1)}, bf16[128,1024]{1,0:T(8,128)(2,1)S(1)}, u32[]{:S(2)}, u32[]{:S(2)}) %collective-permute-start.36) | collective-permute-done | bytes 262176 | tf_op jit(solution)/shard_map/ppermute | solution.py:41
  174.8 3.4 collective-permute-done.40
  178.2 4.8 %collective-permute-done.39 = bf16[128,1024]{1,0:T(8,128)(2,1)S(1)} collective-permute-done((bf16[128,1024]{1,0:T(8,128)(2,1)S(1)}, bf16[128,1024]{1,0:T(8,128)(2,1)S(1)}, u32[]{:S(2)}, u32[]{:S(2)}) %collective-permute-start.39) | collective-permute-done | bytes 262176 | tf_op jit(solution)/shard_map/ppermute | solution.py:41
  188.8 3.7 convert_reduce_fusion
  203.5 3.1 collective-permute-start.44
  206.8 4.5 shard_map.213
  211.4 4.9 %collective-permute-done.45 = bf16[128,1024]{1,0:T(8,128)(2,1)S(1)} collective-permute-done((bf16[128,1024]{1,0:T(8,128)(2,1)S(1)}, bf16[128,1024]{1,0:T(8,128)(2,1)S(1)}, u32[]{:S(2)}, u32[]{:S(2)}) %collective-permute-start.45) | collective-permute-done | bytes 262176 | tf_op jit(solution)/shard_map/ppermute | solution.py:41
  224.1 5.3 %collective-permute-done.49 = bf16[128,1024]{1,0:T(8,128)(2,1)S(1)} collective-permute-done((bf16[128,1024]{1,0:T(8,128)(2,1)S(1)}, bf16[128,1024]{1,0:T(8,128)(2,1)S(1)}, u32[]{:S(2)}, u32[]{:S(2)}) %collective-permute-start.49) | collective-permute-done | bytes 262176 | tf_op jit(solution)/shard_map/ppermute | solution.py:41
  229.4 5.1 %collective-permute-done.48 = bf16[128,1024]{1,0:T(8,128)(2,1)S(1)} collective-permute-done((bf16[128,1024]{1,0:T(8,128)(2,1)S(1)}, bf16[128,1024]{1,0:T(8,128)(2,1)S(1)}, u32[]{:S(2)}, u32[]{:S(2)}) %collective-permute-start.48) | collective-permute-done | bytes 262176 | tf_op jit(solution)/shard_map/ppermute | solution.py:41
  248.1 10.0 %shard_map.214.refs_5_ = bf16[1024,384]{1,0:T(8,128)(2,1)S(1)} custom-call(s32[1,1024]{1,0:T(1,128)S(1)} %bitcast.172, s32[1024,1]{1,0:T(8,128)S(1)} %copy-done.17, f32[2,1024]{1,0:T(2,128)S(1)} %get-tuple-element.171.log_ref, bf16[1024,384]{1,0:T(8,128)(2,1)S(1)} %copy-done.23, bf16[1024,384]{1,0:T(8,128)(2,1)S(1)} %copy-done.23, ...), custom_call_target="tpu_custom_call" | custom-call | flops 2684354560 | bytes 4194304 | tf_op jit(solution)/shard_map/pallas_call | solution.py:312
  263.6 3.4 collective-permute-start.61
  275.7 3.9 shard_map.215
  281.3 6.0 %collective-permute-done.59 = bf16[128,1024]{1,0:T(8,128)(2,1)S(1)} collective-permute-done((bf16[128,1024]{1,0:T(8,128)(2,1)S(1)}, bf16[128,1024]{1,0:T(8,128)(2,1)S(1)}, u32[]{:S(2)}, u32[]{:S(2)}) %collective-permute-start.59) | collective-permute-done | bytes 262176 | tf_op jit(solution)/shard_map/ppermute | solution.py:41
  294.9 3.9 collective-permute-done.66
  302.7 2.8 collective-permute-done.64
  306.0 3.9 collective-permute-start.70
  320.7 3.1 convolution_convert_fusion.4
  330.3 2.8 collective-permute-start.79
  335.8 5.2 %shard_map.216 = (bf16[2,128,1024]{2,1,0:T(8,128)(2,1)S(1)}, bf16[2,128,1024]{2,1,0:T(8,128)(2,1)S(1)}, bf16[2,128,1024]{2,1,0:T(8,128)(2,1)}, bf16[2,128,1024]{2,1,0:T(8,128)(2,1)S(1)}) custom-call(s32[1]{0:T(128)} %bitcast.37.place_ref, bf16[1024,1024]{1,0:T(8,128)(2,1)S(1)} %constant_dynamic-update-slice_fusion.11.refs_0_.refs_1_, ...), custom_call_target="tpu_custom_call" | custom-call | flops 2147483648 | bytes 8388608 | tf_op jit(solution)/shard_map/pallas_call | solution.py:150
  341.1 4.6 collective-permute-done.78
  356.7 4.8 %collective-permute-done.81 = bf16[128,1024]{1,0:T(8,128)(2,1)S(1)} collective-permute-done((bf16[128,1024]{1,0:T(8,128)(2,1)S(1)}, bf16[128,1024]{1,0:T(8,128)(2,1)S(1)}, u32[]{:S(2)}, u32[]{:S(2)}) %collective-permute-start.81) | collective-permute-done | bytes 262176 | tf_op jit(solution)/shard_map/ppermute | solution.py:41
  371.6 3.0 collective-permute-done.72
  382.4 10.0 %shard_map.217.refs_5_ = bf16[1024,384]{1,0:T(8,128)(2,1)S(1)} custom-call(s32[1,1024]{1,0:T(1,128)S(1)} %bitcast.173, s32[1024,1]{1,0:T(8,128)S(1)} %copy-done.18, f32[2,1024]{1,0:T(2,128)S(1)} %get-tuple-element.246.log_ref, bf16[1024,384]{1,0:T(8,128)(2,1)S(1)} %copy-done.21, bf16[1024,384]{1,0:T(8,128)(2,1)S(1)} %copy-done.21, ...), custom_call_target="tpu_custom_call" | custom-call | flops 2684354560 | bytes 4194304 | tf_op jit(solution)/shard_map/pallas_call | solution.py:312
  408.1 3.9 shard_map.218
  412.3 6.8 %collective-permute-done.89 = bf16[128,1024]{1,0:T(8,128)(2,1)S(1)} collective-permute-done((bf16[128,1024]{1,0:T(8,128)(2,1)S(1)}, bf16[128,1024]{1,0:T(8,128)(2,1)S(1)}, u32[]{:S(2)}, u32[]{:S(2)}) %collective-permute-start.89) | collective-permute-done | bytes 262176 | tf_op jit(solution)/shard_map/ppermute | solution.py:41
  429.1 4.7 collective-permute-start.94
  433.8 2.9 collective-permute-done.100
  455.2 3.2 collective-permute-done.108
  458.4 7.2 %collective-permute-start.110 = (f32[108,128]{1,0:T(8,128)S(1)}, f32[108,128]{1,0:T(8,128)S(1)}, u32[]{:S(2)}, u32[]{:S(2)}) collective-permute-start(f32[108,128]{1,0:T(8,128)S(1)} %add_add_fusion.8), channel_id=1, source_target_pairs={{0,8},{8,0},{1,9},{9,1},{2,10},{10,2},{3,11},{11,3},{4,12},{12,4},... | collective-permute-start | bytes 165896 | tf_op jit(solution)/shard_map/ppermute | solution.py:45
  (629 shorter events, 239.8 us)
Async XLA Ops:
  8.4 29.0 %collective-permute-start.5 = (bf16[1024,512]{1,0:T(8,128)(2,1)}, bf16[1024,512]{1,0:T(8,128)(2,1)}, u32[]{:S(2)}, u32[]{:S(2)}) collective-permute-start(bf16[1024,512]{1,0:T(8,128)(2,1)} %get-tuple-element.348), channel_id=1, source_target_pairs={{0,4},{8,0},{4,12},{12,72},{64,68},{72,64},{68,76},{76,8},{1,5},{9... | collective-permute-start | bytes 3145736 | tf_op jit(solution)/shard_map/ppermute | solution.py:66
  10.8 27.0 %collective-permute-start.6 = (bf16[1024,384]{0,1:T(8,128)(2,1)}, bf16[1024,384]{0,1:T(8,128)(2,1)}, u32[]{:S(2)}, u32[]{:S(2)}) collective-permute-start(bf16[1024,384]{0,1:T(8,128)(2,1)} %bitcast.13), channel_id=1, source_target_pairs={{0,68},{8,0},{4,12},{12,8},{64,4},{72,64},{68,76},{76,72},{1,69},{... | collective-permute-start | bytes 2359304 | tf_op jit(solution)/shard_map/ppermute | solution.py:66
  15.6 12.1 %collective-permute-start.2 = (bf16[128,1024]{1,0:T(8,128)(2,1)S(1)}, bf16[128,1024]{1,0:T(8,128)(2,1)S(1)}, u32[]{:S(2)}, u32[]{:S(2)}) collective-permute-start(bf16[128,1024]{1,0:T(8,128)(2,1)S(1)} %fusion.19), channel_id=1, source_target_pairs={{0,3},{1,0},{2,1},{3,2},{4,7},{5,4},{6,5},{7,6},{8,11},{9,8},{10,9... | collective-permute-start | bytes 786440 | tf_op jit(solution)/shard_map/ppermute | solution.py:41
  16.0 16.9 %collective-permute-start.1 = (bf16[128,1024]{1,0:T(8,128)(2,1)S(1)}, bf16[128,1024]{1,0:T(8,128)(2,1)S(1)}, u32[]{:S(2)}, u32[]{:S(2)}) collective-permute-start(bf16[128,1024]{1,0:T(8,128)(2,1)S(1)} %fusion.19), channel_id=1, source_target_pairs={{0,1},{1,2},{2,3},{3,0},{4,5},{5,6},{6,7},{7,4},{8,9},{9,10},{10,1... | collective-permute-start | bytes 786440 | tf_op jit(solution)/shard_map/ppermute | solution.py:41
  20.6 13.7 %collective-permute-start.7 = (f32[12,128]{1,0:T(8,128)S(1)}, f32[12,128]{1,0:T(8,128)S(1)}, u32[]{:S(2)}, u32[]{:S(2)}) collective-permute-start(f32[12,128]{1,0:T(8,128)S(1)} %pad_maximum_fusion.14), channel_id=1, source_target_pairs={{0,4},{8,0},{4,12},{12,72},{64,68},{72,64},{68,76},{76,8},{1,5},{9... | collective-permute-start | bytes 18440 | tf_op jit(solution)/shard_map/ppermute | solution.py:66
  34.3 14.6 %collective-permute-start.10 = (bf16[512,1024]{1,0:T(8,128)(2,1)}, bf16[512,1024]{1,0:T(8,128)(2,1)S(1)}, u32[]{:S(2)}, u32[]{:S(2)}) collective-permute-start(bf16[512,1024]{1,0:T(8,128)(2,1)} %get-tuple-element.346), channel_id=1, source_target_pairs={{0,68},{8,0},{4,12},{12,8},{64,4},{72,64},{68,76},{76,72},{1,69},{... | collective-permute-start | bytes 3145736 | tf_op jit(solution)/shard_map/ppermute | solution.py:66
  35.9 13.0 %collective-permute-start.11 = (bf16[128,1024]{1,0:T(8,128)(2,1)S(1)}, bf16[128,1024]{1,0:T(8,128)(2,1)S(1)}, u32[]{:S(2)}, u32[]{:S(2)}) collective-permute-start(bf16[128,1024]{1,0:T(8,128)(2,1)S(1)} %get-tuple-element.392), channel_id=1, source_target_pairs={{0,4},{8,0},{4,12},{12,72},{64,68},{72,64},{68,76},{76,8},{1,5},{9... | collective-permute-start | bytes 786440 | tf_op jit(solution)/shard_map/ppermute | solution.py:66
  57.7 12.6 %collective-permute-start.14 = (bf16[128,1024]{1,0:T(8,128)(2,1)}, bf16[128,1024]{1,0:T(8,128)(2,1)S(1)}, u32[]{:S(2)}, u32[]{:S(2)}) collective-permute-start(bf16[128,1024]{1,0:T(8,128)(2,1)} %get-tuple-element.380), channel_id=1, source_target_pairs={{0,1},{1,2},{2,3},{3,0},{4,5},{5,6},{6,7},{7,4},{8,9},{9,10},{10,1... | collective-permute-start | bytes 786440 | tf_op jit(solution)/shard_map/ppermute | solution.py:41
  57.7 12.6 %collective-permute-start.13 = (bf16[128,1024]{1,0:T(8,128)(2,1)S(1)}, bf16[128,1024]{1,0:T(8,128)(2,1)S(1)}, u32[]{:S(2)}, u32[]{:S(2)}) collective-permute-start(bf16[128,1024]{1,0:T(8,128)(2,1)S(1)} %get-tuple-element.378), channel_id=1, source_target_pairs={{0,3},{1,0},{2,1},{3,2},{4,7},{5,4},{6,5},{7,6},{8,11},{9,8},{10,9... | collective-permute-start | bytes 786440 | tf_op jit(solution)/shard_map/ppermute | solution.py:41
  62.7 24.8 %collective-permute-start.19 = (bf16[1024,384]{0,1:T(8,128)(2,1)}, bf16[1024,384]{0,1:T(8,128)(2,1)S(1)}, u32[]{:S(2)}, u32[]{:S(2)}) collective-permute-start(bf16[1024,384]{0,1:T(8,128)(2,1)} %bitcast.23), channel_id=1, source_target_pairs={{0,68},{8,0},{4,12},{12,8},{64,4},{72,64},{68,76},{76,72},{1,69},{... | collective-permute-start | bytes 2359304 | tf_op jit(solution)/shard_map/ppermute | solution.py:66
  73.3 13.4 %collective-permute-start.17 = (bf16[128,1024]{1,0:T(8,128)(2,1)S(1)}, bf16[128,1024]{1,0:T(8,128)(2,1)S(1)}, u32[]{:S(2)}, u32[]{:S(2)}) collective-permute-start(bf16[128,1024]{1,0:T(8,128)(2,1)S(1)} %add_convert_fusion.6), channel_id=1, source_target_pairs={{0,3},{1,0},{2,1},{3,2},{4,7},{5,4},{6,5},{7,6},{8,11},{9,8},{10,9... | collective-permute-start | bytes 786440 | tf_op jit(solution)/shard_map/ppermute | solution.py:41
  75.4 12.0 %collective-permute-start.16 = (bf16[128,1024]{1,0:T(8,128)(2,1)S(1)}, bf16[128,1024]{1,0:T(8,128)(2,1)S(1)}, u32[]{:S(2)}, u32[]{:S(2)}) collective-permute-start(bf16[128,1024]{1,0:T(8,128)(2,1)S(1)} %add_convert_fusion.6), channel_id=1, source_target_pairs={{0,1},{1,2},{2,3},{3,0},{4,5},{5,6},{6,7},{7,4},{8,9},{9,10},{10,1... | collective-permute-start | bytes 786440 | tf_op jit(solution)/shard_map/ppermute | solution.py:41
  75.4 12.1 %collective-permute-start.20 = (bf16[128,1024]{1,0:T(8,128)(2,1)S(1)}, bf16[128,1024]{1,0:T(8,128)(2,1)S(1)}, u32[]{:S(2)}, u32[]{:S(2)}) collective-permute-start(bf16[128,1024]{1,0:T(8,128)(2,1)S(1)} %copy-done.74), channel_id=1, source_target_pairs={{0,4},{8,0},{4,12},{12,72},{64,68},{72,64},{68,76},{76,8},{1,5},{9... | collective-permute-start | bytes 786440 | tf_op jit(solution)/shard_map/ppermute | solution.py:66
  103.0 13.4 %collective-permute-start.25 = (bf16[128,1024]{1,0:T(8,128)(2,1)S(1)}, bf16[128,1024]{1,0:T(8,128)(2,1)S(1)}, u32[]{:S(2)}, u32[]{:S(2)}) collective-permute-start(bf16[128,1024]{1,0:T(8,128)(2,1)S(1)} %get-tuple-element.377), channel_id=1, source_target_pairs={{0,1},{1,2},{2,3},{3,0},{4,5},{5,6},{6,7},{7,4},{8,9},{9,10},{10,1... | collective-permute-start | bytes 786440 | tf_op jit(solution)/shard_map/ppermute | solution.py:41
  105.7 27.2 %collective-permute-start.30 = (bf16[1024,512]{1,0:T(8,128)(2,1)S(1)}, bf16[1024,512]{1,0:T(8,128)(2,1)S(1)}, u32[]{:S(2)}, u32[]{:S(2)}) collective-permute-start(bf16[1024,512]{1,0:T(8,128)(2,1)S(1)} %copy-done.54), channel_id=1, source_target_pairs={{0,4},{8,0},{4,12},{12,72},{64,68},{72,64},{68,76},{76,8},{1,5},{9... | collective-permute-start | bytes 3145736 | tf_op jit(solution)/shard_map/ppermute | solution.py:66
  106.9 26.0 %collective-permute-start.31 = (bf16[512,1024]{1,0:T(8,128)(2,1)S(1)}, bf16[512,1024]{1,0:T(8,128)(2,1)S(1)}, u32[]{:S(2)}, u32[]{:S(2)}) collective-permute-start(bf16[512,1024]{1,0:T(8,128)(2,1)S(1)} %copy-done.55), channel_id=1, source_target_pairs={{0,68},{8,0},{4,12},{12,8},{64,4},{72,64},{68,76},{76,72},{1,69},{... | collective-permute-start | bytes 3145736 | tf_op jit(solution)/shard_map/ppermute | solution.py:66
  119.1 13.6 %collective-permute-start.28 = (bf16[128,1024]{1,0:T(8,128)(2,1)S(1)}, bf16[128,1024]{1,0:T(8,128)(2,1)S(1)}, u32[]{:S(2)}, u32[]{:S(2)}) collective-permute-start(bf16[128,1024]{1,0:T(8,128)(2,1)S(1)} %add_convert_fusion.5), channel_id=1, source_target_pairs={{0,3},{1,0},{2,1},{3,2},{4,7},{5,4},{6,5},{7,6},{8,11},{9,8},{10,9... | collective-permute-start | bytes 786440 | tf_op jit(solution)/shard_map/ppermute | solution.py:41
  120.7 12.1 %collective-permute-start.27 = (bf16[128,1024]{1,0:T(8,128)(2,1)S(1)}, bf16[128,1024]{1,0:T(8,128)(2,1)S(1)}, u32[]{:S(2)}, u32[]{:S(2)}) collective-permute-start(bf16[128,1024]{1,0:T(8,128)(2,1)S(1)} %add_convert_fusion.5), channel_id=1, source_target_pairs={{0,1},{1,2},{2,3},{3,0},{4,5},{5,6},{6,7},{7,4},{8,9},{9,10},{10,1... | collective-permute-start | bytes 786440 | tf_op jit(solution)/shard_map/ppermute | solution.py:41
  136.7 11.9 %collective-permute-start.33 = (bf16[128,1024]{1,0:T(8,128)(2,1)S(1)}, bf16[128,1024]{1,0:T(8,128)(2,1)S(1)}, u32[]{:S(2)}, u32[]{:S(2)}) collective-permute-start(bf16[128,1024]{1,0:T(8,128)(2,1)S(1)} %collective-permute-done.8), channel_id=1, source_target_pairs={{0,2},{1,3},{2,0},{3,1},{4,6},{5,7},{6,4},{7,5},{8,10},{9,11},{10,... | collective-permute-start | bytes 786440 | tf_op jit(solution)/shard_map/ppermute | solution.py:41
  154.7 13.2 %collective-permute-start.36 = (bf16[128,1024]{1,0:T(8,128)(2,1)S(1)}, bf16[128,1024]{1,0:T(8,128)(2,1)S(1)}, u32[]{:S(2)}, u32[]{:S(2)}) collective-permute-start(bf16[128,1024]{1,0:T(8,128)(2,1)S(1)} %get-tuple-element.374), channel_id=1, source_target_pairs={{0,1},{1,2},{2,3},{3,0},{4,5},{5,6},{6,7},{7,4},{8,9},{9,10},{10,1... | collective-permute-start | bytes 786440 | tf_op jit(solution)/shard_map/ppermute | solution.py:41
  154.7 13.2 %collective-permute-start.35 = (bf16[128,1024]{1,0:T(8,128)(2,1)S(1)}, bf16[128,1024]{1,0:T(8,128)(2,1)S(1)}, u32[]{:S(2)}, u32[]{:S(2)}) collective-permute-start(bf16[128,1024]{1,0:T(8,128)(2,1)S(1)} %get-tuple-element.372), channel_id=1, source_target_pairs={{0,3},{1,0},{2,1},{3,2},{4,7},{5,4},{6,5},{7,6},{8,11},{9,8},{10,9... | collective-permute-start | bytes 786440 | tf_op jit(solution)/shard_map/ppermute | solution.py:41
  203.5 12.8 %collective-permute-start.45 = (bf16[128,1024]{1,0:T(8,128)(2,1)S(1)}, bf16[128,1024]{1,0:T(8,128)(2,1)S(1)}, u32[]{:S(2)}, u32[]{:S(2)}) collective-permute-start(bf16[128,1024]{1,0:T(8,128)(2,1)S(1)} %get-tuple-element.371), channel_id=1, source_target_pairs={{0,1},{1,2},{2,3},{3,0},{4,5},{5,6},{6,7},{7,4},{8,9},{9,10},{10,1... | collective-permute-start | bytes 786440 | tf_op jit(solution)/shard_map/ppermute | solution.py:41
  203.5 12.8 %collective-permute-start.44 = (bf16[128,1024]{1,0:T(8,128)(2,1)S(1)}, bf16[128,1024]{1,0:T(8,128)(2,1)S(1)}, u32[]{:S(2)}, u32[]{:S(2)}) collective-permute-start(bf16[128,1024]{1,0:T(8,128)(2,1)S(1)} %get-tuple-element.369), channel_id=1, source_target_pairs={{0,3},{1,0},{2,1},{3,2},{4,7},{5,4},{6,5},{7,6},{8,11},{9,8},{10,9... | collective-permute-start | bytes 786440 | tf_op jit(solution)/shard_map/ppermute | solution.py:41
  217.6 18.4 %collective-permute-start.50 = (bf16[2,128,1024]{2,1,0:T(8,128)(2,1)S(1)}, bf16[2,128,1024]{2,1,0:T(8,128)(2,1)S(1)}, u32[]{:S(2)}, u32[]{:S(2)}) collective-permute-start(bf16[2,128,1024]{2,1,0:T(8,128)(2,1)S(1)} %get-tuple-element.187), channel_id=1, source_target_pairs={{0,16},{16,32},{32,48},{48,0},{1,17},{17,33},{33,49},{49,1},{2,18}... | collective-permute-start | bytes 1572872 | tf_op jit(solution)/shard_map/ppermute | solution.py:41
  218.9 17.1 %collective-permute-start.51 = (bf16[2,128,1024]{2,1,0:T(8,128)(2,1)S(1)}, bf16[2,128,1024]{2,1,0:T(8,128)(2,1)S(1)}, u32[]{:S(2)}, u32[]{:S(2)}) collective-permute-start(bf16[2,128,1024]{2,1,0:T(8,128)(2,1)S(1)} %get-tuple-element.188), channel_id=1, source_target_pairs={{0,48},{16,0},{32,16},{48,32},{1,49},{17,1},{33,17},{49,33},{2,50}... | collective-permute-start | bytes 1572872 | tf_op jit(solution)/shard_map/ppermute | solution.py:41
  221.6 12.8 %collective-permute-start.48 = (bf16[128,1024]{1,0:T(8,128)(2,1)S(1)}, bf16[128,1024]{1,0:T(8,128)(2,1)S(1)}, u32[]{:S(2)}, u32[]{:S(2)}) collective-permute-start(bf16[128,1024]{1,0:T(8,128)(2,1)S(1)} %get-tuple-element.329), channel_id=1, source_target_pairs={{0,3},{1,0},{2,1},{3,2},{4,7},{5,4},{6,5},{7,6},{8,11},{9,8},{10,9... | collective-permute-start | bytes 786440 | tf_op jit(solution)/shard_map/ppermute | solution.py:41
  240.7 18.2 %collective-permute-start.56 = (bf16[2,128,1024]{2,1,0:T(8,128)(2,1)S(1)}, bf16[2,128,1024]{2,1,0:T(8,128)(2,1)S(1)}, u32[]{:S(2)}, u32[]{:S(2)}) collective-permute-start(bf16[2,128,1024]{2,1,0:T(8,128)(2,1)S(1)} %get-tuple-element.196), channel_id=1, source_target_pairs={{0,32},{16,48},{32,0},{48,16},{1,33},{17,49},{33,1},{49,17},{2,34}... | collective-permute-start | bytes 1572872 | tf_op jit(solution)/shard_map/ppermute | solution.py:41
  244.5 13.6 %collective-permute-start.55 = (bf16[128,1024]{1,0:T(8,128)(2,1)S(1)}, bf16[128,1024]{1,0:T(8,128)(2,1)S(1)}, u32[]{:S(2)}, u32[]{:S(2)}) collective-permute-start(bf16[128,1024]{1,0:T(8,128)(2,1)S(1)} %get-tuple-element.367), channel_id=1, source_target_pairs={{0,1},{1,2},{2,3},{3,0},{4,5},{5,6},{6,7},{7,4},{8,9},{9,10},{10,1... | collective-permute-start | bytes 786440 | tf_op jit(solution)/shard_map/ppermute | solution.py:41
  245.0 13.1 %collective-permute-start.54 = (bf16[128,1024]{1,0:T(8,128)(2,1)S(1)}, bf16[128,1024]{1,0:T(8,128)(2,1)S(1)}, u32[]{:S(2)}, u32[]{:S(2)}) collective-permute-start(bf16[128,1024]{1,0:T(8,128)(2,1)S(1)} %get-tuple-element.368), channel_id=1, source_target_pairs={{0,3},{1,0},{2,1},{3,2},{4,7},{5,4},{6,5},{7,6},{8,11},{9,8},{10,9... | collective-permute-start | bytes 786440 | tf_op jit(solution)/shard_map/ppermute | solution.py:41
  272.4 14.9 %collective-permute-start.59 = (bf16[128,1024]{1,0:T(8,128)(2,1)S(1)}, bf16[128,1024]{1,0:T(8,128)(2,1)S(1)}, u32[]{:S(2)}, u32[]{:S(2)}) collective-permute-start(bf16[128,1024]{1,0:T(8,128)(2,1)S(1)} %get-tuple-element.365), channel_id=1, source_target_pairs={{0,1},{1,2},{2,3},{3,0},{4,5},{5,6},{6,7},{7,4},{8,9},{9,10},{10,1... | collective-permute-start | bytes 786440 | tf_op jit(solution)/shard_map/ppermute | solution.py:41
  273.1 14.2 %collective-permute-start.58 = (bf16[128,1024]{1,0:T(8,128)(2,1)S(1)}, bf16[128,1024]{1,0:T(8,128)(2,1)S(1)}, u32[]{:S(2)}, u32[]{:S(2)}) collective-permute-start(bf16[128,1024]{1,0:T(8,128)(2,1)S(1)} %get-tuple-element.363), channel_id=1, source_target_pairs={{0,3},{1,0},{2,1},{3,2},{4,7},{5,4},{6,5},{7,6},{8,11},{9,8},{10,9... | collective-permute-start | bytes 786440 | tf_op jit(solution)/shard_map/ppermute | solution.py:41
  290.6 12.1 %collective-permute-start.65 = (bf16[128,1024]{1,0:T(8,128)(2,1)S(1)}, bf16[128,1024]{1,0:T(8,128)(2,1)S(1)}, u32[]{:S(2)}, u32[]{:S(2)}) collective-permute-start(bf16[128,1024]{1,0:T(8,128)(2,1)S(1)} %get-tuple-element.326), channel_id=1, source_target_pairs={{0,3},{1,0},{2,1},{3,2},{4,7},{5,4},{6,5},{7,6},{8,11},{9,8},{10,9... | collective-permute-start | bytes 786440 | tf_op jit(solution)/shard_map/ppermute | solution.py:41
  292.2 13.3 %collective-permute-start.64 = (bf16[128,1024]{1,0:T(8,128)(2,1)S(1)}, bf16[128,1024]{1,0:T(8,128)(2,1)S(1)}, u32[]{:S(2)}, u32[]{:S(2)}) collective-permute-start(bf16[128,1024]{1,0:T(8,128)(2,1)S(1)} %get-tuple-element.326), channel_id=1, source_target_pairs={{0,1},{1,2},{2,3},{3,0},{4,5},{5,6},{6,7},{7,4},{8,9},{9,10},{10,1... | collective-permute-start | bytes 786440 | tf_op jit(solution)/shard_map/ppermute | solution.py:41
  292.2 13.4 %collective-permute-start.67 = (bf16[2,128,512]{2,1,0:T(8,128)(2,1)S(1)}, bf16[2,128,512]{2,1,0:T(8,128)(2,1)S(1)}, u32[]{:S(2)}, u32[]{:S(2)}) collective-permute-start(bf16[2,128,512]{2,1,0:T(8,128)(2,1)S(1)} %get-tuple-element.216), channel_id=1, source_target_pairs={{0,16},{16,32},{32,48},{48,0},{1,17},{17,33},{33,49},{49,1},{2,18}... | collective-permute-start | bytes 786440 | tf_op jit(solution)/shard_map/ppermute | solution.py:41
  292.2 13.4 %collective-permute-start.68 = (bf16[2,128,512]{2,1,0:T(8,128)(2,1)S(1)}, bf16[2,128,512]{2,1,0:T(8,128)(2,1)S(1)}, u32[]{:S(2)}, u32[]{:S(2)}) collective-permute-start(bf16[2,128,512]{2,1,0:T(8,128)(2,1)S(1)} %get-tuple-element.217), channel_id=1, source_target_pairs={{0,48},{16,0},{32,16},{48,32},{1,49},{17,1},{33,17},{49,33},{2,50}... | collective-permute-start | bytes 786440 | tf_op jit(solution)/shard_map/ppermute | solution.py:41
  325.2 26.5 %collective-permute-start.114 = (f32[64,1024]{1,0:T(8,128)}, f32[64,1024]{1,0:T(8,128)S(1)}, u32[]{:S(2)}, u32[]{:S(2)}) collective-permute-start(f32[64,1024]{1,0:T(8,128)} %get-tuple-element.297), channel_id=1, source_target_pairs={{0,8},{12,4},{1,9},{13,5},{2,10},{14,6},{3,11},{15,7},{16,24},{28,... | collective-permute-start | bytes 786440 | tf_op jit(solution)/shard_map/ppermute | solution.py:205
  333.0 12.7 %collective-permute-start.78 = (bf16[128,1024]{1,0:T(8,128)(2,1)S(1)}, bf16[128,1024]{1,0:T(8,128)(2,1)S(1)}, u32[]{:S(2)}, u32[]{:S(2)}) collective-permute-start(bf16[128,1024]{1,0:T(8,128)(2,1)S(1)} %get-tuple-element.359), channel_id=1, source_target_pairs={{0,1},{1,2},{2,3},{3,0},{4,5},{5,6},{6,7},{7,4},{8,9},{9,10},{10,1... | collective-permute-start | bytes 786440 | tf_op jit(solution)/shard_map/ppermute | solution.py:41
  333.0 12.7 %collective-permute-start.77 = (bf16[128,1024]{1,0:T(8,128)(2,1)S(1)}, bf16[128,1024]{1,0:T(8,128)(2,1)S(1)}, u32[]{:S(2)}, u32[]{:S(2)}) collective-permute-start(bf16[128,1024]{1,0:T(8,128)(2,1)S(1)} %get-tuple-element.357), channel_id=1, source_target_pairs={{0,3},{1,0},{2,1},{3,2},{4,7},{5,4},{6,5},{7,6},{8,11},{9,8},{10,9... | collective-permute-start | bytes 786440 | tf_op jit(solution)/shard_map/ppermute | solution.py:41
  348.6 12.9 %collective-permute-start.81 = (bf16[128,1024]{1,0:T(8,128)(2,1)S(1)}, bf16[128,1024]{1,0:T(8,128)(2,1)S(1)}, u32[]{:S(2)}, u32[]{:S(2)}) collective-permute-start(bf16[128,1024]{1,0:T(8,128)(2,1)S(1)} %get-tuple-element.331), channel_id=1, source_target_pairs={{0,3},{1,0},{2,1},{3,2},{4,7},{5,4},{6,5},{7,6},{8,11},{9,8},{10,9... | collective-permute-start | bytes 786440 | tf_op jit(solution)/shard_map/ppermute | solution.py:41
  351.0 12.1 %collective-permute-start.80 = (bf16[128,1024]{1,0:T(8,128)(2,1)S(1)}, bf16[128,1024]{1,0:T(8,128)(2,1)S(1)}, u32[]{:S(2)}, u32[]{:S(2)}) collective-permute-start(bf16[128,1024]{1,0:T(8,128)(2,1)S(1)} %get-tuple-element.331), channel_id=1, source_target_pairs={{0,1},{1,2},{2,3},{3,0},{4,5},{5,6},{6,7},{7,4},{8,9},{9,10},{10,1... | collective-permute-start | bytes 786440 | tf_op jit(solution)/shard_map/ppermute | solution.py:41
  351.0 13.4 %collective-permute-start.83 = (bf16[2,128,1024]{2,1,0:T(8,128)(2,1)S(1)}, bf16[2,128,1024]{2,1,0:T(8,128)(2,1)S(1)}, u32[]{:S(2)}, u32[]{:S(2)}) collective-permute-start(bf16[2,128,1024]{2,1,0:T(8,128)(2,1)S(1)} %get-tuple-element.248), channel_id=1, source_target_pairs={{0,16},{16,32},{32,48},{48,0},{1,17},{17,33},{33,49},{49,1},{2,18}... | collective-permute-start | bytes 1572872 | tf_op jit(solution)/shard_map/ppermute | solution.py:41
  351.7 12.8 %collective-permute-start.84 = (bf16[2,128,1024]{2,1,0:T(8,128)(2,1)S(1)}, bf16[2,128,1024]{2,1,0:T(8,128)(2,1)S(1)}, u32[]{:S(2)}, u32[]{:S(2)}) collective-permute-start(bf16[2,128,1024]{2,1,0:T(8,128)(2,1)S(1)} %get-tuple-element.249), channel_id=1, source_target_pairs={{0,48},{16,0},{32,16},{48,32},{1,49},{17,1},{33,17},{49,33},{2,50}... | collective-permute-start | bytes 1572872 | tf_op jit(solution)/shard_map/ppermute | solution.py:41
  364.4 15.8 %collective-permute-start.85 = (bf16[512,1024]{1,0:T(8,128)(2,1)}, bf16[512,1024]{1,0:T(8,128)(2,1)}, u32[]{:S(2)}, u32[]{:S(2)}) collective-permute-start(bf16[512,1024]{1,0:T(8,128)(2,1)} %pad_maximum_fusion.9), channel_id=1, source_target_pairs={{0,8},{8,0},{1,9},{9,1},{2,10},{10,2},{3,11},{11,3},{4,12},{12,4},... | collective-permute-start | bytes 3145736 | tf_op jit(solution)/shard_map/ppermute | solution.py:45
  375.4 17.0 %collective-permute-start.86 = (bf16[2,128,1024]{2,1,0:T(8,128)(2,1)}, bf16[2,128,1024]{2,1,0:T(8,128)(2,1)}, u32[]{:S(2)}, u32[]{:S(2)}) collective-permute-start(bf16[2,128,1024]{2,1,0:T(8,128)(2,1)} %get-tuple-element.254), channel_id=1, source_target_pairs={{0,32},{16,48},{32,0},{48,16},{1,33},{17,49},{33,1},{49,17},{2,34}... | collective-permute-start | bytes 1572872 | tf_op jit(solution)/shard_map/ppermute | solution.py:41
  405.3 13.8 %collective-permute-start.89 = (bf16[128,1024]{1,0:T(8,128)(2,1)S(1)}, bf16[128,1024]{1,0:T(8,128)(2,1)S(1)}, u32[]{:S(2)}, u32[]{:S(2)}) collective-permute-start(bf16[128,1024]{1,0:T(8,128)(2,1)S(1)} %get-tuple-element.356), channel_id=1, source_target_pairs={{0,1},{1,2},{2,3},{3,0},{4,5},{5,6},{6,7},{7,4},{8,9},{9,10},{10,1... | collective-permute-start | bytes 786440 | tf_op jit(solution)/shard_map/ppermute | solution.py:41
  407.0 12.1 %collective-permute-start.88 = (bf16[128,1024]{1,0:T(8,128)(2,1)S(1)}, bf16[128,1024]{1,0:T(8,128)(2,1)S(1)}, u32[]{:S(2)}, u32[]{:S(2)}) collective-permute-start(bf16[128,1024]{1,0:T(8,128)(2,1)S(1)} %get-tuple-element.354), channel_id=1, source_target_pairs={{0,3},{1,0},{2,1},{3,2},{4,7},{5,4},{6,5},{7,6},{8,11},{9,8},{10,9... | collective-permute-start | bytes 786440 | tf_op jit(solution)/shard_map/ppermute | solution.py:41
  426.8 15.4 %collective-permute-start.113 = (f32[64,1024]{1,0:T(8,128)S(1)}, f32[64,1024]{1,0:T(8,128)}, u32[]{:S(2)}, u32[]{:S(2)}) collective-permute-start(f32[64,1024]{1,0:T(8,128)S(1)} %get-tuple-element.295), channel_id=1, source_target_pairs={{0,8},{12,4},{1,9},{13,5},{2,10},{14,6},{3,11},{15,7},{16,24},{28,... | collective-permute-start | bytes 786440 | tf_op jit(solution)/shard_map/ppermute | solution.py:205
  429.1 15.6 %collective-permute-start.94 = (bf16[128,1024]{1,0:T(8,128)(2,1)}, bf16[128,1024]{1,0:T(8,128)(2,1)S(1)}, u32[]{:S(2)}, u32[]{:S(2)}) collective-permute-start(bf16[128,1024]{1,0:T(8,128)(2,1)} %add_convert_fusion.2), channel_id=1, source_target_pairs={{0,0},{4,8},{8,4},{12,12},{1,1},{5,9},{9,5},{13,13},{2,2},{6,10},{... | collective-permute-start | bytes 786440 | tf_op jit(solution)/shard_map/ppermute | solution.py:49
  (188 other events, 2097.5 us)

commit v5 on v4

--- a/solution.py
+++ b/solution.py
@@ -222,113 +222,176 @@
     return values[:rows] + other[:rows], jnp.where(own, values[rows:], other[rows:]), state
 
 
-def row_places():
+def block_slots():
     core, z = lax.axis_index("c"), lax.axis_index("z")
-    blocks = jnp.stack([cc * 4 + (z + dz) % 4 for cc in (core, 1 - core) for dz in (0, 3, 1, 2)])
-    return (blocks[:, None] * 128 + lax.iota(jnp.int32, 128)[None, :]).reshape(-1)
-
-
+    blocks = lax.iota(jnp.int32, 8)
+    turn = (blocks % 4 - z + 4) % 4
+    order = jnp.where(turn == 0, 0, jnp.where(turn == 3, 1, turn + 1))
+    return (jnp.where(blocks // 4 == core, 0, 4) + order).astype(jnp.int32)
+
+
+BLOCK = 128
 QUERY_ROWS = 256
 VMEM_BYTES = 32 * 1024 * 1024
 
 
-def attend_forward_kernel(query_place, key_place, q_ref, k_ref, v_ref, out_ref, log_ref):
-    mask = query_place[...] >= key_place[...]
-    for head in range(q_ref.shape[1] // HEAD_DIM):
-        cut = slice(head * HEAD_DIM, (head + 1) * HEAD_DIM)
-        scores = against_rows(k_ref[:, cut], q_ref[:, cut] * HEAD_DIM ** (-0.5))
-        scores = jnp.where(mask, scores, NEG_FILL)
-        peak = jnp.max(scores, 0, keepdims=True)
-        weights = jnp.exp(scores - peak)
-        total = jnp.sum(weights, 0, keepdims=True)
-        weights = (weights * (1.0 / total)).astype(BF)
-        out_ref[:, cut] = tokens_inner(v_ref[:, cut], weights).T.astype(BF)
-        log_ref[head : head + 1, :] = peak + jnp.log(total)
-
-
-def attend_forward(qkv, places):
+def slot_rows(slots, block):
+    return pl.ds(pl.multiple_of(slots[block] * BLOCK, BLOCK), BLOCK)
+
+
+def masked_scores(keys, queries):
+    scores = against_rows(keys, queries)
+    count = queries.shape[0]
+    shape = (count, count)
+    mask = lax.broadcasted_iota(jnp.int32, shape, 1) >= lax.broadcasted_iota(jnp.int32, shape, 0)
+    diagonal = jnp.where(mask, scores[-count:], NEG_FILL)
+    if keys.shape[0] == count:
+        return diagonal
+    return jnp.concatenate([scores[:-count], diagonal])
+
+
+def attend_forward_kernel(slots, low_ref, high_ref, k_ref, v_ref, out_ref, log_ref, k_all, v_all):
+    step = pl.program_id(0)
+
+    @pl.when(step == 0)
+    def _():
+        for block in range(8):
+            k_all[block * BLOCK : (block + 1) * BLOCK, :] = k_ref[slot_rows(slots, block), :]
+            v_all[block * BLOCK : (block + 1) * BLOCK, :] = v_ref[slot_rows(slots, block), :]
+
+    for part in range(k_ref.shape[0] // QUERY_ROWS):
+
+        @pl.when(step == part)
+        def _():
+            end = (part + 1) * QUERY_ROWS
+            queries = jnp.concatenate([low_ref[...], high_ref[...]]) * HEAD_DIM ** (-0.5)
+            for head in range(k_ref.shape[1] // HEAD_DIM):
+                cut = slice(head * HEAD_DIM, (head + 1) * HEAD_DIM)
+                scores = masked_scores(k_all[:end, cut], queries[:, cut])
+                peak = jnp.max(scores, 0, keepdims=True)
+                weights = jnp.exp(scores - peak)
+                total = jnp.sum(weights, 0, keepdims=True)
+                weights = (weights * (1.0 / total)).astype(BF)
+                mixed = tokens_inner(v_all[:end, cut], weights).T.astype(BF)
+                out_ref[slot_rows(slots, 2 * part), cut] = mixed[:BLOCK]
+                out_ref[slot_rows(slots, 2 * part + 1), cut] = mixed[BLOCK:]
+                log_ref[head : head + 1, :] = peak + jnp.log(total)
+
+
+def query_specs(width):
+    return [
+        pl.BlockSpec((BLOCK, width), lambda i, s: (s[2 * i], 0)),
+        pl.BlockSpec((BLOCK, width), lambda i, s: (s[2 * i + 1], 0)),
+    ]
+
+
+def attend_forward(qkv, slots):
     tokens, width = qkv.shape[0], qkv.shape[1] // 3
     heads = width // HEAD_DIM
     return pl.pallas_call(
         attend_forward_kernel,
-        grid=(tokens // QUERY_ROWS,),
-        in_specs=[
-            pl.BlockSpec((1, QUERY_ROWS), lambda i: (0, i)),
-            pl.BlockSpec((tokens, 1), lambda i: (0, 0)),
-            pl.BlockSpec((QUERY_ROWS, width), lambda i: (i, 0)),
-            pl.BlockSpec((tokens, width), lambda i: (0, 1)),
-            pl.BlockSpec((tokens, width), lambda i: (0, 2)),
-        ],
-        out_specs=[
-            pl.BlockSpec((QUERY_ROWS, width), lambda i: (i, 0)),
-            pl.BlockSpec((heads, QUERY_ROWS), lambda i: (0, i)),
-        ],
+        grid_spec=pltpu.PrefetchScalarGridSpec(
+            num_scalar_prefetch=1,
+            grid=(tokens // QUERY_ROWS,),
+            in_specs=query_specs(width)
+            + [
+                pl.BlockSpec((tokens, width), lambda i, s: (0, 1)),
+                pl.BlockSpec((tokens, width), lambda i, s: (0, 2)),
+            ],
+            out_specs=[
+                pl.BlockSpec((tokens, width), lambda i, s: (0, 0)),
+                pl.BlockSpec((heads, QUERY_ROWS), lambda i, s: (0, i)),
+            ],
+            scratch_shapes=[pltpu.VMEM((tokens, width), BF), pltpu.VMEM((tokens, width), BF)],
+        ),
         out_shape=[
             jax.ShapeDtypeStruct((tokens, width), BF),
             jax.ShapeDtypeStruct((heads, tokens), F32),
         ],
         compiler_params=pltpu.CompilerParams(vmem_limit_bytes=VMEM_BYTES),
         cost_estimate=pl.CostEstimate(
-            flops=8 * tokens * tokens * width, bytes_accessed=2 ** 21, transcendentals=tokens * tokens * heads
-        ),
-    )(places[None, :], places[:, None], qkv, qkv, qkv)
+            flops=8 * tokens * tokens * width,
+            bytes_accessed=2 ** 21,
+            transcendentals=tokens * tokens * heads,
+        ),
+    )(slots, qkv, qkv, qkv, qkv)
 
 
 def attend_backward_kernel(
-    query_place, key_place, log_ref, q_ref, k_ref, v_ref, do_ref, out_ref, dk_ref, dv_ref
+    slots, log_ref, low_ref, high_ref, k_ref, v_ref, do_low, do_high, out_ref,
+    k_all, v_all, dk_ref, dv_ref,
 ):
     step = pl.program_id(0)
-    width = q_ref.shape[1]
-    rows = pl.ds(pl.multiple_of(step * QUERY_ROWS, QUERY_ROWS), QUERY_ROWS)
-    mask = query_place[...] >= key_place[...]
+    width = k_ref.shape[1]
     scale = HEAD_DIM ** (-0.5)
 
     @pl.when(step == 0)
     def _():
         dk_ref[...] = jnp.zeros_like(dk_ref)
         dv_ref[...] = jnp.zeros_like(dv_ref)
-
-    for head in range(width // HEAD_DIM):
-        cut = slice(head * HEAD_DIM, (head + 1) * HEAD_DIM)
-        q, k, v, do = q_ref[:, cut] * scale, k_ref[:, cut], v_ref[:, cut], do_ref[:, cut]
-        scores = jnp.where(mask, against_rows(k, q), NEG_FILL)
-        weights = jnp.exp(scores - log_ref[head : head + 1, :])
-        grad_weights = against_rows(v, do)
-        mean = jnp.sum(weights * grad_weights, 0, keepdims=True)
-        grad_scores = (weights * (grad_weights - mean)).astype(BF)
-        out_ref[rows, cut] = (tokens_inner(k, grad_scores).T * scale).astype(BF)
-        dk_ref[:, cut] += jnp.dot(grad_scores, q, preferred_element_type=F32)
-        dv_ref[:, cut] += jnp.dot(weights.astype(BF), do, preferred_element_type=F32)
+        for block in range(8):
+            k_all[block * BLOCK : (block + 1) * BLOCK, :] = k_ref[slot_rows(slots, block), :]
+            v_all[block * BLOCK : (block + 1) * BLOCK, :] = v_ref[slot_rows(slots, block), :]
+
+    for part in range(k_ref.shape[0] // QUERY_ROWS):
+
+        @pl.when(step == part)
+        def _():
+            end = (part + 1) * QUERY_ROWS
+            queries = jnp.concatenate([low_ref[...], high_ref[...]]) * scale
+            grad_out = jnp.concatenate([do_low[...], do_high[...]])
+            for head in range(width // HEAD_DIM):
+                cut = slice(head * HEAD_DIM, (head + 1) * HEAD_DIM)
+                q, k, v, do = queries[:, cut], k_all[:end, cut], v_all[:end, cut], grad_out[:, cut]
+                weights = jnp.exp(masked_scores(k, q) - log_ref[head : head + 1, :])
+                grad_weights = against_rows(v, do)
+                mean = jnp.sum(weights * grad_weights, 0, keepdims=True)
+                grad_scores = (weights * (grad_weights - mean)).astype(BF)
+                dq = (tokens_inner(k, grad_scores).T * scale).astype(BF)
+                out_ref[slot_rows(slots, 2 * part), cut] = dq[:BLOCK]
+                out_ref[slot_rows(slots, 2 * part + 1), cut] = dq[BLOCK:]
+                dk_ref[:end, cut] += jnp.dot(grad_scores, q, preferred_element_type=F32)
+                dv_ref[:end, cut] += jnp.dot(weights.astype(BF), do, preferred_element_type=F32)
 
     @pl.when(step == pl.num_programs(0) - 1)
     def _():
-        out_ref[:, width : 2 * width] = dk_ref[...].astype(BF)
-        out_ref[:, 2 * width :] = dv_ref[...].astype(BF)
-
-
-def attend_backward(qkv, grad_out, log_totals, places):
+        for block in range(8):
+            rows = slice(block * BLOCK, (block + 1) * BLOCK)
+            out_ref[slot_rows(slots, block), width : 2 * width] = dk_ref[rows, :].astype(BF)
+            out_ref[slot_rows(slots, block), 2 * width :] = dv_ref[rows, :].astype(BF)
+
+
+def attend_backward(qkv, grad_out, log_totals, slots):
     tokens, width = qkv.shape[0], qkv.shape[1] // 3
     heads = width // HEAD_DIM
     return pl.pallas_call(
         attend_backward_kernel,
-        grid=(tokens // QUERY_ROWS,),
-        in_specs=[
-            pl.BlockSpec((1, QUERY_ROWS), lambda i: (0, i)),
-            pl.BlockSpec((tokens, 1), lambda i: (0, 0)),
-            pl.BlockSpec((heads, QUERY_ROWS), lambda i: (0, i)),
-            pl.BlockSpec((QUERY_ROWS, width), lambda i: (i, 0)),
-            pl.BlockSpec((tokens, width), lambda i: (0, 1)),
-            pl.BlockSpec((tokens, width), lambda i: (0, 2)),
-            pl.BlockSpec((QUERY_ROWS, width), lambda i: (i, 0)),
-        ],
-        out_specs=pl.BlockSpec((tokens, 3 * width), lambda i: (0, 0)),
+        grid_spec=pltpu.PrefetchScalarGridSpec(
+            num_scalar_prefetch=1,
+            grid=(tokens // QUERY_ROWS,),
+            in_specs=[pl.BlockSpec((heads, QUERY_ROWS), lambda i, s: (0, i))]
+            + query_specs(width)
+            + [
+                pl.BlockSpec((tokens, width), lambda i, s: (0, 1)),
+                pl.BlockSpec((tokens, width), lambda i, s: (0, 2)),
+            ]
+            + query_specs(width),
+            out_specs=pl.BlockSpec((tokens, 3 * width), lambda i, s: (0, 0)),
+            scratch_shapes=[
+                pltpu.VMEM((tokens, width), BF),
+                pltpu.VMEM((tokens, width), BF),
+                pltpu.VMEM((tokens, width), F32),
+                pltpu.VMEM((tokens, width), F32),
+            ],
+        ),
         out_shape=jax.ShapeDtypeStruct((tokens, 3 * width), BF),
-        scratch_shapes=[pltpu.VMEM((tokens, width), F32), pltpu.VMEM((tokens, width), F32)],
         compiler_params=pltpu.CompilerParams(vmem_limit_bytes=VMEM_BYTES),
         cost_estimate=pl.CostEstimate(
-            flops=20 * tokens * tokens * width, bytes_accessed=2 ** 22, transcendentals=tokens * tokens * heads
-        ),
-    )(places[None, :], places[:, None], log_totals, qkv, qkv, qkv, grad_out)
+            flops=20 * tokens * tokens * width,
+            bytes_accessed=2 ** 22,
+            transcendentals=tokens * tokens * heads,
+        ),
+    )(slots, log_totals, qkv, qkv, qkv, qkv, grad_out, grad_out)
 
 
 def per_device(
@@ -361,7 +424,7 @@
         w_down.append(fetch_weights(shrink[layer], 1))
     cotangent = swap_halves(cotangent)
 
-    places = row_places()
+    slots = block_slots()
     saved = []
     pieces = {}
 
@@ -386,7 +449,7 @@
         qkv = (
             jnp.dot(normed_all, w_in[layer], preferred_element_type=F32) + qkv_bias
         ).astype(BF)
-        attended, log_totals = attend_forward(qkv, places)
+        attended, log_totals = attend_forward(qkv, slots)
         attended, (piece,) = run_beside(
             normed_all, attended, cotangent_task(1 if layer == 0 else 2)
         )
@@ -471,7 +534,7 @@
     dz_mine, near1 = lax.optimization_barrier((dz_mine, mlp1[:3]))
     dz_all = gather_pair(dz_mine)
     do = against_rows(dz_all, w_out[1]).astype(BF)
-    dqkv = attend_backward(qkv, do, log_totals, places)
+    dqkv = attend_backward(qkv, do, log_totals, slots)
 
     def last_pairs(activated):
         both = scatter_pair(activated, times(w_down[1]))
@@ -516,7 +579,7 @@
     dz_mine, near0 = lax.optimization_barrier((dz_mine, mlp0[:3]))
     dz_all = gather_pair(dz_mine)
     do = against_rows(dz_all, w_out[0]).astype(BF)
-    dqkv = attend_backward(qkv, do, log_totals, places)
+    dqkv = attend_backward(qkv, do, log_totals, slots)
     dqkv, mlp0 = lax.optimization_barrier((dqkv, (*near0, mlp0[3])))
     mlp0 = send_y(*add_x(*mlp0))
     grad_first, (attn0, mlp0) = attn_sum(0, dqkv, dz_all, [(add_y, mlp0)])

time: 482 us -> 477 us (0.990)
  waiting for transfers between devices: 141 us -> 153 us
  Pallas kernels: 53.7 us -> 45.5 us
    ppermute x69, waiting for transfers between devices: 115 us -> 127 us  [ring(): lax.ppermute(values, RINGS[axis], [(i, (i + step) % 4) for i in range(4)])]
    pallas_call x4, Pallas kernels: 36.1 us -> 27.9 us  [the longest x2 15 us: attend_backward(): pl.pallas_call(attend_backward_kernel, grid_spec=pltpu.PrefetchScalarGrid...]
    unnamed x265 -> x257, local copies, waits for them, and re-layouts: 10.6 us -> 11.6 us
  transfers between devices with their start and end apart: 115 -> 115, of which waited for: 48 -> 49; matrix products, arithmetic and copies ran while one was open for 14% -> 13% of each run, Pallas kernels for 11% -> 10%
where the time goes in v5:
time: 477 us; the launch traced here: 468 us
  starting transfers between devices  171 us (36%)
  waiting for transfers between devices  153 us (32%)
  Pallas kernels  45.5 us (10%)
  matrix products  37.6 us (8%)
  local copies, waits for them, and re-layouts  28.7 us (6%)
  other arithmetic  28.4 us (6%)
    ppermute x69, waiting for transfers between devices, ring(): lax.ppermute(values, RINGS[axis], [(i, (i + step) % 4) for i in range(4)])  127 us
    ppermute x69, starting transfers between devices, ring(): lax.ppermute(values, RINGS[axis], [(i, (i + step) % 4) for i in range(4)])  96.5 us
    ppermute x17, starting transfers between devices, swap_cores(): return lax.ppermute(values, 'c', [(0, 1), (1, 0)])  23.5 us
    dot_general x12, matrix products, against_rows(): lax.dot_general(left, right, (((1,), (1,)), ((), ())), preferred_element_...  22.9 us
    pallas_call x4, Pallas kernels, grad_blocks(): pl.pallas_call(kernel, grid_spec=pltpu.PrefetchScalarGridSpec(num_scalar_...  17.6 us
    ppermute x17, waiting for transfers between devices, swap_cores(): return lax.ppermute(values, 'c', [(0, 1), (1, 0)])  17.6 us
    ppermute x4, starting transfers between devices, swap_halves(): return lax.ppermute(values, ('c', 'yl'), [(0, 0), (1, 2), (2, 1), (3, 3)])  15.2 us
    pallas_call x2, Pallas kernels, attend_backward(): pl.pallas_call(attend_backward_kernel, grid_spec=pltpu.PrefetchScalarGrid...  15 us
  transfers between devices with their start and end apart: 115, of which 49 were waited for; matrix products, arithmetic and copies ran while one was open for 13% of the time, Pallas kernels for 10%

profile of v5, /device:TPU:1, one launch (start us, length us, event | category | flops | bytes accessed | tf_op | source)
XLA Modules:
  0.0 467.7 jit_solution(192597760036158587)
XLA Ops:
  0.7 4.7 %collective-permute-start = (bf16[128,1024]{1,0:T(8,128)(2,1)}, bf16[128,1024]{1,0:T(8,128)(2,1)S(1)}, u32[]{:S(2)}, u32[]{:S(2)}) collective-permute-start(bf16[128,1024]{1,0:T(8,128)(2,1)} %param.12), channel_id=1, source_target_pairs={{0,0},{4,8},{8,4},{12,12},{1,1},{5,9},{9,5},{13,13},{2,2},{6,10},{... | collective-permute-start | bytes 786440 | tf_op jit(solution)/shard_map/ppermute | solution.py:49
  5.4 3.0 slice_bitcast_fusion.1
  10.9 3.7 collective-permute-start.3
  17.4 3.7 collective-permute-done.3
  21.8 5.4 %collective-permute-done.2 = bf16[128,1024]{1,0:T(8,128)(2,1)} collective-permute-done((bf16[128,1024]{1,0:T(8,128)(2,1)S(1)}, bf16[128,1024]{1,0:T(8,128)(2,1)}, u32[]{:S(2)}, u32[]{:S(2)}) %collective-permute-start.2) | collective-permute-done | bytes 262176 | tf_op jit(solution)/shard_map/ppermute | solution.py:41
  27.3 3.9 collective-permute-start.8
  42.4 6.5 %shard_map.211 = (bf16[1024,128]{1,0:T(8,128)(2,1)S(1)}, f32[2,1024]{1,0:T(2,128)S(1)}) custom-call(s32[8]{0:T(128)S(1)} %fusion.72.slots, bf16[1024,384]{1,0:T(8,128)(2,1)S(1)} %add_convert_fusion.1.low_ref.high_ref.k_ref.v_ref, bf16[1024,384]{1,0:T(8,128)(2,1)S(1)} %add_convert_fusion.1.low_ref.high_ref.k_ref.v_ref, ...), custom_call_target="tpu_custom_call" | custom-call | flops 1073741824 | bytes 2097152 | tf_op jit(solution)/shard_map/pallas_call | solution.py:291
  56.0 3.0 collective-permute-start.15
  65.4 6.3 %collective-permute-done.14 = bf16[128,1024]{1,0:T(8,128)(2,1)} collective-permute-done((bf16[128,1024]{1,0:T(8,128)(2,1)}, bf16[128,1024]{1,0:T(8,128)(2,1)}, u32[]{:S(2)}, u32[]{:S(2)}) %collective-permute-start.14) | collective-permute-done | bytes 262176 | tf_op jit(solution)/shard_map/ppermute | solution.py:41
  78.7 3.7 collective-permute-done.18
  82.4 6.1 %collective-permute-done.17 = bf16[128,1024]{1,0:T(8,128)(2,1)S(1)} collective-permute-done((bf16[128,1024]{1,0:T(8,128)(2,1)S(1)}, bf16[128,1024]{1,0:T(8,128)(2,1)S(1)}, u32[]{:S(2)}, u32[]{:S(2)}) %collective-permute-start.17) | collective-permute-done | bytes 262176 | tf_op jit(solution)/shard_map/ppermute | solution.py:41
  92.6 5.0 %multiply_convert_fusion.1 = (bf16[1024,512]{1,0:T(8,128)(2,1)S(1)}, f32[1024,512]{1,0:T(8,128)}) fusion(f32[512]{0:T(512)S(1)} %get-tuple-element.415, bf16[1024,1024]{1,0:T(8,128)(2,1)S(1)} %constant_dynamic-update-slice_fusion.refs_2_.refs_3_, bf16[1024,512]{1,0:T(8,128)(2,1)} %collective-permute-done.5), kind=kOutput, calls=%fused_computation.32 | convolution fusion | flops 1078984704 | bytes 6293504 | tf_op jit(solution)/shard_map/dot_general | solution.py:469
  112.0 6.3 %collective-permute-done.25 = bf16[128,1024]{1,0:T(8,128)(2,1)S(1)} collective-permute-done((bf16[128,1024]{1,0:T(8,128)(2,1)S(1)}, bf16[128,1024]{1,0:T(8,128)(2,1)S(1)}, u32[]{:S(2)}, u32[]{:S(2)}) %collective-permute-start.25) | collective-permute-done | bytes 262176 | tf_op jit(solution)/shard_map/ppermute | solution.py:41
  123.0 4.5 collective-permute-done.29
  127.5 7.1 %collective-permute-done.28 = bf16[128,1024]{1,0:T(8,128)(2,1)S(1)} collective-permute-done((bf16[128,1024]{1,0:T(8,128)(2,1)S(1)}, bf16[128,1024]{1,0:T(8,128)(2,1)S(1)}, u32[]{:S(2)}, u32[]{:S(2)}) %collective-permute-start.28) | collective-permute-done | bytes 262176 | tf_op jit(solution)/shard_map/ppermute | solution.py:41
  142.4 6.5 %shard_map.212 = (bf16[1024,128]{1,0:T(8,128)(2,1)S(1)}, f32[2,1024]{1,0:T(2,128)S(1)}) custom-call(s32[8]{0:T(128)S(1)} %fusion.72.slots, bf16[1024,384]{1,0:T(8,128)(2,1)S(1)} %add_convert_fusion.low_ref.high_ref.k_ref.v_ref, bf16[1024,384]{1,0:T(8,128)(2,1)S(1)} %add_convert_fusion.low_ref.high_ref.k_ref.v_ref, ...), custom_call_target="tpu_custom_call" | custom-call | flops 1073741824 | bytes 2097152 | tf_op jit(solution)/shard_map/pallas_call | solution.py:291
  157.8 4.3 collective-permute-done.37
  162.0 6.3 %collective-permute-done.36 = bf16[128,1024]{1,0:T(8,128)(2,1)S(1)} collective-permute-done((bf16[128,1024]{1,0:T(8,128)(2,1)S(1)}, bf16[128,1024]{1,0:T(8,128)(2,1)S(1)}, u32[]{:S(2)}, u32[]{:S(2)}) %collective-permute-start.36) | collective-permute-done | bytes 262176 | tf_op jit(solution)/shard_map/ppermute | solution.py:41
  175.1 3.4 collective-permute-done.40
  178.6 5.0 %collective-permute-done.39 = bf16[128,1024]{1,0:T(8,128)(2,1)S(1)} collective-permute-done((bf16[128,1024]{1,0:T(8,128)(2,1)S(1)}, bf16[128,1024]{1,0:T(8,128)(2,1)S(1)}, u32[]{:S(2)}, u32[]{:S(2)}) %collective-permute-start.39) | collective-permute-done | bytes 262176 | tf_op jit(solution)/shard_map/ppermute | solution.py:41
  189.4 3.7 convert_reduce_fusion
  206.9 4.5 shard_map.213
  211.5 5.4 %collective-permute-done.45 = bf16[128,1024]{1,0:T(8,128)(2,1)S(1)} collective-permute-done((bf16[128,1024]{1,0:T(8,128)(2,1)S(1)}, bf16[128,1024]{1,0:T(8,128)(2,1)S(1)}, u32[]{:S(2)}, u32[]{:S(2)}) %collective-permute-start.45) | collective-permute-done | bytes 262176 | tf_op jit(solution)/shard_map/ppermute | solution.py:41
  224.9 5.0 %collective-permute-done.49 = bf16[128,1024]{1,0:T(8,128)(2,1)S(1)} collective-permute-done((bf16[128,1024]{1,0:T(8,128)(2,1)S(1)}, bf16[128,1024]{1,0:T(8,128)(2,1)S(1)}, u32[]{:S(2)}, u32[]{:S(2)}) %collective-permute-start.49) | collective-permute-done | bytes 262176 | tf_op jit(solution)/shard_map/ppermute | solution.py:41
  229.9 5.4 %collective-permute-done.48 = bf16[128,1024]{1,0:T(8,128)(2,1)S(1)} collective-permute-done((bf16[128,1024]{1,0:T(8,128)(2,1)S(1)}, bf16[128,1024]{1,0:T(8,128)(2,1)S(1)}, u32[]{:S(2)}, u32[]{:S(2)}) %collective-permute-start.48) | collective-permute-done | bytes 262176 | tf_op jit(solution)/shard_map/ppermute | solution.py:41
  248.5 7.5 %shard_map.214.refs_5_ = bf16[1024,384]{1,0:T(8,128)(2,1)S(1)} custom-call(s32[8]{0:T(128)S(1)} %fusion.72.slots, f32[2,1024]{1,0:T(2,128)S(1)} %get-tuple-element.171.log_ref, bf16[1024,384]{1,0:T(8,128)(2,1)S(1)} %copy-done.20, bf16[1024,384]{1,0:T(8,128)(2,1)S(1)} %copy-done.20, bf16[1024,384]{1,0:T(8,128)(2,1)S(1)} %copy-done.20, ...), custom_call_target="tpu_custom_call" | custom-call | flops 2684354560 | bytes 4194304 | tf_op jit(solution)/shard_map/pallas_call | solution.py:367
  264.0 4.1 collective-permute-start.62
  275.2 3.9 shard_map.215
  280.6 5.0 %collective-permute-done.59 = bf16[128,1024]{1,0:T(8,128)(2,1)S(1)} collective-permute-done((bf16[128,1024]{1,0:T(8,128)(2,1)S(1)}, bf16[128,1024]{1,0:T(8,128)(2,1)S(1)}, u32[]{:S(2)}, u32[]{:S(2)}) %collective-permute-start.59) | collective-permute-done | bytes 262176 | tf_op jit(solution)/shard_map/ppermute | solution.py:41
  293.9 3.6 collective-permute-done.66
  299.1 3.0 collective-permute-done.65
  304.8 3.0 collective-permute-start.70
  315.1 2.8 fusion.3.refs_5_
  319.0 3.1 convolution_convert_fusion.4
  334.4 5.2 %shard_map.216 = (bf16[2,128,1024]{2,1,0:T(8,128)(2,1)S(1)}, bf16[2,128,1024]{2,1,0:T(8,128)(2,1)S(1)}, bf16[2,128,1024]{2,1,0:T(8,128)(2,1)}, bf16[2,128,1024]{2,1,0:T(8,128)(2,1)S(1)}) custom-call(s32[1]{0:T(128)} %bitcast.27.place_ref, bf16[1024,1024]{1,0:T(8,128)(2,1)S(1)} %constant_dynamic-update-slice_fusion.11.refs_0_.refs_1_, ...), custom_call_target="tpu_custom_call" | custom-call | flops 2147483648 | bytes 8388608 | tf_op jit(solution)/shard_map/pallas_call | solution.py:150
  339.7 5.1 %collective-permute-done.78 = bf16[128,1024]{1,0:T(8,128)(2,1)S(1)} collective-permute-done((bf16[128,1024]{1,0:T(8,128)(2,1)S(1)}, bf16[128,1024]{1,0:T(8,128)(2,1)S(1)}, u32[]{:S(2)}, u32[]{:S(2)}) %collective-permute-start.78) | collective-permute-done | bytes 262176 | tf_op jit(solution)/shard_map/ppermute | solution.py:41
  355.0 4.9 %collective-permute-done.81 = bf16[128,1024]{1,0:T(8,128)(2,1)S(1)} collective-permute-done((bf16[128,1024]{1,0:T(8,128)(2,1)S(1)}, bf16[128,1024]{1,0:T(8,128)(2,1)S(1)}, u32[]{:S(2)}, u32[]{:S(2)}) %collective-permute-start.81) | collective-permute-done | bytes 262176 | tf_op jit(solution)/shard_map/ppermute | solution.py:41
  369.6 3.6 collective-permute-done.72
  374.1 2.8 collective-permute-start.86
  380.5 7.5 %shard_map.217.refs_5_ = bf16[1024,384]{1,0:T(8,128)(2,1)S(1)} custom-call(s32[8]{0:T(128)S(1)} %fusion.72.slots, f32[2,1024]{1,0:T(2,128)S(1)} %get-tuple-element.246.log_ref, bf16[1024,384]{1,0:T(8,128)(2,1)S(1)} %copy-done.18, bf16[1024,384]{1,0:T(8,128)(2,1)S(1)} %copy-done.18, bf16[1024,384]{1,0:T(8,128)(2,1)S(1)} %copy-done.18, ...), custom_call_target="tpu_custom_call" | custom-call | flops 2684354560 | bytes 4194304 | tf_op jit(solution)/shard_map/pallas_call | solution.py:367
  390.6 2.9 collective-permute-start.91
  401.5 3.9 shard_map.218
  405.7 7.0 %collective-permute-done.89 = bf16[128,1024]{1,0:T(8,128)(2,1)S(1)} collective-permute-done((bf16[128,1024]{1,0:T(8,128)(2,1)S(1)}, bf16[128,1024]{1,0:T(8,128)(2,1)S(1)}, u32[]{:S(2)}, u32[]{:S(2)}) %collective-permute-start.89) | collective-permute-done | bytes 262176 | tf_op jit(solution)/shard_map/ppermute | solution.py:41
  423.8 4.6 collective-permute-start.94
  428.5 3.7 collective-permute-done.100
  445.9 2.8 collective-permute-start.107
  451.2 3.2 collective-permute-done.108
  454.4 6.3 %collective-permute-start.110 = (f32[108,128]{1,0:T(8,128)S(1)}, f32[108,128]{1,0:T(8,128)S(1)}, u32[]{:S(2)}, u32[]{:S(2)}) collective-permute-start(f32[108,128]{1,0:T(8,128)S(1)} %add_add_fusion.8), channel_id=1, source_target_pairs={{0,8},{8,0},{1,9},{9,1},{2,10},{10,2},{3,11},{11,3},{4,12},{12,4},... | collective-permute-start | bytes 165896 | tf_op jit(solution)/shard_map/ppermute | solution.py:45
  (618 shorter events, 242.2 us)
Async XLA Ops:
  8.4 30.8 %collective-permute-start.5 = (bf16[1024,512]{1,0:T(8,128)(2,1)}, bf16[1024,512]{1,0:T(8,128)(2,1)}, u32[]{:S(2)}, u32[]{:S(2)}) collective-permute-start(bf16[1024,512]{1,0:T(8,128)(2,1)} %get-tuple-element.348), channel_id=1, source_target_pairs={{0,4},{8,0},{4,12},{12,72},{64,68},{72,64},{68,76},{76,8},{1,5},{9... | collective-permute-start | bytes 3145736 | tf_op jit(solution)/shard_map/ppermute | solution.py:66
  14.5 12.7 %collective-permute-start.2 = (bf16[128,1024]{1,0:T(8,128)(2,1)S(1)}, bf16[128,1024]{1,0:T(8,128)(2,1)}, u32[]{:S(2)}, u32[]{:S(2)}) collective-permute-start(bf16[128,1024]{1,0:T(8,128)(2,1)S(1)} %fusion.19), channel_id=1, source_target_pairs={{0,3},{1,0},{2,1},{3,2},{4,7},{5,4},{6,5},{7,6},{8,11},{9,8},{10,9... | collective-permute-start | bytes 786440 | tf_op jit(solution)/shard_map/ppermute | solution.py:41
  15.0 16.2 %collective-permute-start.1 = (bf16[128,1024]{1,0:T(8,128)(2,1)S(1)}, bf16[128,1024]{1,0:T(8,128)(2,1)}, u32[]{:S(2)}, u32[]{:S(2)}) collective-permute-start(bf16[128,1024]{1,0:T(8,128)(2,1)S(1)} %fusion.19), channel_id=1, source_target_pairs={{0,1},{1,2},{2,3},{3,0},{4,5},{5,6},{6,7},{7,4},{8,9},{9,10},{10,1... | collective-permute-start | bytes 786440 | tf_op jit(solution)/shard_map/ppermute | solution.py:41
  17.3 22.5 %collective-permute-start.6 = (bf16[1024,384]{0,1:T(8,128)(2,1)}, bf16[1024,384]{0,1:T(8,128)(2,1)S(1)}, u32[]{:S(2)}, u32[]{:S(2)}) collective-permute-start(bf16[1024,384]{0,1:T(8,128)(2,1)} %bitcast.159), channel_id=1, source_target_pairs={{0,68},{8,0},{4,12},{12,8},{64,4},{72,64},{68,76},{76,72},{1,69},{... | collective-permute-start | bytes 2359304 | tf_op jit(solution)/shard_map/ppermute | solution.py:66
  21.0 14.8 %collective-permute-start.7 = (f32[12,128]{1,0:T(8,128)S(1)}, f32[12,128]{1,0:T(8,128)S(1)}, u32[]{:S(2)}, u32[]{:S(2)}) collective-permute-start(f32[12,128]{1,0:T(8,128)S(1)} %pad_maximum_fusion.14), channel_id=1, source_target_pairs={{0,4},{8,0},{4,12},{12,72},{64,68},{72,64},{68,76},{76,8},{1,5},{9... | collective-permute-start | bytes 18440 | tf_op jit(solution)/shard_map/ppermute | solution.py:66
  27.3 11.9 %collective-permute-start.8 = (bf16[128,1024]{1,0:T(8,128)(2,1)}, bf16[128,1024]{1,0:T(8,128)(2,1)S(1)}, u32[]{:S(2)}, u32[]{:S(2)}) collective-permute-start(bf16[128,1024]{1,0:T(8,128)(2,1)} %param.13), channel_id=1, source_target_pairs={{0,0},{4,8},{8,4},{12,12},{1,1},{5,9},{9,5},{13,13},{2,2},{6,10},{... | collective-permute-start | bytes 786440 | tf_op jit(solution)/shard_map/ppermute | solution.py:49
  35.8 13.9 %collective-permute-start.10 = (bf16[512,1024]{1,0:T(8,128)(2,1)}, bf16[512,1024]{1,0:T(8,128)(2,1)S(1)}, u32[]{:S(2)}, u32[]{:S(2)}) collective-permute-start(bf16[512,1024]{1,0:T(8,128)(2,1)} %get-tuple-element.346), channel_id=1, source_target_pairs={{0,68},{8,0},{4,12},{12,8},{64,4},{72,64},{68,76},{76,72},{1,69},{... | collective-permute-start | bytes 3145736 | tf_op jit(solution)/shard_map/ppermute | solution.py:66
  36.4 13.3 %collective-permute-start.11 = (bf16[128,1024]{1,0:T(8,128)(2,1)S(1)}, bf16[128,1024]{1,0:T(8,128)(2,1)S(1)}, u32[]{:S(2)}, u32[]{:S(2)}) collective-permute-start(bf16[128,1024]{1,0:T(8,128)(2,1)S(1)} %get-tuple-element.392), channel_id=1, source_target_pairs={{0,4},{8,0},{4,12},{12,72},{64,68},{72,64},{68,76},{76,8},{1,5},{9... | collective-permute-start | bytes 786440 | tf_op jit(solution)/shard_map/ppermute | solution.py:66
  59.0 12.7 %collective-permute-start.14 = (bf16[128,1024]{1,0:T(8,128)(2,1)}, bf16[128,1024]{1,0:T(8,128)(2,1)}, u32[]{:S(2)}, u32[]{:S(2)}) collective-permute-start(bf16[128,1024]{1,0:T(8,128)(2,1)} %get-tuple-element.380), channel_id=1, source_target_pairs={{0,1},{1,2},{2,3},{3,0},{4,5},{5,6},{6,7},{7,4},{8,9},{9,10},{10,1... | collective-permute-start | bytes 786440 | tf_op jit(solution)/shard_map/ppermute | solution.py:41
  59.2 12.5 %collective-permute-start.13 = (bf16[128,1024]{1,0:T(8,128)(2,1)}, bf16[128,1024]{1,0:T(8,128)(2,1)}, u32[]{:S(2)}, u32[]{:S(2)}) collective-permute-start(bf16[128,1024]{1,0:T(8,128)(2,1)} %get-tuple-element.378), channel_id=1, source_target_pairs={{0,3},{1,0},{2,1},{3,2},{4,7},{5,4},{6,5},{7,6},{8,11},{9,8},{10,9... | collective-permute-start | bytes 786440 | tf_op jit(solution)/shard_map/ppermute | solution.py:41
  62.0 27.0 %collective-permute-start.19 = (bf16[1024,384]{0,1:T(8,128)(2,1)S(1)}, bf16[1024,384]{0,1:T(8,128)(2,1)S(1)}, u32[]{:S(2)}, u32[]{:S(2)}) collective-permute-start(bf16[1024,384]{0,1:T(8,128)(2,1)S(1)} %bitcast.160), channel_id=1, source_target_pairs={{0,68},{8,0},{4,12},{12,8},{64,4},{72,64},{68,76},{76,72},{1,69},{... | collective-permute-start | bytes 2359304 | tf_op jit(solution)/shard_map/ppermute | solution.py:66
  75.0 13.5 %collective-permute-start.17 = (bf16[128,1024]{1,0:T(8,128)(2,1)S(1)}, bf16[128,1024]{1,0:T(8,128)(2,1)S(1)}, u32[]{:S(2)}, u32[]{:S(2)}) collective-permute-start(bf16[128,1024]{1,0:T(8,128)(2,1)S(1)} %add_convert_fusion.6), channel_id=1, source_target_pairs={{0,3},{1,0},{2,1},{3,2},{4,7},{5,4},{6,5},{7,6},{8,11},{9,8},{10,9... | collective-permute-start | bytes 786440 | tf_op jit(solution)/shard_map/ppermute | solution.py:41
  77.0 11.8 %collective-permute-start.16 = (bf16[128,1024]{1,0:T(8,128)(2,1)S(1)}, bf16[128,1024]{1,0:T(8,128)(2,1)S(1)}, u32[]{:S(2)}, u32[]{:S(2)}) collective-permute-start(bf16[128,1024]{1,0:T(8,128)(2,1)S(1)} %add_convert_fusion.6), channel_id=1, source_target_pairs={{0,1},{1,2},{2,3},{3,0},{4,5},{5,6},{6,7},{7,4},{8,9},{9,10},{10,1... | collective-permute-start | bytes 786440 | tf_op jit(solution)/shard_map/ppermute | solution.py:41
  77.0 11.9 %collective-permute-start.20 = (bf16[128,1024]{1,0:T(8,128)(2,1)S(1)}, bf16[128,1024]{1,0:T(8,128)(2,1)S(1)}, u32[]{:S(2)}, u32[]{:S(2)}) collective-permute-start(bf16[128,1024]{1,0:T(8,128)(2,1)S(1)} %copy-done.74), channel_id=1, source_target_pairs={{0,4},{8,0},{4,12},{12,72},{64,68},{72,64},{68,76},{76,8},{1,5},{9... | collective-permute-start | bytes 786440 | tf_op jit(solution)/shard_map/ppermute | solution.py:66
  104.8 13.4 %collective-permute-start.25 = (bf16[128,1024]{1,0:T(8,128)(2,1)S(1)}, bf16[128,1024]{1,0:T(8,128)(2,1)S(1)}, u32[]{:S(2)}, u32[]{:S(2)}) collective-permute-start(bf16[128,1024]{1,0:T(8,128)(2,1)S(1)} %get-tuple-element.377), channel_id=1, source_target_pairs={{0,1},{1,2},{2,3},{3,0},{4,5},{5,6},{6,7},{7,4},{8,9},{9,10},{10,1... | collective-permute-start | bytes 786440 | tf_op jit(solution)/shard_map/ppermute | solution.py:41
  107.5 27.2 %collective-permute-start.30 = (bf16[1024,512]{1,0:T(8,128)(2,1)S(1)}, bf16[1024,512]{1,0:T(8,128)(2,1)S(1)}, u32[]{:S(2)}, u32[]{:S(2)}) collective-permute-start(bf16[1024,512]{1,0:T(8,128)(2,1)S(1)} %copy-done.54), channel_id=1, source_target_pairs={{0,4},{8,0},{4,12},{12,72},{64,68},{72,64},{68,76},{76,8},{1,5},{9... | collective-permute-start | bytes 3145736 | tf_op jit(solution)/shard_map/ppermute | solution.py:66
  108.7 26.0 %collective-permute-start.31 = (bf16[512,1024]{1,0:T(8,128)(2,1)S(1)}, bf16[512,1024]{1,0:T(8,128)(2,1)S(1)}, u32[]{:S(2)}, u32[]{:S(2)}) collective-permute-start(bf16[512,1024]{1,0:T(8,128)(2,1)S(1)} %copy-done.57), channel_id=1, source_target_pairs={{0,68},{8,0},{4,12},{12,8},{64,4},{72,64},{68,76},{76,72},{1,69},{... | collective-permute-start | bytes 3145736 | tf_op jit(solution)/shard_map/ppermute | solution.py:66
  120.9 13.6 %collective-permute-start.28 = (bf16[128,1024]{1,0:T(8,128)(2,1)S(1)}, bf16[128,1024]{1,0:T(8,128)(2,1)S(1)}, u32[]{:S(2)}, u32[]{:S(2)}) collective-permute-start(bf16[128,1024]{1,0:T(8,128)(2,1)S(1)} %add_convert_fusion.5), channel_id=1, source_target_pairs={{0,3},{1,0},{2,1},{3,2},{4,7},{5,4},{6,5},{7,6},{8,11},{9,8},{10,9... | collective-permute-start | bytes 786440 | tf_op jit(solution)/shard_map/ppermute | solution.py:41
  122.5 12.1 %collective-permute-start.27 = (bf16[128,1024]{1,0:T(8,128)(2,1)S(1)}, bf16[128,1024]{1,0:T(8,128)(2,1)S(1)}, u32[]{:S(2)}, u32[]{:S(2)}) collective-permute-start(bf16[128,1024]{1,0:T(8,128)(2,1)S(1)} %add_convert_fusion.5), channel_id=1, source_target_pairs={{0,1},{1,2},{2,3},{3,0},{4,5},{5,6},{6,7},{7,4},{8,9},{9,10},{10,1... | collective-permute-start | bytes 786440 | tf_op jit(solution)/shard_map/ppermute | solution.py:41
  155.1 13.2 %collective-permute-start.36 = (bf16[128,1024]{1,0:T(8,128)(2,1)S(1)}, bf16[128,1024]{1,0:T(8,128)(2,1)S(1)}, u32[]{:S(2)}, u32[]{:S(2)}) collective-permute-start(bf16[128,1024]{1,0:T(8,128)(2,1)S(1)} %get-tuple-element.374), channel_id=1, source_target_pairs={{0,1},{1,2},{2,3},{3,0},{4,5},{5,6},{6,7},{7,4},{8,9},{9,10},{10,1... | collective-permute-start | bytes 786440 | tf_op jit(solution)/shard_map/ppermute | solution.py:41
  155.3 13.0 %collective-permute-start.35 = (bf16[128,1024]{1,0:T(8,128)(2,1)S(1)}, bf16[128,1024]{1,0:T(8,128)(2,1)S(1)}, u32[]{:S(2)}, u32[]{:S(2)}) collective-permute-start(bf16[128,1024]{1,0:T(8,128)(2,1)S(1)} %get-tuple-element.372), channel_id=1, source_target_pairs={{0,3},{1,0},{2,1},{3,2},{4,7},{5,4},{6,5},{7,6},{8,11},{9,8},{10,9... | collective-permute-start | bytes 786440 | tf_op jit(solution)/shard_map/ppermute | solution.py:41
  171.5 12.1 %collective-permute-start.39 = (bf16[128,1024]{1,0:T(8,128)(2,1)S(1)}, bf16[128,1024]{1,0:T(8,128)(2,1)S(1)}, u32[]{:S(2)}, u32[]{:S(2)}) collective-permute-start(bf16[128,1024]{1,0:T(8,128)(2,1)S(1)} %add_convert_fusion.4), channel_id=1, source_target_pairs={{0,3},{1,0},{2,1},{3,2},{4,7},{5,4},{6,5},{7,6},{8,11},{9,8},{10,9... | collective-permute-start | bytes 786440 | tf_op jit(solution)/shard_map/ppermute | solution.py:41
  174.0 11.9 %collective-permute-start.42 = (bf16[512,1024]{1,0:T(8,128)(2,1)S(1)}, bf16[512,1024]{1,0:T(8,128)(2,1)S(1)}, u32[]{:S(2)}, u32[]{:S(2)}) collective-permute-start(bf16[512,1024]{1,0:T(8,128)(2,1)S(1)} %pad_maximum_fusion.6), channel_id=1, source_target_pairs={{0,8},{8,0},{1,9},{9,1},{2,10},{10,2},{3,11},{11,3},{4,12},{12,4},... | collective-permute-start | bytes 3145736 | tf_op jit(solution)/shard_map/ppermute | solution.py:45
  204.1 12.8 %collective-permute-start.45 = (bf16[128,1024]{1,0:T(8,128)(2,1)S(1)}, bf16[128,1024]{1,0:T(8,128)(2,1)S(1)}, u32[]{:S(2)}, u32[]{:S(2)}) collective-permute-start(bf16[128,1024]{1,0:T(8,128)(2,1)S(1)} %get-tuple-element.371), channel_id=1, source_target_pairs={{0,1},{1,2},{2,3},{3,0},{4,5},{5,6},{6,7},{7,4},{8,9},{9,10},{10,1... | collective-permute-start | bytes 786440 | tf_op jit(solution)/shard_map/ppermute | solution.py:41
  204.1 12.8 %collective-permute-start.44 = (bf16[128,1024]{1,0:T(8,128)(2,1)S(1)}, bf16[128,1024]{1,0:T(8,128)(2,1)S(1)}, u32[]{:S(2)}, u32[]{:S(2)}) collective-permute-start(bf16[128,1024]{1,0:T(8,128)(2,1)S(1)} %get-tuple-element.369), channel_id=1, source_target_pairs={{0,3},{1,0},{2,1},{3,2},{4,7},{5,4},{6,5},{7,6},{8,11},{9,8},{10,9... | collective-permute-start | bytes 786440 | tf_op jit(solution)/shard_map/ppermute | solution.py:41
  218.2 18.4 %collective-permute-start.50 = (bf16[2,128,1024]{2,1,0:T(8,128)(2,1)S(1)}, bf16[2,128,1024]{2,1,0:T(8,128)(2,1)S(1)}, u32[]{:S(2)}, u32[]{:S(2)}) collective-permute-start(bf16[2,128,1024]{2,1,0:T(8,128)(2,1)S(1)} %get-tuple-element.187), channel_id=1, source_target_pairs={{0,16},{16,32},{32,48},{48,0},{1,17},{17,33},{33,49},{49,1},{2,18}... | collective-permute-start | bytes 1572872 | tf_op jit(solution)/shard_map/ppermute | solution.py:41
  219.5 17.1 %collective-permute-start.51 = (bf16[2,128,1024]{2,1,0:T(8,128)(2,1)S(1)}, bf16[2,128,1024]{2,1,0:T(8,128)(2,1)S(1)}, u32[]{:S(2)}, u32[]{:S(2)}) collective-permute-start(bf16[2,128,1024]{2,1,0:T(8,128)(2,1)S(1)} %get-tuple-element.188), channel_id=1, source_target_pairs={{0,48},{16,0},{32,16},{48,32},{1,49},{17,1},{33,17},{49,33},{2,50}... | collective-permute-start | bytes 1572872 | tf_op jit(solution)/shard_map/ppermute | solution.py:41
  222.4 12.9 %collective-permute-start.48 = (bf16[128,1024]{1,0:T(8,128)(2,1)S(1)}, bf16[128,1024]{1,0:T(8,128)(2,1)S(1)}, u32[]{:S(2)}, u32[]{:S(2)}) collective-permute-start(bf16[128,1024]{1,0:T(8,128)(2,1)S(1)} %get-tuple-element.329), channel_id=1, source_target_pairs={{0,3},{1,0},{2,1},{3,2},{4,7},{5,4},{6,5},{7,6},{8,11},{9,8},{10,9... | collective-permute-start | bytes 786440 | tf_op jit(solution)/shard_map/ppermute | solution.py:41
  241.3 15.6 %collective-permute-start.56 = (bf16[2,128,1024]{2,1,0:T(8,128)(2,1)S(1)}, bf16[2,128,1024]{2,1,0:T(8,128)(2,1)S(1)}, u32[]{:S(2)}, u32[]{:S(2)}) collective-permute-start(bf16[2,128,1024]{2,1,0:T(8,128)(2,1)S(1)} %get-tuple-element.196), channel_id=1, source_target_pairs={{0,32},{16,48},{32,0},{48,16},{1,33},{17,49},{33,1},{49,17},{2,34}... | collective-permute-start | bytes 1572872 | tf_op jit(solution)/shard_map/ppermute | solution.py:41
  272.0 13.6 %collective-permute-start.59 = (bf16[128,1024]{1,0:T(8,128)(2,1)S(1)}, bf16[128,1024]{1,0:T(8,128)(2,1)S(1)}, u32[]{:S(2)}, u32[]{:S(2)}) collective-permute-start(bf16[128,1024]{1,0:T(8,128)(2,1)S(1)} %get-tuple-element.365), channel_id=1, source_target_pairs={{0,1},{1,2},{2,3},{3,0},{4,5},{5,6},{6,7},{7,4},{8,9},{9,10},{10,1... | collective-permute-start | bytes 786440 | tf_op jit(solution)/shard_map/ppermute | solution.py:41
  272.9 12.8 %collective-permute-start.58 = (bf16[128,1024]{1,0:T(8,128)(2,1)S(1)}, bf16[128,1024]{1,0:T(8,128)(2,1)S(1)}, u32[]{:S(2)}, u32[]{:S(2)}) collective-permute-start(bf16[128,1024]{1,0:T(8,128)(2,1)S(1)} %get-tuple-element.363), channel_id=1, source_target_pairs={{0,3},{1,0},{2,1},{3,2},{4,7},{5,4},{6,5},{7,6},{8,11},{9,8},{10,9... | collective-permute-start | bytes 786440 | tf_op jit(solution)/shard_map/ppermute | solution.py:41
  289.5 12.6 %collective-permute-start.65 = (bf16[128,1024]{1,0:T(8,128)(2,1)S(1)}, bf16[128,1024]{1,0:T(8,128)(2,1)S(1)}, u32[]{:S(2)}, u32[]{:S(2)}) collective-permute-start(bf16[128,1024]{1,0:T(8,128)(2,1)S(1)} %get-tuple-element.326), channel_id=1, source_target_pairs={{0,3},{1,0},{2,1},{3,2},{4,7},{5,4},{6,5},{7,6},{8,11},{9,8},{10,9... | collective-permute-start | bytes 786440 | tf_op jit(solution)/shard_map/ppermute | solution.py:41
  291.2 12.6 %collective-permute-start.64 = (bf16[128,1024]{1,0:T(8,128)(2,1)S(1)}, bf16[128,1024]{1,0:T(8,128)(2,1)S(1)}, u32[]{:S(2)}, u32[]{:S(2)}) collective-permute-start(bf16[128,1024]{1,0:T(8,128)(2,1)S(1)} %get-tuple-element.326), channel_id=1, source_target_pairs={{0,1},{1,2},{2,3},{3,0},{4,5},{5,6},{6,7},{7,4},{8,9},{9,10},{10,1... | collective-permute-start | bytes 786440 | tf_op jit(solution)/shard_map/ppermute | solution.py:41
  291.2 12.7 %collective-permute-start.67 = (bf16[2,128,512]{2,1,0:T(8,128)(2,1)S(1)}, bf16[2,128,512]{2,1,0:T(8,128)(2,1)S(1)}, u32[]{:S(2)}, u32[]{:S(2)}) collective-permute-start(bf16[2,128,512]{2,1,0:T(8,128)(2,1)S(1)} %get-tuple-element.216), channel_id=1, source_target_pairs={{0,16},{16,32},{32,48},{48,0},{1,17},{17,33},{33,49},{49,1},{2,18}... | collective-permute-start | bytes 786440 | tf_op jit(solution)/shard_map/ppermute | solution.py:41
  291.2 12.7 %collective-permute-start.68 = (bf16[2,128,512]{2,1,0:T(8,128)(2,1)S(1)}, bf16[2,128,512]{2,1,0:T(8,128)(2,1)S(1)}, u32[]{:S(2)}, u32[]{:S(2)}) collective-permute-start(bf16[2,128,512]{2,1,0:T(8,128)(2,1)S(1)} %get-tuple-element.217), channel_id=1, source_target_pairs={{0,48},{16,0},{32,16},{48,32},{1,49},{17,1},{33,17},{49,33},{2,50}... | collective-permute-start | bytes 786440 | tf_op jit(solution)/shard_map/ppermute | solution.py:41
  324.3 26.1 %collective-permute-start.114 = (f32[64,1024]{1,0:T(8,128)}, f32[64,1024]{1,0:T(8,128)S(1)}, u32[]{:S(2)}, u32[]{:S(2)}) collective-permute-start(f32[64,1024]{1,0:T(8,128)} %get-tuple-element.297), channel_id=1, source_target_pairs={{0,8},{12,4},{1,9},{13,5},{2,10},{14,6},{3,11},{15,7},{16,24},{28,... | collective-permute-start | bytes 786440 | tf_op jit(solution)/shard_map/ppermute | solution.py:205
  331.4 13.4 %collective-permute-start.78 = (bf16[128,1024]{1,0:T(8,128)(2,1)S(1)}, bf16[128,1024]{1,0:T(8,128)(2,1)S(1)}, u32[]{:S(2)}, u32[]{:S(2)}) collective-permute-start(bf16[128,1024]{1,0:T(8,128)(2,1)S(1)} %get-tuple-element.359), channel_id=1, source_target_pairs={{0,1},{1,2},{2,3},{3,0},{4,5},{5,6},{6,7},{7,4},{8,9},{9,10},{10,1... | collective-permute-start | bytes 786440 | tf_op jit(solution)/shard_map/ppermute | solution.py:41
  331.9 12.9 %collective-permute-start.77 = (bf16[128,1024]{1,0:T(8,128)(2,1)S(1)}, bf16[128,1024]{1,0:T(8,128)(2,1)S(1)}, u32[]{:S(2)}, u32[]{:S(2)}) collective-permute-start(bf16[128,1024]{1,0:T(8,128)(2,1)S(1)} %get-tuple-element.357), channel_id=1, source_target_pairs={{0,3},{1,0},{2,1},{3,2},{4,7},{5,4},{6,5},{7,6},{8,11},{9,8},{10,9... | collective-permute-start | bytes 786440 | tf_op jit(solution)/shard_map/ppermute | solution.py:41
  347.4 12.6 %collective-permute-start.81 = (bf16[128,1024]{1,0:T(8,128)(2,1)S(1)}, bf16[128,1024]{1,0:T(8,128)(2,1)S(1)}, u32[]{:S(2)}, u32[]{:S(2)}) collective-permute-start(bf16[128,1024]{1,0:T(8,128)(2,1)S(1)} %get-tuple-element.331), channel_id=1, source_target_pairs={{0,3},{1,0},{2,1},{3,2},{4,7},{5,4},{6,5},{7,6},{8,11},{9,8},{10,9... | collective-permute-start | bytes 786440 | tf_op jit(solution)/shard_map/ppermute | solution.py:41
  349.8 13.6 %collective-permute-start.83 = (bf16[2,128,1024]{2,1,0:T(8,128)(2,1)S(1)}, bf16[2,128,1024]{2,1,0:T(8,128)(2,1)S(1)}, u32[]{:S(2)}, u32[]{:S(2)}) collective-permute-start(bf16[2,128,1024]{2,1,0:T(8,128)(2,1)S(1)} %get-tuple-element.248), channel_id=1, source_target_pairs={{0,16},{16,32},{32,48},{48,0},{1,17},{17,33},{33,49},{49,1},{2,18}... | collective-permute-start | bytes 1572872 | tf_op jit(solution)/shard_map/ppermute | solution.py:41
  350.4 13.0 %collective-permute-start.84 = (bf16[2,128,1024]{2,1,0:T(8,128)(2,1)S(1)}, bf16[2,128,1024]{2,1,0:T(8,128)(2,1)S(1)}, u32[]{:S(2)}, u32[]{:S(2)}) collective-permute-start(bf16[2,128,1024]{2,1,0:T(8,128)(2,1)S(1)} %get-tuple-element.249), channel_id=1, source_target_pairs={{0,48},{16,0},{32,16},{48,32},{1,49},{17,1},{33,17},{49,33},{2,50}... | collective-permute-start | bytes 1572872 | tf_op jit(solution)/shard_map/ppermute | solution.py:41
  363.4 14.9 %collective-permute-start.85 = (bf16[512,1024]{1,0:T(8,128)(2,1)}, bf16[512,1024]{1,0:T(8,128)(2,1)}, u32[]{:S(2)}, u32[]{:S(2)}) collective-permute-start(bf16[512,1024]{1,0:T(8,128)(2,1)} %pad_maximum_fusion.9), channel_id=1, source_target_pairs={{0,8},{8,0},{1,9},{9,1},{2,10},{10,2},{3,11},{11,3},{4,12},{12,4},... | collective-permute-start | bytes 3145736 | tf_op jit(solution)/shard_map/ppermute | solution.py:45
  374.1 13.9 %collective-permute-start.86 = (bf16[2,128,1024]{2,1,0:T(8,128)(2,1)}, bf16[2,128,1024]{2,1,0:T(8,128)(2,1)}, u32[]{:S(2)}, u32[]{:S(2)}) collective-permute-start(bf16[2,128,1024]{2,1,0:T(8,128)(2,1)} %get-tuple-element.254), channel_id=1, source_target_pairs={{0,32},{16,48},{32,0},{48,16},{1,33},{17,49},{33,1},{49,17},{2,34}... | collective-permute-start | bytes 1572872 | tf_op jit(solution)/shard_map/ppermute | solution.py:41
  398.5 14.2 %collective-permute-start.89 = (bf16[128,1024]{1,0:T(8,128)(2,1)S(1)}, bf16[128,1024]{1,0:T(8,128)(2,1)S(1)}, u32[]{:S(2)}, u32[]{:S(2)}) collective-permute-start(bf16[128,1024]{1,0:T(8,128)(2,1)S(1)} %get-tuple-element.356), channel_id=1, source_target_pairs={{0,1},{1,2},{2,3},{3,0},{4,5},{5,6},{6,7},{7,4},{8,9},{9,10},{10,1... | collective-permute-start | bytes 786440 | tf_op jit(solution)/shard_map/ppermute | solution.py:41
  400.5 12.1 %collective-permute-start.88 = (bf16[128,1024]{1,0:T(8,128)(2,1)S(1)}, bf16[128,1024]{1,0:T(8,128)(2,1)S(1)}, u32[]{:S(2)}, u32[]{:S(2)}) collective-permute-start(bf16[128,1024]{1,0:T(8,128)(2,1)S(1)} %get-tuple-element.354), channel_id=1, source_target_pairs={{0,3},{1,0},{2,1},{3,2},{4,7},{5,4},{6,5},{7,6},{8,11},{9,8},{10,9... | collective-permute-start | bytes 786440 | tf_op jit(solution)/shard_map/ppermute | solution.py:41
  420.2 12.0 %collective-permute-start.100 = (bf16[2,128,512]{2,1,0:T(8,128)(2,1)S(1)}, bf16[2,128,512]{2,1,0:T(8,128)(2,1)S(1)}, u32[]{:S(2)}, u32[]{:S(2)}) collective-permute-start(bf16[2,128,512]{2,1,0:T(8,128)(2,1)S(1)} %get-tuple-element.276), channel_id=1, source_target_pairs={{0,32},{16,48},{32,0},{48,16},{1,33},{17,49},{33,1},{49,17},{2,34}... | collective-permute-start | bytes 786440 | tf_op jit(solution)/shard_map/ppermute | solution.py:41
  421.5 15.6 %collective-permute-start.113 = (f32[64,1024]{1,0:T(8,128)S(1)}, f32[64,1024]{1,0:T(8,128)}, u32[]{:S(2)}, u32[]{:S(2)}) collective-permute-start(f32[64,1024]{1,0:T(8,128)S(1)} %get-tuple-element.295), channel_id=1, source_target_pairs={{0,8},{12,4},{1,9},{13,5},{2,10},{14,6},{3,11},{15,7},{16,24},{28,... | collective-permute-start | bytes 786440 | tf_op jit(solution)/shard_map/ppermute | solution.py:205
  423.8 15.8 %collective-permute-start.94 = (bf16[128,1024]{1,0:T(8,128)(2,1)}, bf16[128,1024]{1,0:T(8,128)(2,1)S(1)}, u32[]{:S(2)}, u32[]{:S(2)}) collective-permute-start(bf16[128,1024]{1,0:T(8,128)(2,1)} %add_convert_fusion.2), channel_id=1, source_target_pairs={{0,0},{4,8},{8,4},{12,12},{1,1},{5,9},{9,5},{13,13},{2,2},{6,10},{... | collective-permute-start | bytes 786440 | tf_op jit(solution)/shard_map/ppermute | solution.py:49
  (184 other events, 1948.3 us)

commit v6 on v5

--- a/solution.py
+++ b/solution.py
@@ -454,8 +454,6 @@
             normed_all, attended, cotangent_task(1 if layer == 0 else 2)
         )
         pieces[1 if layer == 0 else 2] = piece
-        if layer == 0:
-            attended, w_down[0] = lax.optimization_barrier((attended, w_down[0]))
         middle = stream + (
             scatter_rows(attended, times(w_out[layer]))[0]
             + outward_bias[layer]
@@ -463,7 +461,7 @@
         normed_mid = layer_norm(middle, norm_gain[layer, 1], norm_shift[layer, 1]).astype(BF)
         mid_mine, _ = gather_ring(normed_mid)
         if layer == 0:
-            mid_mine, w_in[1], w_out[1] = lax.optimization_barrier((mid_mine, w_in[1], w_out[1]))
+            mid_mine, w_down[0] = lax.optimization_barrier((mid_mine, w_down[0]))
         mid_all = gather_pair(mid_mine)
         hidden_pre = (
             jnp.dot(mid_all, w_up[layer], preferred_element_type=F32) + bias_up[layer]
@@ -479,6 +477,7 @@
                 scatter_rows(activated, times(w_down[layer]))[0]
                 + shrink_bias[layer]
             )
+            stream, w_in[1], w_out[1] = lax.optimization_barrier((stream, w_in[1], w_out[1]))
     cotangent_ring = jnp.concatenate([cotangent, pieces[1], pieces[-1], pieces[2]])
 
     grad_stream = cotangent.astype(F32)

time: 477 us -> 488 us (1.023)
  matrix products: 37.6 us -> 46.8 us
  waiting for transfers between devices: 153 us -> 158 us
    ppermute x69, starting transfers between devices: 96.5 us -> 90.8 us  [ring(): lax.ppermute(values, RINGS[axis], [(i, (i + step) % 4) for i in range(4)])]
    unnamed x257 -> x249, local copies, waits for them, and re-layouts: 11.6 us -> 11.1 us
where the time goes in v6:
time: 488 us; the launch traced here: 479 us
  starting transfers between devices  168 us (34%)
  waiting for transfers between devices  158 us (32%)
  matrix products  46.8 us (10%)
  Pallas kernels  45.5 us (9%)
  local copies, waits for them, and re-layouts  29.5 us (6%)
  other arithmetic  27.2 us (6%)
    ppermute x69, waiting for transfers between devices, ring(): lax.ppermute(values, RINGS[axis], [(i, (i + step) % 4) for i in range(4)])  125 us
    ppermute x69, starting transfers between devices, ring(): lax.ppermute(values, RINGS[axis], [(i, (i + step) % 4) for i in range(4)])  90.8 us
    dot_general x12, matrix products, against_rows(): lax.dot_general(left, right, (((1,), (1,)), ((), ())), preferred_element_...  26.1 us
    ppermute x17, starting transfers between devices, swap_cores(): return lax.ppermute(values, 'c', [(0, 1), (1, 0)])  24.4 us
    ppermute x17, waiting for transfers between devices, swap_cores(): return lax.ppermute(values, 'c', [(0, 1), (1, 0)])  18.3 us
    pallas_call x4, Pallas kernels, grad_blocks(): pl.pallas_call(kernel, grid_spec=pltpu.PrefetchScalarGridSpec(num_scalar_...  17.6 us
    pallas_call x2, Pallas kernels, attend_backward(): pl.pallas_call(attend_backward_kernel, grid_spec=pltpu.PrefetchScalarGrid...  15 us
    ppermute x4, starting transfers between devices, swap_halves(): return lax.ppermute(values, ('c', 'yl'), [(0, 0), (1, 2), (2, 1), (3, 3)])  14.9 us
  transfers between devices with their start and end apart: 115, of which 49 were waited for; matrix products, arithmetic and copies ran while one was open for 13% of the time, Pallas kernels for 10%

profile of v6, /device:TPU:1, one launch (start us, length us, event | category | flops | bytes accessed | tf_op | source)
XLA Modules:
  0.0 478.5 jit_solution(12750437082541086314)
XLA Ops:
  4.1 3.2 collective-permute-start
  8.9 3.5 collective-permute-done
  13.0 3.7 collective-permute-start.3
  19.8 3.4 collective-permute-done.3
  23.2 3.5 collective-permute-done.2
  31.1 3.9 collective-permute-done.7
  34.9 5.1 %collective-permute-start.8 = (bf16[128,1024]{1,0:T(8,128)(2,1)S(1)}, bf16[128,1024]{1,0:T(8,128)(2,1)S(1)}, u32[]{:S(2)}, u32[]{:S(2)}) collective-permute-start(bf16[128,1024]{1,0:T(8,128)(2,1)S(1)} %copy-done.111), channel_id=1, source_target_pairs={{0,0},{4,8},{8,4},{12,12},{1,1},{5,9},{9,5},{13,13},{2,2},{6,10},{... | collective-permute-start | bytes 786440 | tf_op jit(solution)/shard_map/ppermute | solution.py:49
  41.5 2.8 collective-permute-done.8
  47.7 6.5 %shard_map.211 = (bf16[1024,128]{1,0:T(8,128)(2,1)S(1)}, f32[2,1024]{1,0:T(2,128)S(1)}) custom-call(s32[8]{0:T(128)S(1)} %fusion.72.slots, bf16[1024,384]{1,0:T(8,128)(2,1)S(1)} %add_convert_fusion.1.low_ref.high_ref.k_ref.v_ref, bf16[1024,384]{1,0:T(8,128)(2,1)S(1)} %add_convert_fusion.1.low_ref.high_ref.k_ref.v_ref, ...), custom_call_target="tpu_custom_call" | custom-call | flops 1073741824 | bytes 2097152 | tf_op jit(solution)/shard_map/pallas_call | solution.py:291
  69.8 6.0 %collective-permute-done.13 = bf16[128,1024]{1,0:T(8,128)(2,1)S(1)} collective-permute-done((bf16[128,1024]{1,0:T(8,128)(2,1)S(1)}, bf16[128,1024]{1,0:T(8,128)(2,1)S(1)}, u32[]{:S(2)}, u32[]{:S(2)}) %collective-permute-start.13) | collective-permute-done | bytes 262176 | tf_op jit(solution)/shard_map/ppermute | solution.py:41
  79.9 5.8 %collective-permute-done.17 = bf16[128,1024]{1,0:T(8,128)(2,1)S(1)} collective-permute-done((bf16[128,1024]{1,0:T(8,128)(2,1)S(1)}, bf16[128,1024]{1,0:T(8,128)(2,1)S(1)}, u32[]{:S(2)}, u32[]{:S(2)}) %collective-permute-start.17) | collective-permute-done | bytes 262176 | tf_op jit(solution)/shard_map/ppermute | solution.py:41
  85.7 5.2 %collective-permute-done.16 = bf16[128,1024]{1,0:T(8,128)(2,1)S(1)} collective-permute-done((bf16[128,1024]{1,0:T(8,128)(2,1)S(1)}, bf16[128,1024]{1,0:T(8,128)(2,1)S(1)}, u32[]{:S(2)}, u32[]{:S(2)}) %collective-permute-start.16) | collective-permute-done | bytes 262176 | tf_op jit(solution)/shard_map/ppermute | solution.py:41
  95.1 5.0 %multiply_convert_fusion.1 = (bf16[1024,512]{1,0:T(8,128)(2,1)S(1)}, f32[1024,512]{1,0:T(8,128)}) fusion(f32[512]{0:T(512)S(1)} %get-tuple-element.413, bf16[1024,1024]{1,0:T(8,128)(2,1)S(1)} %constant_dynamic-update-slice_fusion.refs_2_.refs_3_, bf16[1024,512]{1,0:T(8,128)(2,1)} %collective-permute-done.5), kind=kOutput, calls=%fused_computation.32 | convolution fusion | flops 1078984704 | bytes 6293504 | tf_op jit(solution)/shard_map/dot_general | solution.py:467
  114.4 3.3 collective-permute-start.26
  118.8 4.3 collective-permute-done.23
  128.9 3.4 collective-permute-done.29
  132.3 7.8 %collective-permute-done.28 = bf16[128,1024]{1,0:T(8,128)(2,1)S(1)} collective-permute-done((bf16[128,1024]{1,0:T(8,128)(2,1)S(1)}, bf16[128,1024]{1,0:T(8,128)(2,1)S(1)}, u32[]{:S(2)}, u32[]{:S(2)}) %collective-permute-start.28) | collective-permute-done | bytes 262176 | tf_op jit(solution)/shard_map/ppermute | solution.py:41
  148.5 6.5 %shard_map.212 = (bf16[1024,128]{1,0:T(8,128)(2,1)S(1)}, f32[2,1024]{1,0:T(2,128)S(1)}) custom-call(s32[8]{0:T(128)S(1)} %fusion.72.slots, bf16[1024,384]{1,0:T(8,128)(2,1)S(1)} %add_convert_fusion.low_ref.high_ref.k_ref.v_ref, bf16[1024,384]{1,0:T(8,128)(2,1)S(1)} %add_convert_fusion.low_ref.high_ref.k_ref.v_ref, ...), custom_call_target="tpu_custom_call" | custom-call | flops 1073741824 | bytes 2097152 | tf_op jit(solution)/shard_map/pallas_call | solution.py:291
  163.4 4.8 collective-permute-done.37
  168.1 6.3 %collective-permute-done.36 = bf16[128,1024]{1,0:T(8,128)(2,1)S(1)} collective-permute-done((bf16[128,1024]{1,0:T(8,128)(2,1)S(1)}, bf16[128,1024]{1,0:T(8,128)(2,1)S(1)}, u32[]{:S(2)}, u32[]{:S(2)}) %collective-permute-start.36) | collective-permute-done | bytes 262176 | tf_op jit(solution)/shard_map/ppermute | solution.py:41
  180.2 3.9 collective-permute-done.40
  184.1 4.5 collective-permute-done.39
  193.7 2.8 fusion.79
  196.6 4.8 %convert_reduce_fusion = (f32[512]{0:T(512)}, bf16[1024,512]{1,0:T(8,128)(2,1)S(1)}, bf16[1024,512]{1,0:T(8,128)(2,1)S(1)}) fusion(f32[1024,512]{1,0:T(8,128)S(1)} %fusion.79, f32[512]{0:T(512)S(1)} %get-tuple-element.412, bf16[1024,1024]{1,0:T(8,128)(2,1)S(1)} %constant_dynamic-update-slice_fusion.4.refs_0_.refs_1_, ...), kind=kOutput, calls=%fused_computation.22 | convolution fusion | flops 1088945664 | bytes 7344128 | tf_op jit(solution)/shard_map/dot_general | solution.py:37
  202.4 3.0 convolution_convert_fusion.6
  216.0 4.5 shard_map.213
  220.6 5.8 %collective-permute-done.45 = bf16[128,1024]{1,0:T(8,128)(2,1)S(1)} collective-permute-done((bf16[128,1024]{1,0:T(8,128)(2,1)S(1)}, bf16[128,1024]{1,0:T(8,128)(2,1)S(1)}, u32[]{:S(2)}, u32[]{:S(2)}) %collective-permute-start.45) | collective-permute-done | bytes 262176 | tf_op jit(solution)/shard_map/ppermute | solution.py:41
  233.9 5.5 %collective-permute-done.49 = bf16[128,1024]{1,0:T(8,128)(2,1)S(1)} collective-permute-done((bf16[128,1024]{1,0:T(8,128)(2,1)S(1)}, bf16[128,1024]{1,0:T(8,128)(2,1)S(1)}, u32[]{:S(2)}, u32[]{:S(2)}) %collective-permute-start.49) | collective-permute-done | bytes 262176 | tf_op jit(solution)/shard_map/ppermute | solution.py:41
  239.4 4.9 %collective-permute-done.48 = bf16[128,1024]{1,0:T(8,128)(2,1)S(1)} collective-permute-done((bf16[128,1024]{1,0:T(8,128)(2,1)S(1)}, bf16[128,1024]{1,0:T(8,128)(2,1)S(1)}, u32[]{:S(2)}, u32[]{:S(2)}) %collective-permute-start.48) | collective-permute-done | bytes 262176 | tf_op jit(solution)/shard_map/ppermute | solution.py:41
  261.0 7.5 %shard_map.214.refs_5_ = bf16[1024,384]{1,0:T(8,128)(2,1)S(1)} custom-call(s32[8]{0:T(128)S(1)} %fusion.72.slots, f32[2,1024]{1,0:T(2,128)S(1)} %get-tuple-element.171.log_ref, bf16[1024,384]{1,0:T(8,128)(2,1)S(1)} %copy-done.20, bf16[1024,384]{1,0:T(8,128)(2,1)S(1)} %copy-done.20, bf16[1024,384]{1,0:T(8,128)(2,1)S(1)} %copy-done.20, ...), custom_call_target="tpu_custom_call" | custom-call | flops 2684354560 | bytes 4194304 | tf_op jit(solution)/shard_map/pallas_call | solution.py:367
  273.9 3.2 collective-permute-start.61
  285.9 3.9 shard_map.215
  291.3 6.7 %collective-permute-done.59 = bf16[128,1024]{1,0:T(8,128)(2,1)S(1)} collective-permute-done((bf16[128,1024]{1,0:T(8,128)(2,1)S(1)}, bf16[128,1024]{1,0:T(8,128)(2,1)S(1)}, u32[]{:S(2)}, u32[]{:S(2)}) %collective-permute-start.59) | collective-permute-done | bytes 262176 | tf_op jit(solution)/shard_map/ppermute | solution.py:41
  305.5 4.3 collective-permute-done.66
  316.5 3.5 collective-permute-start.70
  327.3 2.8 fusion.3.refs_5_
  331.1 3.0 convolution_convert_fusion.4
  346.1 5.2 %shard_map.216 = (bf16[2,128,1024]{2,1,0:T(8,128)(2,1)S(1)}, bf16[2,128,1024]{2,1,0:T(8,128)(2,1)S(1)}, bf16[2,128,1024]{2,1,0:T(8,128)(2,1)}, bf16[2,128,1024]{2,1,0:T(8,128)(2,1)S(1)}) custom-call(s32[1]{0:T(128)} %bitcast.27.place_ref, bf16[1024,1024]{1,0:T(8,128)(2,1)S(1)} %constant_dynamic-update-slice_fusion.11.refs_0_.refs_1_, ...), custom_call_target="tpu_custom_call" | custom-call | flops 2147483648 | bytes 8388608 | tf_op jit(solution)/shard_map/pallas_call | solution.py:150
  351.4 5.3 %collective-permute-done.78 = bf16[128,1024]{1,0:T(8,128)(2,1)S(1)} collective-permute-done((bf16[128,1024]{1,0:T(8,128)(2,1)S(1)}, bf16[128,1024]{1,0:T(8,128)(2,1)S(1)}, u32[]{:S(2)}, u32[]{:S(2)}) %collective-permute-start.78) | collective-permute-done | bytes 262176 | tf_op jit(solution)/shard_map/ppermute | solution.py:41
  367.7 4.2 collective-permute-done.81
  382.3 3.0 collective-permute-done.72
  386.1 2.9 collective-permute-start.86
  394.2 7.5 %shard_map.217.refs_5_ = bf16[1024,384]{1,0:T(8,128)(2,1)S(1)} custom-call(s32[8]{0:T(128)S(1)} %fusion.72.slots, f32[2,1024]{1,0:T(2,128)S(1)} %get-tuple-element.246.log_ref, bf16[1024,384]{1,0:T(8,128)(2,1)S(1)} %copy-done.18, bf16[1024,384]{1,0:T(8,128)(2,1)S(1)} %copy-done.18, bf16[1024,384]{1,0:T(8,128)(2,1)S(1)} %copy-done.18, ...), custom_call_target="tpu_custom_call" | custom-call | flops 2684354560 | bytes 4194304 | tf_op jit(solution)/shard_map/pallas_call | solution.py:367
  414.3 3.9 shard_map.218
  418.5 6.6 %collective-permute-done.89 = bf16[128,1024]{1,0:T(8,128)(2,1)S(1)} collective-permute-done((bf16[128,1024]{1,0:T(8,128)(2,1)S(1)}, bf16[128,1024]{1,0:T(8,128)(2,1)S(1)}, u32[]{:S(2)}, u32[]{:S(2)}) %collective-permute-start.89) | collective-permute-done | bytes 262176 | tf_op jit(solution)/shard_map/ppermute | solution.py:41
  435.8 4.8 collective-permute-start.94
  440.6 3.3 collective-permute-done.100
  464.1 7.6 %collective-permute-start.110 = (f32[108,128]{1,0:T(8,128)S(1)}, f32[108,128]{1,0:T(8,128)S(1)}, u32[]{:S(2)}, u32[]{:S(2)}) collective-permute-start(f32[108,128]{1,0:T(8,128)S(1)} %add_add_fusion.8), channel_id=1, source_target_pairs={{0,8},{8,0},{1,9},{9,1},{2,10},{10,2},{3,11},{11,3},{4,12},{12,4},... | collective-permute-start | bytes 165896 | tf_op jit(solution)/shard_map/ppermute | solution.py:45
  (611 shorter events, 252.2 us)
Async XLA Ops:
  2.7 52.2 %collective-permute-start.10 = (bf16[128,1024]{1,0:T(8,128)(2,1)}, bf16[128,1024]{1,0:T(8,128)(2,1)}, u32[]{:S(2)}, u32[]{:S(2)}) collective-permute-start(bf16[128,1024]{1,0:T(8,128)(2,1)} %get-tuple-element.390), channel_id=1, source_target_pairs={{0,4},{8,0},{4,12},{12,72},{64,68},{72,64},{68,76},{76,8},{1,5},{9... | collective-permute-start | bytes 786440 | tf_op jit(solution)/shard_map/ppermute | solution.py:66
  19.7 21.8 %collective-permute-start.5 = (bf16[1024,512]{1,0:T(8,128)(2,1)}, bf16[1024,512]{1,0:T(8,128)(2,1)}, u32[]{:S(2)}, u32[]{:S(2)}) collective-permute-start(bf16[1024,512]{1,0:T(8,128)(2,1)} %get-tuple-element.346), channel_id=1, source_target_pairs={{0,4},{8,0},{4,12},{12,72},{64,68},{72,64},{68,76},{76,8},{1,5},{9... | collective-permute-start | bytes 3145736 | tf_op jit(solution)/shard_map/ppermute | solution.py:66
  26.8 13.3 %collective-permute-start.4 = (bf16[512,1024]{1,0:T(8,128)(2,1)S(1)}, bf16[512,1024]{1,0:T(8,128)(2,1)}, u32[]{:S(2)}, u32[]{:S(2)}) collective-permute-start(bf16[512,1024]{1,0:T(8,128)(2,1)S(1)} %pad_maximum_fusion.2), channel_id=1, source_target_pairs={{0,8},{8,0},{1,9},{9,1},{2,10},{10,2},{3,11},{11,3},{4,12},{12,4},... | collective-permute-start | bytes 3145736 | tf_op jit(solution)/shard_map/ppermute | solution.py:45
  28.2 16.8 %collective-permute-start.6 = (bf16[1024,384]{0,1:T(8,128)(2,1)}, bf16[1024,384]{0,1:T(8,128)(2,1)S(1)}, u32[]{:S(2)}, u32[]{:S(2)}) collective-permute-start(bf16[1024,384]{0,1:T(8,128)(2,1)} %bitcast.159), channel_id=1, source_target_pairs={{0,68},{8,0},{4,12},{12,8},{64,4},{72,64},{68,76},{76,72},{1,69},{... | collective-permute-start | bytes 2359304 | tf_op jit(solution)/shard_map/ppermute | solution.py:66
  62.6 13.3 %collective-permute-start.13 = (bf16[128,1024]{1,0:T(8,128)(2,1)S(1)}, bf16[128,1024]{1,0:T(8,128)(2,1)S(1)}, u32[]{:S(2)}, u32[]{:S(2)}) collective-permute-start(bf16[128,1024]{1,0:T(8,128)(2,1)S(1)} %get-tuple-element.378), channel_id=1, source_target_pairs={{0,1},{1,2},{2,3},{3,0},{4,5},{5,6},{6,7},{7,4},{8,9},{9,10},{10,1... | collective-permute-start | bytes 786440 | tf_op jit(solution)/shard_map/ppermute | solution.py:41
  63.6 12.3 %collective-permute-start.12 = (bf16[128,1024]{1,0:T(8,128)(2,1)S(1)}, bf16[128,1024]{1,0:T(8,128)(2,1)S(1)}, u32[]{:S(2)}, u32[]{:S(2)}) collective-permute-start(bf16[128,1024]{1,0:T(8,128)(2,1)S(1)} %get-tuple-element.376), channel_id=1, source_target_pairs={{0,3},{1,0},{2,1},{3,2},{4,7},{5,4},{6,5},{7,6},{8,11},{9,8},{10,9... | collective-permute-start | bytes 786440 | tf_op jit(solution)/shard_map/ppermute | solution.py:41
  66.9 25.2 %collective-permute-start.18 = (bf16[512,1024]{1,0:T(8,128)(2,1)S(1)}, bf16[512,1024]{1,0:T(8,128)(2,1)S(1)}, u32[]{:S(2)}, u32[]{:S(2)}) collective-permute-start(bf16[512,1024]{1,0:T(8,128)(2,1)S(1)} %get-tuple-element.344), channel_id=1, source_target_pairs={{0,68},{8,0},{4,12},{12,8},{64,4},{72,64},{68,76},{76,72},{1,69},{... | collective-permute-start | bytes 3145736 | tf_op jit(solution)/shard_map/ppermute | solution.py:66
  78.4 12.5 %collective-permute-start.16 = (bf16[128,1024]{1,0:T(8,128)(2,1)S(1)}, bf16[128,1024]{1,0:T(8,128)(2,1)S(1)}, u32[]{:S(2)}, u32[]{:S(2)}) collective-permute-start(bf16[128,1024]{1,0:T(8,128)(2,1)S(1)} %add_convert_fusion.6), channel_id=1, source_target_pairs={{0,3},{1,0},{2,1},{3,2},{4,7},{5,4},{6,5},{7,6},{8,11},{9,8},{10,9... | collective-permute-start | bytes 786440 | tf_op jit(solution)/shard_map/ppermute | solution.py:41
  79.3 12.8 %collective-permute-start.15 = (bf16[128,1024]{1,0:T(8,128)(2,1)S(1)}, bf16[128,1024]{1,0:T(8,128)(2,1)S(1)}, u32[]{:S(2)}, u32[]{:S(2)}) collective-permute-start(bf16[128,1024]{1,0:T(8,128)(2,1)S(1)} %add_convert_fusion.6), channel_id=1, source_target_pairs={{0,1},{1,2},{2,3},{3,0},{4,5},{5,6},{6,7},{7,4},{8,9},{9,10},{10,1... | collective-permute-start | bytes 786440 | tf_op jit(solution)/shard_map/ppermute | solution.py:41
  109.3 13.8 %collective-permute-start.23 = (bf16[128,1024]{1,0:T(8,128)(2,1)}, bf16[128,1024]{1,0:T(8,128)(2,1)S(1)}, u32[]{:S(2)}, u32[]{:S(2)}) collective-permute-start(bf16[128,1024]{1,0:T(8,128)(2,1)} %get-tuple-element.375), channel_id=1, source_target_pairs={{0,1},{1,2},{2,3},{3,0},{4,5},{5,6},{6,7},{7,4},{8,9},{9,10},{10,1... | collective-permute-start | bytes 786440 | tf_op jit(solution)/shard_map/ppermute | solution.py:41
  111.4 12.2 %collective-permute-start.22 = (bf16[128,1024]{1,0:T(8,128)(2,1)}, bf16[128,1024]{1,0:T(8,128)(2,1)S(1)}, u32[]{:S(2)}, u32[]{:S(2)}) collective-permute-start(bf16[128,1024]{1,0:T(8,128)(2,1)} %get-tuple-element.373), channel_id=1, source_target_pairs={{0,3},{1,0},{2,1},{3,2},{4,7},{5,4},{6,5},{7,6},{8,11},{9,8},{10,9... | collective-permute-start | bytes 786440 | tf_op jit(solution)/shard_map/ppermute | solution.py:41
  113.2 11.8 %collective-permute-start.25 = (bf16[1024,384]{0,1:T(8,128)(2,1)}, bf16[1024,384]{0,1:T(8,128)(2,1)S(1)}, u32[]{:S(2)}, u32[]{:S(2)}) collective-permute-start(bf16[1024,384]{0,1:T(8,128)(2,1)} %bitcast.15), channel_id=1, source_target_pairs={{0,68},{8,0},{4,12},{12,8},{64,4},{72,64},{68,76},{76,72},{1,69},{... | collective-permute-start | bytes 2359304 | tf_op jit(solution)/shard_map/ppermute | solution.py:66
  118.3 21.9 %collective-permute-start.30 = (bf16[1024,512]{1,0:T(8,128)(2,1)}, bf16[1024,512]{1,0:T(8,128)(2,1)}, u32[]{:S(2)}, u32[]{:S(2)}) collective-permute-start(bf16[1024,512]{1,0:T(8,128)(2,1)} %get-tuple-element.345), channel_id=1, source_target_pairs={{0,4},{8,0},{4,12},{12,72},{64,68},{72,64},{68,76},{76,8},{1,5},{9... | collective-permute-start | bytes 3145736 | tf_op jit(solution)/shard_map/ppermute | solution.py:66
  123.1 17.0 %collective-permute-start.31 = (bf16[512,1024]{1,0:T(8,128)(2,1)}, bf16[512,1024]{1,0:T(8,128)(2,1)}, u32[]{:S(2)}, u32[]{:S(2)}) collective-permute-start(bf16[512,1024]{1,0:T(8,128)(2,1)} %get-tuple-element.343), channel_id=1, source_target_pairs={{0,68},{8,0},{4,12},{12,8},{64,4},{72,64},{68,76},{76,72},{1,69},{... | collective-permute-start | bytes 3145736 | tf_op jit(solution)/shard_map/ppermute | solution.py:66
  127.3 12.8 %collective-permute-start.28 = (bf16[128,1024]{1,0:T(8,128)(2,1)S(1)}, bf16[128,1024]{1,0:T(8,128)(2,1)S(1)}, u32[]{:S(2)}, u32[]{:S(2)}) collective-permute-start(bf16[128,1024]{1,0:T(8,128)(2,1)S(1)} %add_convert_fusion.5), channel_id=1, source_target_pairs={{0,3},{1,0},{2,1},{3,2},{4,7},{5,4},{6,5},{7,6},{8,11},{9,8},{10,9... | collective-permute-start | bytes 786440 | tf_op jit(solution)/shard_map/ppermute | solution.py:41
  128.4 11.7 %collective-permute-start.27 = (bf16[128,1024]{1,0:T(8,128)(2,1)S(1)}, bf16[128,1024]{1,0:T(8,128)(2,1)S(1)}, u32[]{:S(2)}, u32[]{:S(2)}) collective-permute-start(bf16[128,1024]{1,0:T(8,128)(2,1)S(1)} %add_convert_fusion.5), channel_id=1, source_target_pairs={{0,1},{1,2},{2,3},{3,0},{4,5},{5,6},{6,7},{7,4},{8,9},{9,10},{10,1... | collective-permute-start | bytes 786440 | tf_op jit(solution)/shard_map/ppermute | solution.py:41
  160.7 13.7 %collective-permute-start.36 = (bf16[128,1024]{1,0:T(8,128)(2,1)S(1)}, bf16[128,1024]{1,0:T(8,128)(2,1)S(1)}, u32[]{:S(2)}, u32[]{:S(2)}) collective-permute-start(bf16[128,1024]{1,0:T(8,128)(2,1)S(1)} %get-tuple-element.372), channel_id=1, source_target_pairs={{0,1},{1,2},{2,3},{3,0},{4,5},{5,6},{6,7},{7,4},{8,9},{9,10},{10,1... | collective-permute-start | bytes 786440 | tf_op jit(solution)/shard_map/ppermute | solution.py:41
  160.9 13.5 %collective-permute-start.35 = (bf16[128,1024]{1,0:T(8,128)(2,1)S(1)}, bf16[128,1024]{1,0:T(8,128)(2,1)S(1)}, u32[]{:S(2)}, u32[]{:S(2)}) collective-permute-start(bf16[128,1024]{1,0:T(8,128)(2,1)S(1)} %get-tuple-element.370), channel_id=1, source_target_pairs={{0,3},{1,0},{2,1},{3,2},{4,7},{5,4},{6,5},{7,6},{8,11},{9,8},{10,9... | collective-permute-start | bytes 786440 | tf_op jit(solution)/shard_map/ppermute | solution.py:41
  176.5 12.1 %collective-permute-start.39 = (bf16[128,1024]{1,0:T(8,128)(2,1)S(1)}, bf16[128,1024]{1,0:T(8,128)(2,1)S(1)}, u32[]{:S(2)}, u32[]{:S(2)}) collective-permute-start(bf16[128,1024]{1,0:T(8,128)(2,1)S(1)} %add_convert_fusion.4), channel_id=1, source_target_pairs={{0,3},{1,0},{2,1},{3,2},{4,7},{5,4},{6,5},{7,6},{8,11},{9,8},{10,9... | collective-permute-start | bytes 786440 | tf_op jit(solution)/shard_map/ppermute | solution.py:41
  179.0 11.5 %collective-permute-start.38 = (bf16[128,1024]{1,0:T(8,128)(2,1)S(1)}, bf16[128,1024]{1,0:T(8,128)(2,1)S(1)}, u32[]{:S(2)}, u32[]{:S(2)}) collective-permute-start(bf16[128,1024]{1,0:T(8,128)(2,1)S(1)} %add_convert_fusion.4), channel_id=1, source_target_pairs={{0,1},{1,2},{2,3},{3,0},{4,5},{5,6},{6,7},{7,4},{8,9},{9,10},{10,1... | collective-permute-start | bytes 786440 | tf_op jit(solution)/shard_map/ppermute | solution.py:41
  179.1 12.5 %collective-permute-start.42 = (bf16[512,1024]{1,0:T(8,128)(2,1)S(1)}, bf16[512,1024]{1,0:T(8,128)(2,1)S(1)}, u32[]{:S(2)}, u32[]{:S(2)}) collective-permute-start(bf16[512,1024]{1,0:T(8,128)(2,1)S(1)} %pad_maximum_fusion.6), channel_id=1, source_target_pairs={{0,8},{8,0},{1,9},{9,1},{2,10},{10,2},{3,11},{11,3},{4,12},{12,4},... | collective-permute-start | bytes 3145736 | tf_op jit(solution)/shard_map/ppermute | solution.py:45
  213.1 13.3 %collective-permute-start.45 = (bf16[128,1024]{1,0:T(8,128)(2,1)S(1)}, bf16[128,1024]{1,0:T(8,128)(2,1)S(1)}, u32[]{:S(2)}, u32[]{:S(2)}) collective-permute-start(bf16[128,1024]{1,0:T(8,128)(2,1)S(1)} %get-tuple-element.369), channel_id=1, source_target_pairs={{0,1},{1,2},{2,3},{3,0},{4,5},{5,6},{6,7},{7,4},{8,9},{9,10},{10,1... | collective-permute-start | bytes 786440 | tf_op jit(solution)/shard_map/ppermute | solution.py:41
  213.1 13.3 %collective-permute-start.44 = (bf16[128,1024]{1,0:T(8,128)(2,1)S(1)}, bf16[128,1024]{1,0:T(8,128)(2,1)S(1)}, u32[]{:S(2)}, u32[]{:S(2)}) collective-permute-start(bf16[128,1024]{1,0:T(8,128)(2,1)S(1)} %get-tuple-element.367), channel_id=1, source_target_pairs={{0,3},{1,0},{2,1},{3,2},{4,7},{5,4},{6,5},{7,6},{8,11},{9,8},{10,9... | collective-permute-start | bytes 786440 | tf_op jit(solution)/shard_map/ppermute | solution.py:41
  227.7 18.6 %collective-permute-start.50 = (bf16[2,128,1024]{2,1,0:T(8,128)(2,1)S(1)}, bf16[2,128,1024]{2,1,0:T(8,128)(2,1)S(1)}, u32[]{:S(2)}, u32[]{:S(2)}) collective-permute-start(bf16[2,128,1024]{2,1,0:T(8,128)(2,1)S(1)} %get-tuple-element.187), channel_id=1, source_target_pairs={{0,16},{16,32},{32,48},{48,0},{1,17},{17,33},{33,49},{49,1},{2,18}... | collective-permute-start | bytes 1572872 | tf_op jit(solution)/shard_map/ppermute | solution.py:41
  229.0 17.3 %collective-permute-start.51 = (bf16[2,128,1024]{2,1,0:T(8,128)(2,1)S(1)}, bf16[2,128,1024]{2,1,0:T(8,128)(2,1)S(1)}, u32[]{:S(2)}, u32[]{:S(2)}) collective-permute-start(bf16[2,128,1024]{2,1,0:T(8,128)(2,1)S(1)} %get-tuple-element.188), channel_id=1, source_target_pairs={{0,48},{16,0},{32,16},{48,32},{1,49},{17,1},{33,17},{49,33},{2,50}... | collective-permute-start | bytes 1572872 | tf_op jit(solution)/shard_map/ppermute | solution.py:41
  232.0 12.3 %collective-permute-start.48 = (bf16[128,1024]{1,0:T(8,128)(2,1)S(1)}, bf16[128,1024]{1,0:T(8,128)(2,1)S(1)}, u32[]{:S(2)}, u32[]{:S(2)}) collective-permute-start(bf16[128,1024]{1,0:T(8,128)(2,1)S(1)} %get-tuple-element.329), channel_id=1, source_target_pairs={{0,3},{1,0},{2,1},{3,2},{4,7},{5,4},{6,5},{7,6},{8,11},{9,8},{10,9... | collective-permute-start | bytes 786440 | tf_op jit(solution)/shard_map/ppermute | solution.py:41
  233.9 12.3 %collective-permute-start.47 = (bf16[128,1024]{1,0:T(8,128)(2,1)S(1)}, bf16[128,1024]{1,0:T(8,128)(2,1)S(1)}, u32[]{:S(2)}, u32[]{:S(2)}) collective-permute-start(bf16[128,1024]{1,0:T(8,128)(2,1)S(1)} %get-tuple-element.329), channel_id=1, source_target_pairs={{0,1},{1,2},{2,3},{3,0},{4,5},{5,6},{6,7},{7,4},{8,9},{9,10},{10,1... | collective-permute-start | bytes 786440 | tf_op jit(solution)/shard_map/ppermute | solution.py:41
  252.5 16.8 %collective-permute-start.56 = (bf16[2,128,1024]{2,1,0:T(8,128)(2,1)S(1)}, bf16[2,128,1024]{2,1,0:T(8,128)(2,1)S(1)}, u32[]{:S(2)}, u32[]{:S(2)}) collective-permute-start(bf16[2,128,1024]{2,1,0:T(8,128)(2,1)S(1)} %get-tuple-element.196), channel_id=1, source_target_pairs={{0,32},{16,48},{32,0},{48,16},{1,33},{17,49},{33,1},{49,17},{2,34}... | collective-permute-start | bytes 1572872 | tf_op jit(solution)/shard_map/ppermute | solution.py:41
  282.9 15.2 %collective-permute-start.59 = (bf16[128,1024]{1,0:T(8,128)(2,1)S(1)}, bf16[128,1024]{1,0:T(8,128)(2,1)S(1)}, u32[]{:S(2)}, u32[]{:S(2)}) collective-permute-start(bf16[128,1024]{1,0:T(8,128)(2,1)S(1)} %get-tuple-element.363), channel_id=1, source_target_pairs={{0,1},{1,2},{2,3},{3,0},{4,5},{5,6},{6,7},{7,4},{8,9},{9,10},{10,1... | collective-permute-start | bytes 786440 | tf_op jit(solution)/shard_map/ppermute | solution.py:41
  284.3 13.8 %collective-permute-start.58 = (bf16[128,1024]{1,0:T(8,128)(2,1)S(1)}, bf16[128,1024]{1,0:T(8,128)(2,1)S(1)}, u32[]{:S(2)}, u32[]{:S(2)}) collective-permute-start(bf16[128,1024]{1,0:T(8,128)(2,1)S(1)} %get-tuple-element.361), channel_id=1, source_target_pairs={{0,3},{1,0},{2,1},{3,2},{4,7},{5,4},{6,5},{7,6},{8,11},{9,8},{10,9... | collective-permute-start | bytes 786440 | tf_op jit(solution)/shard_map/ppermute | solution.py:41
  301.1 12.8 %collective-permute-start.65 = (bf16[128,1024]{1,0:T(8,128)(2,1)S(1)}, bf16[128,1024]{1,0:T(8,128)(2,1)S(1)}, u32[]{:S(2)}, u32[]{:S(2)}) collective-permute-start(bf16[128,1024]{1,0:T(8,128)(2,1)S(1)} %get-tuple-element.326), channel_id=1, source_target_pairs={{0,3},{1,0},{2,1},{3,2},{4,7},{5,4},{6,5},{7,6},{8,11},{9,8},{10,9... | collective-permute-start | bytes 786440 | tf_op jit(solution)/shard_map/ppermute | solution.py:41
  302.8 13.5 %collective-permute-start.64 = (bf16[128,1024]{1,0:T(8,128)(2,1)S(1)}, bf16[128,1024]{1,0:T(8,128)(2,1)S(1)}, u32[]{:S(2)}, u32[]{:S(2)}) collective-permute-start(bf16[128,1024]{1,0:T(8,128)(2,1)S(1)} %get-tuple-element.326), channel_id=1, source_target_pairs={{0,1},{1,2},{2,3},{3,0},{4,5},{5,6},{6,7},{7,4},{8,9},{9,10},{10,1... | collective-permute-start | bytes 786440 | tf_op jit(solution)/shard_map/ppermute | solution.py:41
  302.8 13.5 %collective-permute-start.67 = (bf16[2,128,512]{2,1,0:T(8,128)(2,1)S(1)}, bf16[2,128,512]{2,1,0:T(8,128)(2,1)S(1)}, u32[]{:S(2)}, u32[]{:S(2)}) collective-permute-start(bf16[2,128,512]{2,1,0:T(8,128)(2,1)S(1)} %get-tuple-element.216), channel_id=1, source_target_pairs={{0,16},{16,32},{32,48},{48,0},{1,17},{17,33},{33,49},{49,1},{2,18}... | collective-permute-start | bytes 786440 | tf_op jit(solution)/shard_map/ppermute | solution.py:41
  302.8 13.5 %collective-permute-start.68 = (bf16[2,128,512]{2,1,0:T(8,128)(2,1)S(1)}, bf16[2,128,512]{2,1,0:T(8,128)(2,1)S(1)}, u32[]{:S(2)}, u32[]{:S(2)}) collective-permute-start(bf16[2,128,512]{2,1,0:T(8,128)(2,1)S(1)} %get-tuple-element.217), channel_id=1, source_target_pairs={{0,48},{16,0},{32,16},{48,32},{1,49},{17,1},{33,17},{49,33},{2,50}... | collective-permute-start | bytes 786440 | tf_op jit(solution)/shard_map/ppermute | solution.py:41
  335.9 26.5 %collective-permute-start.114 = (f32[64,1024]{1,0:T(8,128)}, f32[64,1024]{1,0:T(8,128)S(1)}, u32[]{:S(2)}, u32[]{:S(2)}) collective-permute-start(f32[64,1024]{1,0:T(8,128)} %get-tuple-element.297), channel_id=1, source_target_pairs={{0,8},{12,4},{1,9},{13,5},{2,10},{14,6},{3,11},{15,7},{16,24},{28,... | collective-permute-start | bytes 786440 | tf_op jit(solution)/shard_map/ppermute | solution.py:205
  343.4 13.3 %collective-permute-start.78 = (bf16[128,1024]{1,0:T(8,128)(2,1)S(1)}, bf16[128,1024]{1,0:T(8,128)(2,1)S(1)}, u32[]{:S(2)}, u32[]{:S(2)}) collective-permute-start(bf16[128,1024]{1,0:T(8,128)(2,1)S(1)} %get-tuple-element.357), channel_id=1, source_target_pairs={{0,1},{1,2},{2,3},{3,0},{4,5},{5,6},{6,7},{7,4},{8,9},{9,10},{10,1... | collective-permute-start | bytes 786440 | tf_op jit(solution)/shard_map/ppermute | solution.py:41
  343.4 13.3 %collective-permute-start.77 = (bf16[128,1024]{1,0:T(8,128)(2,1)S(1)}, bf16[128,1024]{1,0:T(8,128)(2,1)S(1)}, u32[]{:S(2)}, u32[]{:S(2)}) collective-permute-start(bf16[128,1024]{1,0:T(8,128)(2,1)S(1)} %get-tuple-element.355), channel_id=1, source_target_pairs={{0,3},{1,0},{2,1},{3,2},{4,7},{5,4},{6,5},{7,6},{8,11},{9,8},{10,9... | collective-permute-start | bytes 786440 | tf_op jit(solution)/shard_map/ppermute | solution.py:41
  359.6 12.2 %collective-permute-start.81 = (bf16[128,1024]{1,0:T(8,128)(2,1)S(1)}, bf16[128,1024]{1,0:T(8,128)(2,1)S(1)}, u32[]{:S(2)}, u32[]{:S(2)}) collective-permute-start(bf16[128,1024]{1,0:T(8,128)(2,1)S(1)} %get-tuple-element.331), channel_id=1, source_target_pairs={{0,3},{1,0},{2,1},{3,2},{4,7},{5,4},{6,5},{7,6},{8,11},{9,8},{10,9... | collective-permute-start | bytes 786440 | tf_op jit(solution)/shard_map/ppermute | solution.py:41
  361.9 12.3 %collective-permute-start.80 = (bf16[128,1024]{1,0:T(8,128)(2,1)S(1)}, bf16[128,1024]{1,0:T(8,128)(2,1)S(1)}, u32[]{:S(2)}, u32[]{:S(2)}) collective-permute-start(bf16[128,1024]{1,0:T(8,128)(2,1)S(1)} %get-tuple-element.331), channel_id=1, source_target_pairs={{0,1},{1,2},{2,3},{3,0},{4,5},{5,6},{6,7},{7,4},{8,9},{9,10},{10,1... | collective-permute-start | bytes 786440 | tf_op jit(solution)/shard_map/ppermute | solution.py:41
  361.9 13.5 %collective-permute-start.83 = (bf16[2,128,1024]{2,1,0:T(8,128)(2,1)S(1)}, bf16[2,128,1024]{2,1,0:T(8,128)(2,1)S(1)}, u32[]{:S(2)}, u32[]{:S(2)}) collective-permute-start(bf16[2,128,1024]{2,1,0:T(8,128)(2,1)S(1)} %get-tuple-element.248), channel_id=1, source_target_pairs={{0,16},{16,32},{32,48},{48,0},{1,17},{17,33},{33,49},{49,1},{2,18}... | collective-permute-start | bytes 1572872 | tf_op jit(solution)/shard_map/ppermute | solution.py:41
  362.4 12.9 %collective-permute-start.84 = (bf16[2,128,1024]{2,1,0:T(8,128)(2,1)S(1)}, bf16[2,128,1024]{2,1,0:T(8,128)(2,1)S(1)}, u32[]{:S(2)}, u32[]{:S(2)}) collective-permute-start(bf16[2,128,1024]{2,1,0:T(8,128)(2,1)S(1)} %get-tuple-element.249), channel_id=1, source_target_pairs={{0,48},{16,0},{32,16},{48,32},{1,49},{17,1},{33,17},{49,33},{2,50}... | collective-permute-start | bytes 1572872 | tf_op jit(solution)/shard_map/ppermute | solution.py:41
  375.3 15.8 %collective-permute-start.85 = (bf16[512,1024]{1,0:T(8,128)(2,1)}, bf16[512,1024]{1,0:T(8,128)(2,1)}, u32[]{:S(2)}, u32[]{:S(2)}) collective-permute-start(bf16[512,1024]{1,0:T(8,128)(2,1)} %pad_maximum_fusion.9), channel_id=1, source_target_pairs={{0,8},{8,0},{1,9},{9,1},{2,10},{10,2},{3,11},{11,3},{4,12},{12,4},... | collective-permute-start | bytes 3145736 | tf_op jit(solution)/shard_map/ppermute | solution.py:45
  386.1 15.6 %collective-permute-start.86 = (bf16[2,128,1024]{2,1,0:T(8,128)(2,1)}, bf16[2,128,1024]{2,1,0:T(8,128)(2,1)S(1)}, u32[]{:S(2)}, u32[]{:S(2)}) collective-permute-start(bf16[2,128,1024]{2,1,0:T(8,128)(2,1)} %get-tuple-element.254), channel_id=1, source_target_pairs={{0,32},{16,48},{32,0},{48,16},{1,33},{17,49},{33,1},{49,17},{2,34}... | collective-permute-start | bytes 1572872 | tf_op jit(solution)/shard_map/ppermute | solution.py:41
  411.3 13.8 %collective-permute-start.89 = (bf16[128,1024]{1,0:T(8,128)(2,1)S(1)}, bf16[128,1024]{1,0:T(8,128)(2,1)S(1)}, u32[]{:S(2)}, u32[]{:S(2)}) collective-permute-start(bf16[128,1024]{1,0:T(8,128)(2,1)S(1)} %get-tuple-element.354), channel_id=1, source_target_pairs={{0,1},{1,2},{2,3},{3,0},{4,5},{5,6},{6,7},{7,4},{8,9},{9,10},{10,1... | collective-permute-start | bytes 786440 | tf_op jit(solution)/shard_map/ppermute | solution.py:41
  413.0 12.1 %collective-permute-start.88 = (bf16[128,1024]{1,0:T(8,128)(2,1)S(1)}, bf16[128,1024]{1,0:T(8,128)(2,1)S(1)}, u32[]{:S(2)}, u32[]{:S(2)}) collective-permute-start(bf16[128,1024]{1,0:T(8,128)(2,1)S(1)} %get-tuple-element.352), channel_id=1, source_target_pairs={{0,3},{1,0},{2,1},{3,2},{4,7},{5,4},{6,5},{7,6},{8,11},{9,8},{10,9... | collective-permute-start | bytes 786440 | tf_op jit(solution)/shard_map/ppermute | solution.py:41
  432.5 11.3 %collective-permute-start.100 = (bf16[2,128,512]{2,1,0:T(8,128)(2,1)S(1)}, bf16[2,128,512]{2,1,0:T(8,128)(2,1)S(1)}, u32[]{:S(2)}, u32[]{:S(2)}) collective-permute-start(bf16[2,128,512]{2,1,0:T(8,128)(2,1)S(1)} %get-tuple-element.276), channel_id=1, source_target_pairs={{0,32},{16,48},{32,0},{48,16},{1,33},{17,49},{33,1},{49,17},{2,34}... | collective-permute-start | bytes 786440 | tf_op jit(solution)/shard_map/ppermute | solution.py:41
  433.5 14.6 %collective-permute-start.113 = (f32[64,1024]{1,0:T(8,128)S(1)}, f32[64,1024]{1,0:T(8,128)}, u32[]{:S(2)}, u32[]{:S(2)}) collective-permute-start(f32[64,1024]{1,0:T(8,128)S(1)} %get-tuple-element.295), channel_id=1, source_target_pairs={{0,8},{12,4},{1,9},{13,5},{2,10},{14,6},{3,11},{15,7},{16,24},{28,... | collective-permute-start | bytes 786440 | tf_op jit(solution)/shard_map/ppermute | solution.py:205
  435.8 14.8 %collective-permute-start.94 = (bf16[128,1024]{1,0:T(8,128)(2,1)}, bf16[128,1024]{1,0:T(8,128)(2,1)S(1)}, u32[]{:S(2)}, u32[]{:S(2)}) collective-permute-start(bf16[128,1024]{1,0:T(8,128)(2,1)} %add_convert_fusion.2), channel_id=1, source_target_pairs={{0,0},{4,8},{8,4},{12,12},{1,1},{5,9},{9,5},{13,13},{2,2},{6,10},{... | collective-permute-start | bytes 786440 | tf_op jit(solution)/shard_map/ppermute | solution.py:49
  (180 other events, 1806.7 us)
